TPU v7x, 32 devices: a whole 2x2x4 slice. The times are simulated.
32 devices in a mesh: grp: 2 (over y), gx: 4 (over x, core), gy: 4 (over z).
Axes of the slice: x: 2, y: 2, z: 4, core: 2. Of those that a mesh axis runs over, the one named last changes fastest.
Arguments:
- load_current: bfloat16 [16, 256, 512], P(None, ('grp', 'gx'), 'gy'), parts along dimension 1, may hold values from 0.29 to 9, as said below
- row_conductance: float32 [256, 512], P(('grp', 'gx'), 'gy'), parts along dimension 0, may hold values from 0.5 to 8
- col_conductance: float32 [256, 512], P(('grp', 'gx'), 'gy'), parts along dimension 0, may hold values from 0.5 to 8
- via_conductance: float32 [256, 512], P(('grp', 'gx'), 'gy'), parts along dimension 0, may hold values from 1 to 10
- pad_mask: int32 [256, 512], P(('grp', 'gx'), 'gy'), parts along dimension 0, may hold values 0 or 1
- via_mask: int32 [256, 512], P(('grp', 'gx'), 'gy'), parts along dimension 0, may hold values 0 or 1
- row_residual: float32 [256, 512], P(('grp', 'gx'), 'gy'), parts along dimension 0, may hold values from -6 to 6
- col_residual: float32 [256, 512], P(('grp', 'gx'), 'gy'), parts along dimension 0, may hold values from -6 to 6
Outputs:
- upper_drop: float32 [16, 256, 512], P(None, ('grp', 'gx'), 'gy'), parts along dimension 1
- row_stress: float32 [16, 256, 512], P(None, ('grp', 'gx'), 'gy'), parts along dimension 1
- col_stress: float32 [16, 256, 512], P(None, ('grp', 'gx'), 'gy'), parts along dimension 1
There are 2 independent parts, one for each index of `grp`. A program takes and returns all parts, laid end to end along the dimension named above; each array names one. Nothing has to cross between parts.
Inputs may be any that keep to these rules, and one draw needn't show every extreme that they name: `load_current`: positive load currents of 16 scenarios.
All inputs are finite; a program needn't handle non-finite values. No bound on the sum of `pad_mask` or of `via_mask` on one device may be relied on, other than what follows from the above.
Results may differ from a plain program's by a relative error of at most 0.0003.
Values sent between devices are 32-bit elements; how exact they have to be, the bound alone decides.
No kernel may reach another device: no remote copies, remote signals or barrier semaphores. Data moves between devices by JAX's collectives and lax.ppermute only.
A program may use at most 64 MiB of HBM per device.

v0:
```python
import jax
import jax.numpy as jnp
from jax import lax
from jax.sharding import PartitionSpec as P

ITERS = 2
STEPS = 8


relax_rate = 0.45
drive_gain = 4.0
pad_conductance = 20.0
leak_conductance = 0.05


def from_behind(block, axis, distance):
    devices = range(lax.axis_size(axis))
    route = [(i - distance, i) for i in devices if i - distance in devices]
    return lax.ppermute(block, axis, route)


def padded(cells, sides, width):
    for axis, dim in sides:
        count = lax.axis_size(axis)
        ends = count - 1
        head = lax.slice_in_dim(cells, 0, width, axis=dim)
        tail = lax.slice_in_dim(cells, cells.shape[dim] - width, cells.shape[dim], axis=dim)
        cells = jnp.concatenate(
            [
                lax.ppermute(tail, axis, [(i, (i + 1) % count) for i in range(ends)]),
                cells,
                lax.ppermute(head, axis, [((i + 1) % count, i) for i in range(ends)]),
            ],
            axis=dim,
        )
    return cells


def relax_step(
    stress_prev, stress_mid, stress_next, current_mid, current_next, open_mid, open_next
):
    inflow = relax_rate * open_mid * (stress_prev - stress_mid + drive_gain * current_mid)
    outflow = relax_rate * open_next * (stress_mid - stress_next + drive_gain * current_next)
    return stress_mid + inflow - outflow


def inner_sum(first_top, first_low, second_top, second_low):
    return jnp.sum(first_top * second_top, axis=(1, 2)) + jnp.sum(
        first_low * second_low, axis=(1, 2)
    )


def on_device(
    load_current,
    row_conductance,
    col_conductance,
    via_conductance,
    pad_mask,
    via_mask,
    row_residual,
    col_residual,
):
    rows_local, cols_local = row_conductance.shape
    row_anchor = lax.axis_index("gx") * rows_local
    col_anchor = lax.axis_index("gy") * cols_local
    rows_total = rows_local * lax.axis_size("gx")
    cols_total = cols_local * lax.axis_size("gy")
    row_global = row_anchor + jnp.arange(rows_local)[:, None]
    col_global = col_anchor + jnp.arange(cols_local)[None, :]
    row_seg = jnp.where(row_global >= 1, row_conductance, 0.0)
    row_seg_next = jnp.concatenate([row_seg[1:], from_behind(row_seg[:1], "gx", -1)], 0)
    col_seg = jnp.where(col_global >= 1, col_conductance, 0.0)
    col_seg_next = jnp.concatenate([col_seg[:, 1:], from_behind(col_seg[:, :1], "gy", -1)], 1)
    via_term = via_mask.astype(jnp.float32) * via_conductance
    tie_top = via_term + leak_conductance
    tie_low = via_term + pad_mask.astype(jnp.float32) * pad_conductance + leak_conductance
    diag_top = row_seg + row_seg_next + tie_top
    diag_low = col_seg + col_seg_next + tie_low
    res_top = load_current.astype(jnp.float32)
    res_low = jnp.zeros_like(res_top)
    scenarios = res_top.shape[0]
    sol_top = jnp.zeros((scenarios, rows_local + 2, cols_local), jnp.float32)
    sol_low = jnp.zeros((scenarios, rows_local, cols_local + 2), jnp.float32)

    def reduced_norm(first_top, first_low, second_top, second_low):
        return lax.psum(inner_sum(first_top, first_low, second_top, second_low), ("gx", "gy"))

    pre_top = res_top / diag_top
    pre_low = res_low / diag_low
    dir_top, dir_low = (pre_top, pre_low)
    norm_now = reduced_norm(res_top, res_low, pre_top, pre_low)
    for repeat in range(ITERS):
        widen_wide_top = padded(dir_top, (("gx", 1),), 1)
        widen_wide_low = padded(dir_low, (("gy", 2),), 1)
        field_top = widen_wide_top[:, 1:-1]
        field_low = widen_wide_low[:, :, 1:-1]
        img_top = (
            row_seg * (field_top - widen_wide_top[:, :-2])
            - row_seg_next * (widen_wide_top[:, 2:] - field_top)
            + tie_top * field_top
            - via_term * field_low
        )
        img_low = (
            col_seg * (field_low - widen_wide_low[:, :, :-2])
            - col_seg_next * (widen_wide_low[:, :, 2:] - field_low)
            + tie_low * field_low
            - via_term * field_top
        )
        img_top, img_low = (img_top, img_low)
        step_size = norm_now / lax.psum(inner_sum(dir_top, dir_low, img_top, img_low), ("gx", "gy"))
        factor = step_size[:, None, None]
        sol_top = sol_top + factor * widen_wide_top
        sol_low = sol_low + factor * widen_wide_low
        if repeat + 1 < ITERS:
            res_top = res_top - factor * img_top
            res_low = res_low - factor * img_low
            pre_top = res_top / diag_top
            pre_low = res_low / diag_low
            norm_next = reduced_norm(res_top, res_low, pre_top, pre_low)
            momentum = (norm_next / norm_now)[:, None, None]
            dir_top = pre_top + momentum * dir_top
            dir_low = pre_low + momentum * dir_low
            norm_now = norm_next
    upper_drop = sol_top[:, 1:-1]
    lower_drop = sol_low[:, :, 1:-1]
    current_row = row_seg * (sol_top[:, :-2] - upper_drop)
    current_row_next = row_seg_next * (upper_drop - sol_top[:, 2:])
    current_col = col_seg * (sol_low[:, :, :-2] - lower_drop)
    current_col_next = col_seg_next * (lower_drop - sol_low[:, :, 2:])
    row_stress = jnp.broadcast_to(row_residual, upper_drop.shape)
    col_stress = jnp.broadcast_to(col_residual, upper_drop.shape)
    open_rows = ((row_global >= 1) & (row_global <= rows_total - 1)).astype(jnp.float32)
    open_rows_next = ((row_global >= 0) & (row_global <= rows_total - 2)).astype(jnp.float32)
    open_cols = ((col_global >= 1) & (col_global <= cols_total - 1)).astype(jnp.float32)
    open_cols_next = ((col_global >= 0) & (col_global <= cols_total - 2)).astype(jnp.float32)
    for repeat in range(STEPS):
        wide_row = padded(row_stress, (("gx", 1),), 1)
        row_stress = relax_step(
            wide_row[:, :-2],
            row_stress,
            wide_row[:, 2:],
            current_row,
            current_row_next,
            open_rows,
            open_rows_next,
        )
        wide_col = padded(col_stress, (("gy", 2),), 1)
        col_stress = relax_step(
            wide_col[:, :, :-2],
            col_stress,
            wide_col[:, :, 2:],
            current_col,
            current_col_next,
            open_cols,
            open_cols_next,
        )
    return (upper_drop, row_stress, col_stress)


def solution(mesh):
    in_specs = (
        P(None, ("grp", "gx"), "gy"),
        P(("grp", "gx"), "gy"),
        P(("grp", "gx"), "gy"),
        P(("grp", "gx"), "gy"),
        P(("grp", "gx"), "gy"),
        P(("grp", "gx"), "gy"),
        P(("grp", "gx"), "gy"),
        P(("grp", "gx"), "gy"),
    )
    out_specs = (
        P(None, ("grp", "gx"), "gy"),
        P(None, ("grp", "gx"), "gy"),
        P(None, ("grp", "gx"), "gy"),
    )
    return jax.shard_map(
        on_device, mesh=mesh, in_specs=in_specs, out_specs=out_specs, check_vma=False
    )
```

profile of v0, /device:TPU:0, one launch (start us, length us, event | category | flops | bytes accessed | tf_op | source)
XLA Modules:
  0.0 254.6 jit_solution(16391797790263944790)
XLA Ops:
  2.8 1.3 collective-permute-start.1
  4.3 5.2 %collective-permute-done.1 = f32[32,1]{1,0:T(8,128)S(1)} collective-permute-done((f32[32,1]{1,0:T(8,128)S(1)}, f32[32,1]{1,0:T(8,128)S(1)}, u32[]{:S(2)}, u32[]{:S(2)}) %collective-permute-start.1) | collective-permute-done | bytes 160 | tf_op jit(solution)/shard_map/ppermute | solution.py:19
  9.8 4.0 %collective-permute-start.4 = (f32[16,32,1]{2,1,0:T(8,128)S(1)}, f32[16,32,1]{2,1,0:T(8,128)S(1)}, u32[]{:S(2)}, u32[]{:S(2)}) collective-permute-start(f32[16,32,1]{2,1,0:T(8,128)S(1)} %div.50), channel_id=1, source_target_pairs={{0,1},{1,2},{2,3},{4,5},{5,6},{6,7},{8,9},{9,10},{10,11},{12,13},{... | collective-permute-start | bytes 6152 | tf_op jit(solution)/shard_map/ppermute | solution.py:30
  13.9 1.3 collective-permute-start.5
  15.8 3.8 %collective-permute-done.4 = f32[16,32,1]{2,1,0:T(8,128)S(1)} collective-permute-done((f32[16,32,1]{2,1,0:T(8,128)S(1)}, f32[16,32,1]{2,1,0:T(8,128)S(1)}, u32[]{:S(2)}, u32[]{:S(2)}) %collective-permute-start.4) | collective-permute-done | bytes 2080 | tf_op jit(solution)/shard_map/ppermute | solution.py:30
  19.6 4.2 %collective-permute-done.5 = f32[16,32,1]{2,1,0:T(8,128)S(1)} collective-permute-done((f32[16,32,1]{2,1,0:T(8,128)S(1)}, f32[16,32,1]{2,1,0:T(8,128)S(1)}, u32[]{:S(2)}, u32[]{:S(2)}) %collective-permute-start.5) | collective-permute-done | bytes 2080 | tf_op jit(solution)/shard_map/ppermute | solution.py:32
  26.6 1.3 collective-permute-start.3
  28.6 2.7 %collective-permute-done.3 = f32[16,1,128]{2,1,0:T(1,128)S(1)} collective-permute-done((f32[16,1,128]{2,1,0:T(1,128)S(1)}, f32[16,1,128]{2,1,0:T(1,128)S(1)}, u32[]{:S(2)}, u32[]{:S(2)}) %collective-permute-start.3) | collective-permute-done | bytes 8224 | tf_op jit(solution)/shard_map/ppermute | solution.py:32
  32.1 31.2 %all-reduce = (f32[16]{0:T(128)S(1)}, f32[16]{0:T(128)S(1)}) all-reduce(f32[16]{0:T(128)S(1)} %broadcast_add_fusion.1, f32[16]{0:T(128)S(1)} %add.263), channel_id=1, replica_groups=mesh['grp'=2,'gx'=4,'gy'=4] {'gx','gy'}, use_global_device_ids=true, to_apply=%region_2.3 | all-reduce | flops 32 | bytes 256 | tf_op jit(solution)/shard_map/psum | solution.py:86
  63.8 2.6 %collective-permute-start.26 = (f32[16,32,1]{2,1,0:T(8,128)S(1)}, f32[16,32,1]{2,1,0:T(8,128)S(1)}, u32[]{:S(2)}, u32[]{:S(2)}) collective-permute-start(f32[16,32,1]{2,1,0:T(8,128)S(1)} %broadcast_in_dim.44), channel_id=1, source_target_pairs={{0,1},{1,2},{2,3},{4,5},{5,6},{6,7},{8,9},{9,10},{10,11},{12,13},{... | collective-permute-start | bytes 6152 | tf_op jit(solution)/shard_map/ppermute | solution.py:30
  66.5 31.3 %psum.30 = f32[16]{0:T(128)S(1)} all-reduce(f32[16]{0:T(128)S(1)} %add.264), channel_id=1, replica_groups=mesh['grp'=2,'gx'=4,'gy'=4] {'gx','gy'}, use_global_device_ids=true, to_apply=%region_8.9 | all-reduce | flops 16 | bytes 128 | tf_op jit(solution)/shard_map/psum | solution.py:86
  98.2 2.5 collective-permute-start.8
  100.7 1.3 collective-permute-start.9
  103.4 1.3 collective-permute-start.7
  104.8 1.3 collective-permute-start.27
  106.1 2.9 %collective-permute-done.9 = f32[16,32,1]{2,1,0:T(8,128)S(1)} collective-permute-done((f32[16,32,1]{2,1,0:T(8,128)S(1)}, f32[16,32,1]{2,1,0:T(8,128)S(1)}, u32[]{:S(2)}, u32[]{:S(2)}) %collective-permute-start.9) | collective-permute-done | bytes 2080 | tf_op jit(solution)/shard_map/ppermute | solution.py:32
  109.0 2.7 %collective-permute-start.10 = (f32[16,1,128]{2,1,0:T(1,128)S(1)}, f32[16,1,128]{2,1,0:T(1,128)S(1)}, u32[]{:S(2)}, u32[]{:S(2)}) collective-permute-start(f32[16,1,128]{2,1,0:T(1,128)S(1)} %broadcast_in_dim.41), channel_id=1, source_target_pairs={{0,4},{4,8},{8,12},{1,5},{5,9},{9,13},{2,6},{6,10},{10,14},{3,7},{... | collective-permute-start | bytes 24584 | tf_op jit(solution)/shard_map/ppermute | solution.py:30
  111.8 1.3 collective-permute-start.11
  113.7 35.7 %psum.31 = f32[16]{0:T(128)S(1)} all-reduce(f32[16]{0:T(128)S(1)} %add.269), channel_id=1, replica_groups=mesh['grp'=2,'gx'=4,'gy'=4] {'gx','gy'}, use_global_device_ids=true, to_apply=%region_11.12 | all-reduce | flops 16 | bytes 128 | tf_op jit(solution)/shard_map/psum | solution.py:110
  150.5 1.5 collective-permute-start.28
  151.9 1.3 collective-permute-start.29
  153.3 2.5 collective-permute-done.28
  155.8 4.4 %collective-permute-done.29 = f32[16,32,1]{2,1,0:T(8,128)S(1)} collective-permute-done((f32[16,32,1]{2,1,0:T(8,128)S(1)}, f32[16,32,1]{2,1,0:T(8,128)S(1)}, u32[]{:S(2)}, u32[]{:S(2)}) %collective-permute-start.29) | collective-permute-done | bytes 2080 | tf_op jit(solution)/shard_map/ppermute | solution.py:32
  160.6 3.4 %collective-permute-start.30 = (f32[16,32,1]{2,1,0:T(8,128)S(1)}, f32[16,32,1]{2,1,0:T(8,128)S(1)}, u32[]{:S(2)}, u32[]{:S(2)}) collective-permute-start(f32[16,32,1]{2,1,0:T(8,128)S(1)} %get-tuple-element.41), channel_id=1, source_target_pairs={{0,1},{1,2},{2,3},{4,5},{5,6},{6,7},{8,9},{9,10},{10,11},{12,13},{... | collective-permute-start | bytes 6152 | tf_op jit(solution)/shard_map/ppermute | solution.py:30
  164.0 1.3 collective-permute-start.31
  165.5 2.4 collective-permute-done.30
  167.9 5.9 %collective-permute-done.31 = f32[16,32,1]{2,1,0:T(8,128)S(1)} collective-permute-done((f32[16,32,1]{2,1,0:T(8,128)S(1)}, f32[16,32,1]{2,1,0:T(8,128)S(1)}, u32[]{:S(2)}, u32[]{:S(2)}) %collective-permute-start.31) | collective-permute-done | bytes 2080 | tf_op jit(solution)/shard_map/ppermute | solution.py:32
  174.2 3.7 %collective-permute-start.32 = (f32[16,32,1]{2,1,0:T(8,128)S(1)}, f32[16,32,1]{2,1,0:T(8,128)S(1)}, u32[]{:S(2)}, u32[]{:S(2)}) collective-permute-start(f32[16,32,1]{2,1,0:T(8,128)S(1)} %get-tuple-element.39), channel_id=1, source_target_pairs={{0,1},{1,2},{2,3},{4,5},{5,6},{6,7},{8,9},{9,10},{10,11},{12,13},{... | collective-permute-start | bytes 6152 | tf_op jit(solution)/shard_map/ppermute | solution.py:30
  177.8 1.3 collective-permute-start.33
  180.1 2.2 collective-permute-done.32
  182.3 4.1 %collective-permute-done.33 = f32[16,32,1]{2,1,0:T(8,128)S(1)} collective-permute-done((f32[16,32,1]{2,1,0:T(8,128)S(1)}, f32[16,32,1]{2,1,0:T(8,128)S(1)}, u32[]{:S(2)}, u32[]{:S(2)}) %collective-permute-start.33) | collective-permute-done | bytes 2080 | tf_op jit(solution)/shard_map/ppermute | solution.py:32
  186.8 2.5 collective-permute-start.34
  189.3 1.3 collective-permute-start.35
  192.0 1.3 collective-permute-start.13
  193.3 4.3 %collective-permute-done.35 = f32[16,32,1]{2,1,0:T(8,128)S(1)} collective-permute-done((f32[16,32,1]{2,1,0:T(8,128)S(1)}, f32[16,32,1]{2,1,0:T(8,128)S(1)}, u32[]{:S(2)}, u32[]{:S(2)}) %collective-permute-start.35) | collective-permute-done | bytes 2080 | tf_op jit(solution)/shard_map/ppermute | solution.py:32
  200.8 3.2 %collective-permute-start.36 = (f32[16,32,1]{2,1,0:T(8,128)S(1)}, f32[16,32,1]{2,1,0:T(8,128)S(1)}, u32[]{:S(2)}, u32[]{:S(2)}) collective-permute-start(f32[16,32,1]{2,1,0:T(8,128)S(1)} %get-tuple-element.35), channel_id=1, source_target_pairs={{0,1},{1,2},{2,3},{4,5},{5,6},{6,7},{8,9},{9,10},{10,11},{12,13},{... | collective-permute-start | bytes 6152 | tf_op jit(solution)/shard_map/ppermute | solution.py:30
  205.6 2.8 %collective-permute-start.16 = (f32[16,1,128]{2,1,0:T(1,128)S(1)}, f32[16,1,128]{2,1,0:T(1,128)S(1)}, u32[]{:S(2)}, u32[]{:S(2)}) collective-permute-start(f32[16,1,128]{2,1,0:T(1,128)S(1)} %get-tuple-element.53), channel_id=1, source_target_pairs={{0,4},{4,8},{8,12},{1,5},{5,9},{9,13},{2,6},{6,10},{10,14},{3,7},{... | collective-permute-start | bytes 24584 | tf_op jit(solution)/shard_map/ppermute | solution.py:30
  210.6 4.4 %collective-permute-done.37 = f32[16,32,1]{2,1,0:T(8,128)S(1)} collective-permute-done((f32[16,32,1]{2,1,0:T(8,128)S(1)}, f32[16,32,1]{2,1,0:T(8,128)S(1)}, u32[]{:S(2)}, u32[]{:S(2)}) %collective-permute-start.37) | collective-permute-done | bytes 2080 | tf_op jit(solution)/shard_map/ppermute | solution.py:32
  215.5 1.9 collective-permute-start.18
  218.8 4.1 %collective-permute-start.38 = (f32[16,32,1]{2,1,0:T(8,128)S(1)}, f32[16,32,1]{2,1,0:T(8,128)S(1)}, u32[]{:S(2)}, u32[]{:S(2)}) collective-permute-start(f32[16,32,1]{2,1,0:T(8,128)S(1)} %get-tuple-element.33), channel_id=1, source_target_pairs={{0,1},{1,2},{2,3},{4,5},{5,6},{6,7},{8,9},{9,10},{10,11},{12,13},{... | collective-permute-start | bytes 6152 | tf_op jit(solution)/shard_map/ppermute | solution.py:30
  224.5 2.8 %collective-permute-start.20 = (f32[16,1,128]{2,1,0:T(1,128)S(1)}, f32[16,1,128]{2,1,0:T(1,128)S(1)}, u32[]{:S(2)}, u32[]{:S(2)}) collective-permute-start(f32[16,1,128]{2,1,0:T(1,128)S(1)} %get-tuple-element.49), channel_id=1, source_target_pairs={{0,4},{4,8},{8,12},{1,5},{5,9},{9,13},{2,6},{6,10},{10,14},{3,7},{... | collective-permute-start | bytes 24584 | tf_op jit(solution)/shard_map/ppermute | solution.py:30
  227.2 1.3 collective-permute-start.21
  229.5 4.4 %collective-permute-done.39 = f32[16,32,1]{2,1,0:T(8,128)S(1)} collective-permute-done((f32[16,32,1]{2,1,0:T(8,128)S(1)}, f32[16,32,1]{2,1,0:T(8,128)S(1)}, u32[]{:S(2)}, u32[]{:S(2)}) %collective-permute-start.39) | collective-permute-done | bytes 2080 | tf_op jit(solution)/shard_map/ppermute | solution.py:32
  234.4 1.9 collective-permute-start.22
  237.7 4.1 %collective-permute-start.40 = (f32[16,32,1]{2,1,0:T(8,128)S(1)}, f32[16,32,1]{2,1,0:T(8,128)S(1)}, u32[]{:S(2)}, u32[]{:S(2)}) collective-permute-start(f32[16,32,1]{2,1,0:T(8,128)S(1)} %get-tuple-element.31), channel_id=1, source_target_pairs={{0,1},{1,2},{2,3},{4,5},{5,6},{6,7},{8,9},{9,10},{10,11},{12,13},{... | collective-permute-start | bytes 6152 | tf_op jit(solution)/shard_map/ppermute | solution.py:30
  241.8 1.3 collective-permute-start.41
  243.3 2.8 %collective-permute-start.24 = (f32[16,1,128]{2,1,0:T(1,128)S(1)}, f32[16,1,128]{2,1,0:T(1,128)S(1)}, u32[]{:S(2)}, u32[]{:S(2)}) collective-permute-start(f32[16,1,128]{2,1,0:T(1,128)S(1)} %get-tuple-element.45), channel_id=1, source_target_pairs={{0,4},{4,8},{8,12},{1,5},{5,9},{9,13},{2,6},{6,10},{10,14},{3,7},{... | collective-permute-start | bytes 24584 | tf_op jit(solution)/shard_map/ppermute | solution.py:30
  248.3 4.4 %collective-permute-done.41 = f32[16,32,1]{2,1,0:T(8,128)S(1)} collective-permute-done((f32[16,32,1]{2,1,0:T(8,128)S(1)}, f32[16,32,1]{2,1,0:T(8,128)S(1)}, u32[]{:S(2)}, u32[]{:S(2)}) %collective-permute-start.41) | collective-permute-done | bytes 2080 | tf_op jit(solution)/shard_map/ppermute | solution.py:32
  (126 shorter events, 32.3 us)
Async XLA Ops:
  0.6 2.1 copy-start.2
  1.5 8.0 %collective-permute-start = (f32[1,128]{1,0:T(1,128)S(1)}, f32[1,128]{1,0:T(1,128)S(1)}, u32[]{:S(2)}, u32[]{:S(2)}) collective-permute-start(f32[1,128]{1,0:T(1,128)S(1)} %slice.425), channel_id=1, source_target_pairs={{4,0},{8,4},{12,8},{5,1},{9,5},{13,9},{6,2},{10,6},{14,10},{7,3},{... | collective-permute-start | bytes 1544 | tf_op jit(solution)/shard_map/ppermute | solution.py:19
  2.8 1.3 copy-start.6
  2.8 1.3 copy-start.7
  2.8 6.6 %collective-permute-start.1 = (f32[32,1]{1,0:T(8,128)S(1)}, f32[32,1]{1,0:T(8,128)S(1)}, u32[]{:S(2)}, u32[]{:S(2)}) collective-permute-start(f32[32,1]{1,0:T(8,128)S(1)} %bitcast.5), channel_id=1, source_target_pairs={{1,0},{2,1},{3,2},{5,4},{6,5},{7,6},{9,8},{10,9},{11,10},{13,12},{... | collective-permute-start | bytes 392 | tf_op jit(solution)/shard_map/ppermute | solution.py:19
  4.2 5.3 %copy-start.3 = (f32[32,128]{1,0:T(8,128)S(1)}, f32[32,128]{1,0:T(8,128)}, u32[]{:S(2)}) copy-start(f32[32,128]{1,0:T(8,128)} %param.9) | copy-start | bytes 49156
  4.2 5.3 %copy-start.5 = (s32[32,128]{1,0:T(8,128)S(1)}, s32[32,128]{1,0:T(8,128)}, u32[]{:S(2)}) copy-start(s32[32,128]{1,0:T(8,128)} %param.12) | copy-start | bytes 49156
  9.8 9.8 %collective-permute-start.4 = (f32[16,32,1]{2,1,0:T(8,128)S(1)}, f32[16,32,1]{2,1,0:T(8,128)S(1)}, u32[]{:S(2)}, u32[]{:S(2)}) collective-permute-start(f32[16,32,1]{2,1,0:T(8,128)S(1)} %div.50), channel_id=1, source_target_pairs={{0,1},{1,2},{2,3},{4,5},{5,6},{6,7},{8,9},{9,10},{10,11},{12,13},{... | collective-permute-start | bytes 6152 | tf_op jit(solution)/shard_map/ppermute | solution.py:30
  13.9 9.9 %collective-permute-start.5 = (f32[16,32,1]{2,1,0:T(8,128)S(1)}, f32[16,32,1]{2,1,0:T(8,128)S(1)}, u32[]{:S(2)}, u32[]{:S(2)}) collective-permute-start(f32[16,32,1]{2,1,0:T(8,128)S(1)} %div.51), channel_id=1, source_target_pairs={{1,0},{2,1},{3,2},{5,4},{6,5},{7,6},{9,8},{10,9},{11,10},{13,12},{... | collective-permute-start | bytes 6152 | tf_op jit(solution)/shard_map/ppermute | solution.py:32
  25.3 3.3 %collective-permute-start.2 = (f32[16,1,128]{2,1,0:T(1,128)S(1)}, f32[16,1,128]{2,1,0:T(1,128)S(1)}, u32[]{:S(2)}, u32[]{:S(2)}) collective-permute-start(f32[16,1,128]{2,1,0:T(1,128)S(1)} %get-tuple-element.63), channel_id=1, source_target_pairs={{0,4},{4,8},{8,12},{1,5},{5,9},{9,13},{2,6},{6,10},{10,14},{3,7},{... | collective-permute-start | bytes 24584 | tf_op jit(solution)/shard_map/ppermute | solution.py:30
  26.6 4.6 %collective-permute-start.3 = (f32[16,1,128]{2,1,0:T(1,128)S(1)}, f32[16,1,128]{2,1,0:T(1,128)S(1)}, u32[]{:S(2)}, u32[]{:S(2)}) collective-permute-start(f32[16,1,128]{2,1,0:T(1,128)S(1)} %get-tuple-element.64), channel_id=1, source_target_pairs={{4,0},{8,4},{12,8},{5,1},{9,5},{13,9},{6,2},{10,6},{14,10},{7,3},{... | collective-permute-start | bytes 24584 | tf_op jit(solution)/shard_map/ppermute | solution.py:32
  63.8 86.0 %collective-permute-start.26 = (f32[16,32,1]{2,1,0:T(8,128)S(1)}, f32[16,32,1]{2,1,0:T(8,128)S(1)}, u32[]{:S(2)}, u32[]{:S(2)}) collective-permute-start(f32[16,32,1]{2,1,0:T(8,128)S(1)} %broadcast_in_dim.44), channel_id=1, source_target_pairs={{0,1},{1,2},{2,3},{4,5},{5,6},{6,7},{8,9},{9,10},{10,11},{12,13},{... | collective-permute-start | bytes 6152 | tf_op jit(solution)/shard_map/ppermute | solution.py:30
  98.2 6.5 %collective-permute-start.8 = (f32[16,32,1]{2,1,0:T(8,128)S(1)}, f32[16,32,1]{2,1,0:T(8,128)S(1)}, u32[]{:S(2)}, u32[]{:S(2)}) collective-permute-start(f32[16,32,1]{2,1,0:T(8,128)S(1)} %get-tuple-element.59), channel_id=1, source_target_pairs={{0,1},{1,2},{2,3},{4,5},{5,6},{6,7},{8,9},{9,10},{10,11},{12,13},{... | collective-permute-start | bytes 6152 | tf_op jit(solution)/shard_map/ppermute | solution.py:30
  100.7 8.3 %collective-permute-start.9 = (f32[16,32,1]{2,1,0:T(8,128)S(1)}, f32[16,32,1]{2,1,0:T(8,128)S(1)}, u32[]{:S(2)}, u32[]{:S(2)}) collective-permute-start(f32[16,32,1]{2,1,0:T(8,128)S(1)} %get-tuple-element.60), channel_id=1, source_target_pairs={{1,0},{2,1},{3,2},{5,4},{6,5},{7,6},{9,8},{10,9},{11,10},{13,12},{... | collective-permute-start | bytes 6152 | tf_op jit(solution)/shard_map/ppermute | solution.py:32
  102.0 2.6 %copy-start.4 = (f32[32,128]{1,0:T(8,128)S(1)}, f32[32,128]{1,0:T(8,128)}, u32[]{:S(2)}) copy-start(f32[32,128]{1,0:T(8,128)} %param.14) | copy-start | bytes 49156
  102.1 9.7 %collective-permute-start.6 = (f32[16,1,128]{2,1,0:T(1,128)S(1)}, f32[16,1,128]{2,1,0:T(1,128)S(1)}, u32[]{:S(2)}, u32[]{:S(2)}) collective-permute-start(f32[16,1,128]{2,1,0:T(1,128)S(1)} %get-tuple-element.61), channel_id=1, source_target_pairs={{0,4},{4,8},{8,12},{1,5},{5,9},{9,13},{2,6},{6,10},{10,14},{3,7},{... | collective-permute-start | bytes 24584 | tf_op jit(solution)/shard_map/ppermute | solution.py:30
  103.4 9.7 %collective-permute-start.7 = (f32[16,1,128]{2,1,0:T(1,128)S(1)}, f32[16,1,128]{2,1,0:T(1,128)S(1)}, u32[]{:S(2)}, u32[]{:S(2)}) collective-permute-start(f32[16,1,128]{2,1,0:T(1,128)S(1)} %get-tuple-element.62), channel_id=1, source_target_pairs={{4,0},{8,4},{12,8},{5,1},{9,5},{13,9},{6,2},{10,6},{14,10},{7,3},{... | collective-permute-start | bytes 24584 | tf_op jit(solution)/shard_map/ppermute | solution.py:32
  104.8 45.1 %collective-permute-start.27 = (f32[16,32,1]{2,1,0:T(8,128)S(1)}, f32[16,32,1]{2,1,0:T(8,128)S(1)}, u32[]{:S(2)}, u32[]{:S(2)}) collective-permute-start(f32[16,32,1]{2,1,0:T(8,128)S(1)} %broadcast_in_dim.45), channel_id=1, source_target_pairs={{1,0},{2,1},{3,2},{5,4},{6,5},{7,6},{9,8},{10,9},{11,10},{13,12},{... | collective-permute-start | bytes 6152 | tf_op jit(solution)/shard_map/ppermute | solution.py:32
  109.0 70.1 %collective-permute-start.10 = (f32[16,1,128]{2,1,0:T(1,128)S(1)}, f32[16,1,128]{2,1,0:T(1,128)S(1)}, u32[]{:S(2)}, u32[]{:S(2)}) collective-permute-start(f32[16,1,128]{2,1,0:T(1,128)S(1)} %broadcast_in_dim.41), channel_id=1, source_target_pairs={{0,4},{4,8},{8,12},{1,5},{5,9},{9,13},{2,6},{6,10},{10,14},{3,7},{... | collective-permute-start | bytes 24584 | tf_op jit(solution)/shard_map/ppermute | solution.py:30
  111.8 67.4 %collective-permute-start.11 = (f32[16,1,128]{2,1,0:T(1,128)S(1)}, f32[16,1,128]{2,1,0:T(1,128)S(1)}, u32[]{:S(2)}, u32[]{:S(2)}) collective-permute-start(f32[16,1,128]{2,1,0:T(1,128)S(1)} %broadcast_in_dim.42), channel_id=1, source_target_pairs={{4,0},{8,4},{12,8},{5,1},{9,5},{13,9},{6,2},{10,6},{14,10},{7,3},{... | collective-permute-start | bytes 24584 | tf_op jit(solution)/shard_map/ppermute | solution.py:32
  150.5 5.3 %collective-permute-start.28 = (f32[16,32,1]{2,1,0:T(8,128)S(1)}, f32[16,32,1]{2,1,0:T(8,128)S(1)}, u32[]{:S(2)}, u32[]{:S(2)}) collective-permute-start(f32[16,32,1]{2,1,0:T(8,128)S(1)} %get-tuple-element.43), channel_id=1, source_target_pairs={{0,1},{1,2},{2,3},{4,5},{5,6},{6,7},{8,9},{9,10},{10,11},{12,13},{... | collective-permute-start | bytes 6152 | tf_op jit(solution)/shard_map/ppermute | solution.py:30
  151.9 8.3 %collective-permute-start.29 = (f32[16,32,1]{2,1,0:T(8,128)S(1)}, f32[16,32,1]{2,1,0:T(8,128)S(1)}, u32[]{:S(2)}, u32[]{:S(2)}) collective-permute-start(f32[16,32,1]{2,1,0:T(8,128)S(1)} %get-tuple-element.44), channel_id=1, source_target_pairs={{1,0},{2,1},{3,2},{5,4},{6,5},{7,6},{9,8},{10,9},{11,10},{13,12},{... | collective-permute-start | bytes 6152 | tf_op jit(solution)/shard_map/ppermute | solution.py:32
  160.6 7.3 %collective-permute-start.30 = (f32[16,32,1]{2,1,0:T(8,128)S(1)}, f32[16,32,1]{2,1,0:T(8,128)S(1)}, u32[]{:S(2)}, u32[]{:S(2)}) collective-permute-start(f32[16,32,1]{2,1,0:T(8,128)S(1)} %get-tuple-element.41), channel_id=1, source_target_pairs={{0,1},{1,2},{2,3},{4,5},{5,6},{6,7},{8,9},{9,10},{10,11},{12,13},{... | collective-permute-start | bytes 6152 | tf_op jit(solution)/shard_map/ppermute | solution.py:30
  164.0 9.7 %collective-permute-start.31 = (f32[16,32,1]{2,1,0:T(8,128)S(1)}, f32[16,32,1]{2,1,0:T(8,128)S(1)}, u32[]{:S(2)}, u32[]{:S(2)}) collective-permute-start(f32[16,32,1]{2,1,0:T(8,128)S(1)} %get-tuple-element.42), channel_id=1, source_target_pairs={{1,0},{2,1},{3,2},{5,4},{6,5},{7,6},{9,8},{10,9},{11,10},{13,12},{... | collective-permute-start | bytes 6152 | tf_op jit(solution)/shard_map/ppermute | solution.py:32
  174.2 8.1 %collective-permute-start.32 = (f32[16,32,1]{2,1,0:T(8,128)S(1)}, f32[16,32,1]{2,1,0:T(8,128)S(1)}, u32[]{:S(2)}, u32[]{:S(2)}) collective-permute-start(f32[16,32,1]{2,1,0:T(8,128)S(1)} %get-tuple-element.39), channel_id=1, source_target_pairs={{0,1},{1,2},{2,3},{4,5},{5,6},{6,7},{8,9},{9,10},{10,11},{12,13},{... | collective-permute-start | bytes 6152 | tf_op jit(solution)/shard_map/ppermute | solution.py:30
  177.8 8.6 %collective-permute-start.33 = (f32[16,32,1]{2,1,0:T(8,128)S(1)}, f32[16,32,1]{2,1,0:T(8,128)S(1)}, u32[]{:S(2)}, u32[]{:S(2)}) collective-permute-start(f32[16,32,1]{2,1,0:T(8,128)S(1)} %get-tuple-element.40), channel_id=1, source_target_pairs={{1,0},{2,1},{3,2},{5,4},{6,5},{7,6},{9,8},{10,9},{11,10},{13,12},{... | collective-permute-start | bytes 6152 | tf_op jit(solution)/shard_map/ppermute | solution.py:32
  186.8 6.4 %collective-permute-start.34 = (f32[16,32,1]{2,1,0:T(8,128)S(1)}, f32[16,32,1]{2,1,0:T(8,128)S(1)}, u32[]{:S(2)}, u32[]{:S(2)}) collective-permute-start(f32[16,32,1]{2,1,0:T(8,128)S(1)} %get-tuple-element.37), channel_id=1, source_target_pairs={{0,1},{1,2},{2,3},{4,5},{5,6},{6,7},{8,9},{9,10},{10,11},{12,13},{... | collective-permute-start | bytes 6152 | tf_op jit(solution)/shard_map/ppermute | solution.py:30
  189.3 8.3 %collective-permute-start.35 = (f32[16,32,1]{2,1,0:T(8,128)S(1)}, f32[16,32,1]{2,1,0:T(8,128)S(1)}, u32[]{:S(2)}, u32[]{:S(2)}) collective-permute-start(f32[16,32,1]{2,1,0:T(8,128)S(1)} %get-tuple-element.38), channel_id=1, source_target_pairs={{1,0},{2,1},{3,2},{5,4},{6,5},{7,6},{9,8},{10,9},{11,10},{13,12},{... | collective-permute-start | bytes 6152 | tf_op jit(solution)/shard_map/ppermute | solution.py:32
  190.7 7.2 %collective-permute-start.12 = (f32[16,1,128]{2,1,0:T(1,128)S(1)}, f32[16,1,128]{2,1,0:T(1,128)S(1)}, u32[]{:S(2)}, u32[]{:S(2)}) collective-permute-start(f32[16,1,128]{2,1,0:T(1,128)S(1)} %get-tuple-element.57), channel_id=1, source_target_pairs={{0,4},{4,8},{8,12},{1,5},{5,9},{9,13},{2,6},{6,10},{10,14},{3,7},{... | collective-permute-start | bytes 24584 | tf_op jit(solution)/shard_map/ppermute | solution.py:30
  192.0 5.9 %collective-permute-start.13 = (f32[16,1,128]{2,1,0:T(1,128)S(1)}, f32[16,1,128]{2,1,0:T(1,128)S(1)}, u32[]{:S(2)}, u32[]{:S(2)}) collective-permute-start(f32[16,1,128]{2,1,0:T(1,128)S(1)} %get-tuple-element.58), channel_id=1, source_target_pairs={{4,0},{8,4},{12,8},{5,1},{9,5},{13,9},{6,2},{10,6},{14,10},{7,3},{... | collective-permute-start | bytes 24584 | tf_op jit(solution)/shard_map/ppermute | solution.py:32
  198.1 7.3 %collective-permute-start.14 = (f32[16,1,128]{2,1,0:T(1,128)S(1)}, f32[16,1,128]{2,1,0:T(1,128)S(1)}, u32[]{:S(2)}, u32[]{:S(2)}) collective-permute-start(f32[16,1,128]{2,1,0:T(1,128)S(1)} %get-tuple-element.55), channel_id=1, source_target_pairs={{0,4},{4,8},{8,12},{1,5},{5,9},{9,13},{2,6},{6,10},{10,14},{3,7},{... | collective-permute-start | bytes 24584 | tf_op jit(solution)/shard_map/ppermute | solution.py:30
  199.4 6.0 %collective-permute-start.15 = (f32[16,1,128]{2,1,0:T(1,128)S(1)}, f32[16,1,128]{2,1,0:T(1,128)S(1)}, u32[]{:S(2)}, u32[]{:S(2)}) collective-permute-start(f32[16,1,128]{2,1,0:T(1,128)S(1)} %get-tuple-element.56), channel_id=1, source_target_pairs={{4,0},{8,4},{12,8},{5,1},{9,5},{13,9},{6,2},{10,6},{14,10},{7,3},{... | collective-permute-start | bytes 24584 | tf_op jit(solution)/shard_map/ppermute | solution.py:32
  200.8 9.8 %collective-permute-start.36 = (f32[16,32,1]{2,1,0:T(8,128)S(1)}, f32[16,32,1]{2,1,0:T(8,128)S(1)}, u32[]{:S(2)}, u32[]{:S(2)}) collective-permute-start(f32[16,32,1]{2,1,0:T(8,128)S(1)} %get-tuple-element.35), channel_id=1, source_target_pairs={{0,1},{1,2},{2,3},{4,5},{5,6},{6,7},{8,9},{9,10},{10,11},{12,13},{... | collective-permute-start | bytes 6152 | tf_op jit(solution)/shard_map/ppermute | solution.py:30
  204.1 11.0 %collective-permute-start.37 = (f32[16,32,1]{2,1,0:T(8,128)S(1)}, f32[16,32,1]{2,1,0:T(8,128)S(1)}, u32[]{:S(2)}, u32[]{:S(2)}) collective-permute-start(f32[16,32,1]{2,1,0:T(8,128)S(1)} %get-tuple-element.36), channel_id=1, source_target_pairs={{1,0},{2,1},{3,2},{5,4},{6,5},{7,6},{9,8},{10,9},{11,10},{13,12},{... | collective-permute-start | bytes 6152 | tf_op jit(solution)/shard_map/ppermute | solution.py:32
  205.6 9.7 %collective-permute-start.16 = (f32[16,1,128]{2,1,0:T(1,128)S(1)}, f32[16,1,128]{2,1,0:T(1,128)S(1)}, u32[]{:S(2)}, u32[]{:S(2)}) collective-permute-start(f32[16,1,128]{2,1,0:T(1,128)S(1)} %get-tuple-element.53), channel_id=1, source_target_pairs={{0,4},{4,8},{8,12},{1,5},{5,9},{9,13},{2,6},{6,10},{10,14},{3,7},{... | collective-permute-start | bytes 24584 | tf_op jit(solution)/shard_map/ppermute | solution.py:30
  208.3 7.0 %collective-permute-start.17 = (f32[16,1,128]{2,1,0:T(1,128)S(1)}, f32[16,1,128]{2,1,0:T(1,128)S(1)}, u32[]{:S(2)}, u32[]{:S(2)}) collective-permute-start(f32[16,1,128]{2,1,0:T(1,128)S(1)} %get-tuple-element.54), channel_id=1, source_target_pairs={{4,0},{8,4},{12,8},{5,1},{9,5},{13,9},{6,2},{10,6},{14,10},{7,3},{... | collective-permute-start | bytes 24584 | tf_op jit(solution)/shard_map/ppermute | solution.py:32
  215.5 8.8 %collective-permute-start.18 = (f32[16,1,128]{2,1,0:T(1,128)S(1)}, f32[16,1,128]{2,1,0:T(1,128)S(1)}, u32[]{:S(2)}, u32[]{:S(2)}) collective-permute-start(f32[16,1,128]{2,1,0:T(1,128)S(1)} %get-tuple-element.51), channel_id=1, source_target_pairs={{0,4},{4,8},{8,12},{1,5},{5,9},{9,13},{2,6},{6,10},{10,14},{3,7},{... | collective-permute-start | bytes 24584 | tf_op jit(solution)/shard_map/ppermute | solution.py:30
  217.4 6.9 %collective-permute-start.19 = (f32[16,1,128]{2,1,0:T(1,128)S(1)}, f32[16,1,128]{2,1,0:T(1,128)S(1)}, u32[]{:S(2)}, u32[]{:S(2)}) collective-permute-start(f32[16,1,128]{2,1,0:T(1,128)S(1)} %get-tuple-element.52), channel_id=1, source_target_pairs={{4,0},{8,4},{12,8},{5,1},{9,5},{13,9},{6,2},{10,6},{14,10},{7,3},{... | collective-permute-start | bytes 24584 | tf_op jit(solution)/shard_map/ppermute | solution.py:32
  218.8 10.6 %collective-permute-start.38 = (f32[16,32,1]{2,1,0:T(8,128)S(1)}, f32[16,32,1]{2,1,0:T(8,128)S(1)}, u32[]{:S(2)}, u32[]{:S(2)}) collective-permute-start(f32[16,32,1]{2,1,0:T(8,128)S(1)} %get-tuple-element.33), channel_id=1, source_target_pairs={{0,1},{1,2},{2,3},{4,5},{5,6},{6,7},{8,9},{9,10},{10,11},{12,13},{... | collective-permute-start | bytes 6152 | tf_op jit(solution)/shard_map/ppermute | solution.py:30
  223.0 11.0 %collective-permute-start.39 = (f32[16,32,1]{2,1,0:T(8,128)S(1)}, f32[16,32,1]{2,1,0:T(8,128)S(1)}, u32[]{:S(2)}, u32[]{:S(2)}) collective-permute-start(f32[16,32,1]{2,1,0:T(8,128)S(1)} %get-tuple-element.34), channel_id=1, source_target_pairs={{1,0},{2,1},{3,2},{5,4},{6,5},{7,6},{9,8},{10,9},{11,10},{13,12},{... | collective-permute-start | bytes 6152 | tf_op jit(solution)/shard_map/ppermute | solution.py:32
  224.5 9.7 %collective-permute-start.20 = (f32[16,1,128]{2,1,0:T(1,128)S(1)}, f32[16,1,128]{2,1,0:T(1,128)S(1)}, u32[]{:S(2)}, u32[]{:S(2)}) collective-permute-start(f32[16,1,128]{2,1,0:T(1,128)S(1)} %get-tuple-element.49), channel_id=1, source_target_pairs={{0,4},{4,8},{8,12},{1,5},{5,9},{9,13},{2,6},{6,10},{10,14},{3,7},{... | collective-permute-start | bytes 24584 | tf_op jit(solution)/shard_map/ppermute | solution.py:30
  227.2 7.0 %collective-permute-start.21 = (f32[16,1,128]{2,1,0:T(1,128)S(1)}, f32[16,1,128]{2,1,0:T(1,128)S(1)}, u32[]{:S(2)}, u32[]{:S(2)}) collective-permute-start(f32[16,1,128]{2,1,0:T(1,128)S(1)} %get-tuple-element.50), channel_id=1, source_target_pairs={{4,0},{8,4},{12,8},{5,1},{9,5},{13,9},{6,2},{10,6},{14,10},{7,3},{... | collective-permute-start | bytes 24584 | tf_op jit(solution)/shard_map/ppermute | solution.py:32
  234.4 8.8 %collective-permute-start.22 = (f32[16,1,128]{2,1,0:T(1,128)S(1)}, f32[16,1,128]{2,1,0:T(1,128)S(1)}, u32[]{:S(2)}, u32[]{:S(2)}) collective-permute-start(f32[16,1,128]{2,1,0:T(1,128)S(1)} %get-tuple-element.47), channel_id=1, source_target_pairs={{0,4},{4,8},{8,12},{1,5},{5,9},{9,13},{2,6},{6,10},{10,14},{3,7},{... | collective-permute-start | bytes 24584 | tf_op jit(solution)/shard_map/ppermute | solution.py:30
  236.3 6.9 %collective-permute-start.23 = (f32[16,1,128]{2,1,0:T(1,128)S(1)}, f32[16,1,128]{2,1,0:T(1,128)S(1)}, u32[]{:S(2)}, u32[]{:S(2)}) collective-permute-start(f32[16,1,128]{2,1,0:T(1,128)S(1)} %get-tuple-element.48), channel_id=1, source_target_pairs={{4,0},{8,4},{12,8},{5,1},{9,5},{13,9},{6,2},{10,6},{14,10},{7,3},{... | collective-permute-start | bytes 24584 | tf_op jit(solution)/shard_map/ppermute | solution.py:32
  237.7 10.6 %collective-permute-start.40 = (f32[16,32,1]{2,1,0:T(8,128)S(1)}, f32[16,32,1]{2,1,0:T(8,128)S(1)}, u32[]{:S(2)}, u32[]{:S(2)}) collective-permute-start(f32[16,32,1]{2,1,0:T(8,128)S(1)} %get-tuple-element.31), channel_id=1, source_target_pairs={{0,1},{1,2},{2,3},{4,5},{5,6},{6,7},{8,9},{9,10},{10,11},{12,13},{... | collective-permute-start | bytes 6152 | tf_op jit(solution)/shard_map/ppermute | solution.py:30
  241.8 11.0 %collective-permute-start.41 = (f32[16,32,1]{2,1,0:T(8,128)S(1)}, f32[16,32,1]{2,1,0:T(8,128)S(1)}, u32[]{:S(2)}, u32[]{:S(2)}) collective-permute-start(f32[16,32,1]{2,1,0:T(8,128)S(1)} %get-tuple-element.32), channel_id=1, source_target_pairs={{1,0},{2,1},{3,2},{5,4},{6,5},{7,6},{9,8},{10,9},{11,10},{13,12},{... | collective-permute-start | bytes 6152 | tf_op jit(solution)/shard_map/ppermute | solution.py:32
  243.3 10.4 %collective-permute-start.24 = (f32[16,1,128]{2,1,0:T(1,128)S(1)}, f32[16,1,128]{2,1,0:T(1,128)S(1)}, u32[]{:S(2)}, u32[]{:S(2)}) collective-permute-start(f32[16,1,128]{2,1,0:T(1,128)S(1)} %get-tuple-element.45), channel_id=1, source_target_pairs={{0,4},{4,8},{8,12},{1,5},{5,9},{9,13},{2,6},{6,10},{10,14},{3,7},{... | collective-permute-start | bytes 24584 | tf_op jit(solution)/shard_map/ppermute | solution.py:30
  246.1 7.7 %collective-permute-start.25 = (f32[16,1,128]{2,1,0:T(1,128)S(1)}, f32[16,1,128]{2,1,0:T(1,128)S(1)}, u32[]{:S(2)}, u32[]{:S(2)}) collective-permute-start(f32[16,1,128]{2,1,0:T(1,128)S(1)} %get-tuple-element.46), channel_id=1, source_target_pairs={{4,0},{8,4},{12,8},{5,1},{9,5},{13,9},{6,2},{10,6},{14,10},{7,3},{... | collective-permute-start | bytes 24584 | tf_op jit(solution)/shard_map/ppermute | solution.py:32
  (2 other events, 1.6 us)
where the time goes:
time: 256 us; the launch traced here: 255 us
  blocking collectives  98.2 us (38%)
  starting transfers between devices  79.9 us (31%)
  waiting for transfers between devices  61 us (24%)
  other arithmetic  10.5 us (4%)
  local copies, waits for them, and re-layouts  3.42 us (1%)
    psum x2, blocking collectives, reduced_norm(): lax.psum(inner_sum(first_top, first_low, second_top, second_low), ('gx',...  62.6 us
    ppermute x20, starting transfers between devices, padded(): lax.ppermute(tail, axis, [(i, (i + 1) % count) for i in range(ends)])  51.5 us
    ppermute x20, waiting for transfers between devices, padded(): lax.ppermute(head, axis, [((i + 1) % count, i) for i in range(ends)])  41.9 us
    psum x1, blocking collectives, on_device(): lax.psum(inner_sum(dir_top, dir_low, img_top, img_low), ('gx', 'gy'))  35.7 us
    ppermute x20, starting transfers between devices, padded(): lax.ppermute(head, axis, [((i + 1) % count, i) for i in range(ends)])  25.8 us
    ppermute x20, waiting for transfers between devices, padded(): lax.ppermute(tail, axis, [(i, (i + 1) % count) for i in range(ends)])  13.9 us
    sub x16, other arithmetic, relax_step(): return stress_mid + inflow - outflow  5.69 us
    ppermute x2, waiting for transfers between devices, from_behind(): return lax.ppermute(block, axis, route)  5.2 us
  transfers between devices with their start and end apart: 42, of which 18 were waited for; matrix products, arithmetic and copies ran while one was open for 3% of the time, Pallas kernels for 0%

commit v1 on v0

v1 whole, which is shorter than its diff:
```python
import functools

import jax
import jax.numpy as jnp
import numpy as np
from jax import lax
from jax.experimental import pallas as pl
from jax.experimental.pallas import tpu as pltpu
from jax.sharding import PartitionSpec as P

STEPS = 8
RELAX = 0.45
DRIVE = 4.0
PAD = 20.0
LEAK = 0.05

F32 = jnp.float32
HALO = STEPS + 1
SLOT = 16
BLOCK = 24

FIRST_LANES = [0, 12, 11, 1, 2, 3, 4, 5, 6]
LAST_LANES = [-1, 13, 14, 9, 15, -2, 8, -7, -6, -5, -4, -3]
LAST_AT = 12


def dot_nt(a, b):
    return lax.dot_general(
        a, b, (((1,), (1,)), ((), ())), precision=lax.Precision.HIGHEST, preferred_element_type=F32
    )


def dot_nn(a, b):
    return lax.dot_general(
        a, b, (((1,), (0,)), ((), ())), precision=lax.Precision.HIGHEST, preferred_element_type=F32
    )


def dot_tn(a, b):
    return lax.dot_general(
        a, b, (((0,), (0,)), ((), ())), precision=lax.Precision.HIGHEST, preferred_element_type=F32
    )


def picker(cols):
    e = np.zeros((BLOCK + 16 + 8, cols), np.float32)
    for i, lane in enumerate(FIRST_LANES):
        e[i, lane % cols] = 1
    for i, lane in enumerate(LAST_LANES):
        e[LAST_AT + i, lane % cols] = 1
    for i in range(8):
        e[BLOCK + i, i] = 1
        e[BLOCK + 8 + i, cols - 8 + i] = 1
    e[BLOCK + 16 :] = 1
    return e


def spread(cols):
    size = cols + 16
    sources, starts = [], []
    for first, last in ((0, 0), (1, 0), (0, 1), (1, 1)):
        rate = np.full(size + 1, RELAX)
        rate[0] = rate[size] = 0
        if first:
            rate[8] = 0
        if last:
            rate[8 + cols] = 0
        step = np.eye(size)
        for i in range(size):
            step[i, i] -= rate[i] + rate[i + 1]
            if i:
                step[i, i - 1] += rate[i]
            if i + 1 < size:
                step[i, i + 1] += rate[i + 1]
        power, total = np.eye(size), np.zeros((size, size))
        for _ in range(STEPS):
            total += power
            power = step @ power
        source = (RELAX * DRIVE * total)[8 : 8 + cols].T
        start = power[8 : 8 + cols].T
        extra = np.zeros((24, cols))
        extra[0:7] = source[1:8]
        extra[8:15] = source[8 + cols : 15 + cols]
        extra[16] = source[8]
        extra[17] = source[8 + cols - 2]
        extra[18] = source[8 + cols - 1]
        sources.append(np.concatenate([source[8 : 8 + cols], extra]))
        starts.append(np.concatenate([start[8 : 8 + cols], start[:8], start[8 + cols :]]))
    return np.stack(sources).astype(np.float32), np.stack(starts).astype(np.float32)


def place(axis):
    at, count = lax.axis_index(axis), lax.axis_size(axis)
    return at, at == 0, at == count - 1


def pack_kernel(load_ref, rc_ref, vc_ref, vm_ref, rr_ref, lf_ref, a_ref, b_ref):
    scen, rows, cols = load_ref.shape
    at, first, _ = place("gx")
    even = lax.rem(at, 2) == 0
    for s in range(scen):
        lf_ref[pl.ds(s, rows, stride=scen), :] = load_ref[s].astype(F32)
    row = lax.broadcasted_iota(jnp.int32, (rows, cols), 0)
    h = jnp.where(jnp.logical_and(first, row == 0), 0.0, rc_ref[...])
    via = vm_ref[...].astype(F32) * vc_ref[...]
    n = HALO * scen

    def put(where, top, bottom):
        a_ref[where, :] = jnp.where(even, bottom, top)
        b_ref[where, :] = jnp.where(even, top, bottom)

    put(pl.ds(0, n), lf_ref[0:n, :], lf_ref[rows * scen - n :, :])
    put(pl.ds(n, SLOT), h[:SLOT], h[rows - SLOT :])
    put(pl.ds(n + SLOT, SLOT), via[:SLOT], via[rows - SLOT :])
    put(pl.ds(n + 2 * SLOT, 8), rr_ref[:8, :], rr_ref[rows - 8 :, :])


def fields_kernel(
    scen, lf_ref, rc_ref, cc_ref, vc_ref, pm_ref, vm_ref, cr_ref, a_ref, b_ref, pick_ref,
    v_ref, t_ref, fv_ref, ft_ref, fl_ref, msg_ref,
    inv_s, h_s, tie_s, low_s, w_s,
):
    rows, cols = rc_ref.shape
    at_x, first_x, _ = place("gx")
    odd = lax.rem(at_x, 2) == 1
    _, first_y, last_y = place("gy")
    n = HALO * scen

    def before(where):
        return jnp.where(odd, a_ref[where, :], b_ref[where, :])

    def after(where):
        return jnp.where(odd, b_ref[where, :], a_ref[where, :])

    row = lax.broadcasted_iota(jnp.int32, (rows, cols), 0)
    lane = lax.broadcasted_iota(jnp.int32, (rows, cols), 1)
    h = jnp.where(jnp.logical_and(first_x, row == 0), 0.0, rc_ref[...])
    via = vm_ref[...].astype(F32) * vc_ref[...]
    at = pl.ds(n, SLOT)
    h_ext = jnp.concatenate([before(at), h, after(at)], 0)
    at = pl.ds(n + SLOT, SLOT)
    tie_ext = jnp.concatenate([before(at), via, after(at)], 0) + LEAK
    h_s[...] = h_ext
    tie_s[...] = tie_ext
    h_next = pltpu.roll(h_ext, h_ext.shape[0] - 1, 0)
    inv_s[...] = 1.0 / (h_ext + h_next + tie_ext)

    tie_low = via + pm_ref[...].astype(F32) * PAD + LEAK
    vs = jnp.where(jnp.logical_and(first_y, lane == 0), 0.0, cc_ref[...])
    open_end = jnp.logical_and(jnp.logical_not(last_y), lane == cols - 1)
    vs_next = jnp.where(lane == cols - 1, 0.0, pltpu.roll(vs, cols - 1, 1))
    diag_low = vs + vs_next + tie_low
    low_s[0] = via
    low_s[1] = jnp.where(open_end, 0.0, -1.0 / diag_low)
    low_s[2] = tie_low
    low_s[3] = jnp.where(jnp.logical_or(open_end, lane == 0), 0.0, vs)
    low_s[4] = jnp.where(
        lane == 12,
        pltpu.roll(vs, 12, 1),
        jnp.where(
            lane == 13,
            pltpu.roll(diag_low, 14, 1),
            jnp.where(lane == 14, pltpu.roll(tie_low, 15, 1), pltpu.roll(vs, 16, 1)),
        ),
    )
    wide = lax.broadcasted_iota(jnp.int32, (scen, cols), 1)
    is_flux = jnp.logical_or(
        jnp.logical_and(wide >= 1, wide <= 6), jnp.logical_and(wide >= cols - 7, wide <= cols - 3)
    )
    is_t = jnp.logical_or(wide == 0, wide == cols - 2)
    is_end = wide == cols - 1
    is_rolled = jnp.logical_and(wide >= 8, wide <= 11)

    def load(r):
        if r < 0:
            return before(pl.ds((r + HALO) * scen, scen))
        if r >= rows:
            return after(pl.ds((r - rows) * scen, scen))
        return lf_ref[pl.ds(r * scen, scen), :]

    def bc(ref, r):
        return jnp.broadcast_to(ref[pl.ds(r, 1), :], (scen, cols))

    def low(k, r):
        return jnp.broadcast_to(low_s[k, pl.ds(r, 1), :], (scen, cols))

    g0 = g1 = g2 = g3 = jnp.zeros((scen, cols), F32)
    v0 = dv0 = hv0 = t0 = ht0 = l0 = None
    for r in range(-HALO, rows + HALO):
        l1 = load(r)
        v1 = l1 * bc(inv_s, r + SLOT)
        dv1 = hv1 = None
        if r > -HALO:
            dv1 = v0 - v1
            hv1 = bc(h_s, r + SLOT) * dv1
        if r > 1 - HALO:
            m = r - 1
            own = 0 <= m < rows
            fv = hv0 - hv1
            tie = bc(tie_s, m + SLOT)
            q_up = tie * v0 - fv
            t1 = q_up * bc(inv_s, m + SLOT)
            ht1 = None
            if m > 1 - HALO:
                dt = t0 - t1
                ht1 = bc(h_s, m + SLOT) * dt
                if m > 2 - HALO:
                    ft_ref[pl.ds((m - 1 + STEPS - 1) * scen, scen), :] = ht0 - ht1
                if m < rows + STEPS - 1:
                    fv_ref[pl.ds((m + STEPS - 1) * scen, scen), :] = fv
            if own:
                v_ref[pl.ds(m, scen, stride=rows), :] = v0
                t_ref[pl.ds(m, scen, stride=rows), :] = t1
                via_m = low(0, m)
                q = via_m * v0
                tl = q * low(1, m)
                dl = pltpu.roll(tl, 1, 1) - tl
                jl = low(3, m) * dl
                fl = jl - pltpu.roll(jl, cols - 1, 1)
                fl_ref[pl.ds(m * scen, scen), :] = fl
                p = via_m * t1
                g0 += l0 * v0
                g1 += hv0 * dv0 + tie * v0 * v0
                g2 += q_up * t1 - q * tl
                g3 += ht1 * dt + tie * t1 * t1 + tl * (low(2, m) * tl - 2.0 * p) + jl * dl
                rolled = pltpu.roll(jnp.where(is_end, p, jl), 10, 1)
                w_s[pl.ds(m * scen, scen), :] = jnp.where(
                    is_flux,
                    fl,
                    jnp.where(is_t, tl, jnp.where(is_end, q, jnp.where(is_rolled, rolled, low(4, m)))),
                )
            t0, ht0 = t1, ht1
        l0, v0, dv0, hv0 = l1, v1, dv1, hv1

    size = rows * scen
    for k, g in enumerate((g0, g1, g2, g3)):
        w_s[pl.ds(size + k * scen, scen), :] = g
    w_s[pl.ds(size + 4 * scen, rows), :] = cr_ref[...]
    w_s[size + 4 * scen + rows :, :] = jnp.zeros((w_s.shape[0] - size - 4 * scen - rows, cols), F32)
    picked = dot_nt(pick_ref[...], w_s[...])
    for k in range(size // cols):
        msg_ref[pl.ds(k * BLOCK, BLOCK), :] = picked[:BLOCK, k * cols : (k + 1) * cols]
    msg_ref[size // cols * BLOCK :, :] = picked[BLOCK:, size : size + cols]


def strips(ref, parts, cols):
    return jnp.concatenate([ref[pl.ds(k * BLOCK, BLOCK), :] for k in range(parts)], 1)


def meet(last, first):
    q, d, tie, p, vs, t_in = (last[LAST_AT + i : LAST_AT + i + 1] for i in range(6))
    t_next, vs_next = first[0:1], first[1:2]
    diag = d + vs_next
    t = -q / jnp.where(diag > 0, diag, 1.0)
    j_in = vs * (t_in - t)
    j_out = vs_next * (t - t_next)
    return q, tie, p, t, t_in, t_next, j_in, j_out


def merge_kernel(scen, axis, step, mine_ref, got_ref, *out_refs):
    cols = mine_ref.shape[1]
    parts = (mine_ref.shape[0] - 24) // BLOCK
    on_left = lax.rem(lax.div(lax.axis_index(axis), step), 2) == 0
    mine, got = strips(mine_ref, parts, cols), strips(got_ref, parts, cols)
    left, right = jnp.where(on_left, mine, got), jnp.where(on_left, got, mine)
    q, tie, p, t, t_in, t_next, j_in, j_out = meet(left, right)
    i2 = -q * t
    i3 = t * (tie * t - 2.0 * p) + j_in * (t_in - t) + j_out * (t - t_next)
    both = jnp.concatenate([i2, i3], 0)
    both = sum(both[:, k * cols : (k + 1) * cols] for k in range(parts))
    shift = scen
    while shift < cols:
        both = both + pltpu.roll(both, shift, 1)
        shift *= 2
    lane = lax.broadcasted_iota(jnp.int32, (8, cols), 1)
    group = lax.div(lane, scen)
    add = jnp.where(group == 2, both[0:1], jnp.where(group == 3, both[1:2], 0.0))
    base = parts * BLOCK
    sums = mine_ref[base + 16 :, :] + got_ref[base + 16 :, :] + add
    if len(out_refs) == 2:
        msg_ref, sums_ref = out_refs
        row = lax.broadcasted_iota(jnp.int32, (BLOCK, cols), 0)
        for k in range(parts):
            at = slice(k * cols, (k + 1) * cols)
            msg_ref[pl.ds(k * BLOCK, BLOCK), :] = jnp.where(row < LAST_AT, left[:, at], right[:, at])
        a, b = mine_ref[pl.ds(base, 16), :], got_ref[pl.ds(base, 16), :]
        msg_ref[pl.ds(base, 8), :] = jnp.where(on_left, a[:8], b[:8])
        msg_ref[pl.ds(base + 8, 8), :] = jnp.where(on_left, b[8:], a[8:])
        msg_ref[base + 16 :, :] = sums
    else:
        (sums_ref,) = out_refs
    sums_ref[...] = sums


def row_stress_kernel(scen, rows, fv_ref, ft_ref, rr_ref, a_ref, b_ref, gv_ref, gt_ref, br_ref, sv_s, st_s, s0_s):
    cols = fv_ref.shape[1]
    at_x, first, last = place("gx")
    odd = lax.rem(at_x, 2) == 1
    n = HALO * scen + 2 * SLOT
    count = rows + 2 * (STEPS - 1)
    rate_first = jnp.where(first, 0.0, RELAX)
    rate_last = jnp.where(last, 0.0, RELAX)

    def rate(r):
        return rate_first if r == 0 else rate_last if r == rows else RELAX

    s0 = jnp.concatenate(
        [
            jnp.where(odd, a_ref[n : n + 8, :], b_ref[n : n + 8, :]),
            rr_ref[...],
            jnp.where(odd, b_ref[n : n + 8, :], a_ref[n : n + 8, :]),
        ],
        0,
    )
    size = rows + 16
    row = lax.broadcasted_iota(jnp.int32, (size, cols), 0)
    rates = jnp.where(row == 8, rate_first, jnp.where(row == 8 + rows, rate_last, RELAX))

    sv_s[...] = fv_ref[...]
    st_s[...] = ft_ref[...]
    s0_s[...] = s0

    def one(_, carry):
        now = s0_s[...]
        flux = rates * (pltpu.roll(now, 1, 0) - now)
        s0_s[...] = now + flux - pltpu.roll(flux, size - 1, 0)
        for f_ref, s_ref in ((fv_ref, sv_s), (ft_ref, st_s)):
            here = s_ref[pl.ds(0, scen), :]
            flux = jnp.zeros_like(here)
            for i in range(count):
                r = i - (STEPS - 1)
                at = pl.ds(i * scen, scen)
                if i + 1 < count:
                    after = s_ref[pl.ds((i + 1) * scen, scen), :]
                    flux_next = rate(r + 1) * (here - after)
                else:
                    after, flux_next = here, jnp.zeros_like(here)
                s_ref[at, :] = here + (flux - flux_next) + f_ref[at, :]
                here, flux = after, flux_next
        return carry

    lax.fori_loop(0, STEPS - 1, one, 0)
    now = s0_s[...]
    flux = rates * (pltpu.roll(now, 1, 0) - now)
    now = now + flux - pltpu.roll(flux, size - 1, 0)
    br_ref[...] = now[8 : 8 + rows]
    gain = RELAX * DRIVE
    for m in range(rows):
        at = pl.ds((m + STEPS - 1) * scen, scen)
        gv_ref[pl.ds(m, scen, stride=rows), :] = gain * sv_s[at, :]
        gt_ref[pl.ds(m, scen, stride=rows), :] = gain * st_s[at, :]


def col_stress_kernel(scen, rows, fl_ref, cr_ref, mine_ref, *rest):
    *got_refs, source_ref, start_ref, gl_ref, bc_ref, out_s = rest
    cols = fl_ref.shape[1]
    parts = rows * scen // cols
    base = parts * BLOCK
    at, first, last = place("gy")
    kind = first.astype(jnp.int32) + 2 * last.astype(jnp.int32)
    own = strips(mine_ref, parts, cols)
    before, after = jnp.zeros_like(own), jnp.zeros_like(own)
    res_before = jnp.zeros((8, cols), F32)
    res_after = jnp.zeros((8, cols), F32)
    for k, ref in enumerate(got_refs):
        step = 1 << k
        rest_of = lax.rem(at, step)
        bit = lax.rem(lax.div(at, step), 2)
        block = strips(ref, parts, cols)
        from_right = jnp.logical_and(bit == 0, rest_of == step - 1)
        from_left = jnp.logical_and(bit == 1, rest_of == 0)
        after = jnp.where(from_right, block, after)
        before = jnp.where(from_left, block, before)
        res_after = jnp.where(from_right, ref[pl.ds(base, 8), :], res_after)
        res_before = jnp.where(from_left, ref[pl.ds(base + 8, 8), :], res_before)
    _, _, _, _, _, _, jl_last, jl_0 = meet(before, own)
    _, _, _, _, _, _, jr_last, jr_0 = meet(own, after)
    jr_last = jnp.where(last, 0.0, jr_last)
    jr_0 = jnp.where(last, 0.0, jr_0)
    lo = LAST_AT + 6
    zero = jnp.zeros_like(jl_0)
    strip = jnp.concatenate(
        [
            before[lo + 1 : lo + 6],
            before[lo : lo + 1] - jl_last,
            jl_last - jl_0,
            zero,
            jr_0 - after[2:3],
            after[3:9],
            zero,
            jl_0,
            -jr_last,
            jr_last - jr_0,
            zero,
            zero,
            zero,
            zero,
            zero,
        ],
        0,
    )
    source = source_ref[kind]
    out_s[...] = dot_nn(fl_ref[...], source[:cols]) + dot_tn(strip, source[cols:])
    for m in range(rows):
        gl_ref[pl.ds(m, scen, stride=rows), :] = out_s[pl.ds(m * scen, scen), :]
    start = start_ref[kind]
    edge = dot_tn(jnp.concatenate([res_before, res_after], 0), start[cols:])
    skip = 4 * scen
    bc_ref[...] = dot_nn(cr_ref[...], start[:cols]) + edge[skip : skip + rows]


def final_kernel(
    scen, rows, a_ref, b_ref, v_ref, t_ref, gv_ref, gt_ref, gl_ref, br_ref, bc_ref, up_ref, row_ref, col_ref
):
    cols = v_ref.shape[1]
    sums = a_ref[...] + b_ref[...]
    g0, g1, g2, g3 = (sums if k == 0 else pltpu.roll(sums, cols - k * scen, 1) for k in range(4))
    alpha = g0 / g1
    rz = alpha * alpha * g2 - g0
    grow = alpha * g2 / g1
    beta_alpha = rz / (alpha * alpha * (g3 - g2 * g2 / g1))
    c0 = alpha + beta_alpha * grow
    c1 = -alpha * beta_alpha
    lane = lax.broadcasted_iota(jnp.int32, (scen, cols), 1)
    sub = lax.broadcasted_iota(jnp.int32, (scen, cols), 0)

    def column(c):
        tall = jnp.concatenate([c] * (scen // 8), 0)
        return jnp.sum(jnp.where(lane == sub, tall, 0.0), 1, keepdims=True)

    c0, c1 = column(c0), column(c1)
    br, bc = br_ref[...], bc_ref[...]
    for s in range(scen):
        at = pl.ds(s * rows, rows)
        a = jnp.broadcast_to(c0[s : s + 1], (rows, cols))
        b = jnp.broadcast_to(c1[s : s + 1], (rows, cols))
        up_ref[s] = a * v_ref[at, :] + b * t_ref[at, :]
        row_ref[s] = br + a * gv_ref[at, :] + b * gt_ref[at, :]
        col_ref[s] = bc + b * gl_ref[at, :]


def swap(block, axis, step):
    count = lax.axis_size(axis)
    return lax.ppermute(block, axis, [(i, i ^ step) for i in range(count)])


def exchange(even_side, odd_side, axis):
    count = lax.axis_size(axis)

    def pairs(start):
        return [(i + a, i + 1 - a) for i in range(start, count - 1, 2) for a in (0, 1)]

    return lax.ppermute(even_side, axis, pairs(0)), lax.ppermute(odd_side, axis, pairs(1))


def call(kernel, out, scratch, cost, *args):
    return pl.pallas_call(
        kernel,
        out_shape=out,
        in_specs=[pl.BlockSpec(memory_space=pltpu.VMEM)] * len(args),
        out_specs=jax.tree.map(lambda _: pl.BlockSpec(memory_space=pltpu.VMEM), out),
        scratch_shapes=scratch,
        compiler_params=pltpu.CompilerParams(vmem_limit_bytes=24 * 2**20),
        cost_estimate=pl.CostEstimate(flops=cost, bytes_accessed=0, transcendentals=0),
    )(*args)


def on_device(
    load_current, row_conductance, col_conductance, via_conductance, pad_mask, via_mask, row_residual, col_residual
):
    scen, rows, cols = load_current.shape
    size = rows * scen

    def f32(*shape):
        return jax.ShapeDtypeStruct(shape, F32)

    def vmem(*shape):
        return pltpu.VMEM(shape, F32)

    pick = jnp.asarray(picker(cols))
    source, start = (jnp.asarray(m) for m in spread(cols))

    wide = HALO * scen + 2 * SLOT + 8
    lf, msg_a, msg_b = call(
        pack_kernel,
        (f32(size, cols), f32(wide, cols), f32(wide, cols)),
        [],
        10**5,
        load_current, row_conductance, via_conductance, via_mask, row_residual,
    )
    got_a, got_b = exchange(msg_a, msg_b, "gx")

    ext = rows + 2 * SLOT
    reach = (rows + 2 * (STEPS - 1)) * scen
    packed = size + cols * (-(-(4 * scen + rows) // cols))
    v, t, fv, ft, fl, msg = call(
        functools.partial(fields_kernel, scen),
        (
            f32(size, cols), f32(size, cols), f32(reach, cols), f32(reach, cols), f32(size, cols),
            f32(size // cols * BLOCK + 24, cols),
        ),
        [vmem(ext, cols), vmem(ext, cols), vmem(ext, cols), vmem(5, rows, cols), vmem(packed, cols)],
        10**7,
        lf, row_conductance, col_conductance, via_conductance, pad_mask, via_mask, col_residual, got_a, got_b, pick,
    )

    gv, gt, br = call(
        functools.partial(row_stress_kernel, scen, rows),
        (f32(size, cols), f32(size, cols), f32(rows, cols)),
        [vmem(reach, cols), vmem(reach, cols), vmem(rows + 16, cols)],
        10**7,
        fv, ft, row_residual, got_a, got_b,
    )

    first_msg, received = msg, []
    step, count = 1, lax.axis_size("gy")
    sums = msg[-8:]
    while step < count:
        got = swap(msg, "gy", step)
        received.append(got)
        merge = functools.partial(merge_kernel, scen, "gy", step)
        if 2 * step < count:
            msg, sums = call(merge, (f32(*msg.shape), f32(8, cols)), [], 10**5, msg, got)
        else:
            sums = call(merge, (f32(8, cols),), [], 10**5, msg, got)[0]
        step *= 2

    gl, bc = call(
        functools.partial(col_stress_kernel, scen, rows),
        (f32(size, cols), f32(rows, cols)),
        [vmem(size, cols)],
        10**7,
        fl, col_residual, first_msg, *received, source, start,
    )

    step = lax.axis_size("gx") // 2
    while step > 1:
        sums = sums + swap(sums, "gx", step)
        step //= 2
    other = swap(sums, "gx", 1)

    shape = f32(scen, rows, cols)
    return call(
        functools.partial(final_kernel, scen, rows),
        (shape, shape, shape),
        [],
        10**6,
        sums, other, v, t, gv, gt, gl, br, bc,
    )


def solution(mesh):
    field = P(None, ("grp", "gx"), "gy")
    grid = P(("grp", "gx"), "gy")
    return jax.shard_map(
        on_device,
        mesh=mesh,
        in_specs=(field,) + (grid,) * 7,
        out_specs=(field,) * 3,
        check_vma=False,
    )
```

time: 256 us -> 31.2 us (0.12)
  the two profiles are of different devices: /device:TPU:0 before, /device:TPU:31 now
where the time goes in v1:
time: 31.2 us; the launch traced here: 30.7 us
  starting transfers between devices  11.3 us (36%)
  waiting for transfers between devices  8.88 us (28%)
  Pallas kernels  5.95 us (19%)
  local copies, waits for them, and re-layouts  3.79 us (12%)
  between operations  0.73 us (2%)
    ppermute x4, starting transfers between devices, swap(): return lax.ppermute(block, axis, [(i, i ^ step) for i in range(count)])  9.93 us
    ppermute x4, waiting for transfers between devices, swap(): return lax.ppermute(block, axis, [(i, i ^ step) for i in range(count)])  8.6 us
    pallas_call x7, Pallas kernels, call(): pl.pallas_call(kernel, out_shape=out, in_specs=[pl.BlockSpec(memory_space...  5.95 us
    unnamed x22, local copies, waits for them, and re-layouts  3.79 us
    ppermute x1, starting transfers between devices, exchange(): lax.ppermute(even_side, axis, pairs(0))  0.74 us
    ppermute x1, starting transfers between devices, exchange(): lax.ppermute(odd_side, axis, pairs(1))  0.65 us
  transfers between devices with their start and end apart: 6, of which 4 were waited for; matrix products, arithmetic and copies ran while one was open for 0% of the time, Pallas kernels for 8%

profile of v1, /device:TPU:31, one launch (start us, length us, event | category | flops | bytes accessed | tf_op | source)
XLA Modules:
  0.0 30.7 jit_solution(13963300170989972616)
XLA Ops:
  0.6 0.0 copy-start.2
  0.6 0.9 %copy-done.2 = bf16[16,32,128]{2,1,0:T(8,128)(2,1)S(1)} copy-done((bf16[16,32,128]{2,1,0:T(8,128)(2,1)S(1)}, bf16[16,32,128]{2,1,0:T(8,128)(2,1)}, u32[]{:S(2)}) %copy-start.2) | copy-done | bytes 131096
  1.5 0.0 copy-start.4
  1.5 0.7 %copy-done.4 = f32[32,128]{1,0:T(8,128)S(1)} copy-done((f32[32,128]{1,0:T(8,128)S(1)}, f32[32,128]{1,0:T(8,128)}, u32[]{:S(2)}) %copy-start.4) | copy-done | bytes 16408
  2.3 0.0 copy-start.5
  2.3 0.7 %copy-done.5 = f32[32,128]{1,0:T(8,128)S(1)} copy-done((f32[32,128]{1,0:T(8,128)S(1)}, f32[32,128]{1,0:T(8,128)}, u32[]{:S(2)}) %copy-start.5) | copy-done | bytes 16408
  3.0 0.0 copy-start.6
  3.0 0.7 %copy-done.6 = s32[32,128]{1,0:T(8,128)S(1)} copy-done((s32[32,128]{1,0:T(8,128)S(1)}, s32[32,128]{1,0:T(8,128)}, u32[]{:S(2)}) %copy-start.6) | copy-done | bytes 16408
  3.7 0.0 copy-start.7
  3.7 0.7 %copy-done.7 = f32[32,128]{1,0:T(8,128)S(1)} copy-done((f32[32,128]{1,0:T(8,128)S(1)}, f32[32,128]{1,0:T(8,128)}, u32[]{:S(2)}) %copy-start.7) | copy-done | bytes 16408
  4.4 0.0 copy-start.3
  4.4 0.0 copy-start.8
  4.4 0.0 copy-start.9
  4.4 0.0 copy-start.10
  4.4 0.1 shard_map.130
  4.6 0.7 %collective-permute-start = (f32[184,128]{1,0:T(8,128)S(1)}, f32[184,128]{1,0:T(8,128)S(1)}, u32[]{:S(2)}, u32[]{:S(2)}) collective-permute-start(f32[184,128]{1,0:T(8,128)S(1)} %get-tuple-element.19), channel_id=1, source_target_pairs={{0,4},{4,0},{8,12},{12,8},{1,5},{5,1},{9,13},{13,9},{2,6},{6,2},{1... | collective-permute-start | bytes 282632 | tf_op jit(solution)/shard_map/ppermute | solution.py:453
  5.3 0.7 %collective-permute-start.1 = (f32[184,128]{1,0:T(8,128)S(1)}, f32[184,128]{1,0:T(8,128)S(1)}, u32[]{:S(2)}, u32[]{:S(2)}) collective-permute-start(f32[184,128]{1,0:T(8,128)S(1)} %get-tuple-element.20), channel_id=1, source_target_pairs={{4,8},{8,4},{5,9},{9,5},{6,10},{10,6},{7,11},{11,7},{20,24},{24,20... | collective-permute-start | bytes 282632 | tf_op jit(solution)/shard_map/ppermute | solution.py:453
  6.0 0.3 collective-permute-done.a_ref
  6.2 0.0 collective-permute-done.1.b_ref
  6.2 0.0 copy-done.3
  6.2 0.0 copy-done.8
  6.2 0.0 copy-done.9
  6.3 0.0 copy-done.10
  6.3 1.3 %shard_map.131 = (f32[512,128]{1,0:T(8,128)S(1)}, f32[512,128]{1,0:T(8,128)S(1)}, f32[736,128]{1,0:T(8,128)S(1)}, f32[736,128]{1,0:T(8,128)S(1)}, f32[512,128]{1,0:T(8,128)S(1)}, /*index=5*/f32[120,128]{1,0:T(8,128)S(1)}) custom-call(f32[512,128]{1,0:T(8,128)S(1)} %get-tuple-element.18.lf_ref, f32[32,128]{1,0:T(8,128)S(1)} %copy-done.4, ...), custom_call_target="tpu_custom_call" | custom-call | flops 10000000 | tf_op jit(solution)/shard_map/pallas_call | solution.py:457
  7.6 0.2 collective-permute-start.2
  7.8 3.0 %collective-permute-done.2.got_ref.rest_0_ = f32[120,128]{1,0:T(8,128)S(1)} collective-permute-done((f32[120,128]{1,0:T(8,128)S(1)}, f32[120,128]{1,0:T(8,128)S(1)}, u32[]{:S(2)}, u32[]{:S(2)}) %collective-permute-start.2) | collective-permute-done | bytes 61472 | tf_op jit(solution)/shard_map/ppermute | solution.py:444
  10.8 0.8 %shard_map.132 = (f32[120,128]{1,0:T(8,128)S(1)}, f32[8,128]{1,0:T(8,128)}) custom-call(f32[120,128]{1,0:T(8,128)S(1)} %get-tuple-element.21.mine_ref, f32[120,128]{1,0:T(8,128)S(1)} %collective-permute-done.2.got_ref.rest_0_), custom_call_target="tpu_custom_call" | custom-call | flops 100000 | tf_op jit(solution)/shard_map/pallas_call | solution.py:457
  11.6 0.1 collective-permute-start.3
  11.7 4.6 %collective-permute-done.3.got_ref.rest_1_ = f32[120,128]{1,0:T(8,128)S(1)} collective-permute-done((f32[120,128]{1,0:T(8,128)S(1)}, f32[120,128]{1,0:T(8,128)S(1)}, u32[]{:S(2)}, u32[]{:S(2)}) %collective-permute-start.3) | collective-permute-done | bytes 61472 | tf_op jit(solution)/shard_map/ppermute | solution.py:444
  16.3 0.2 shard_map.133
  16.5 5.4 %collective-permute-start.4 = (f32[8,128]{1,0:T(8,128)S(1)}, f32[8,128]{1,0:T(8,128)S(1)}, u32[]{:S(2)}, u32[]{:S(2)}) collective-permute-start(f32[8,128]{1,0:T(8,128)S(1)} %shard_map.133), channel_id=1, source_target_pairs={{0,8},{4,12},{8,0},{12,4},{1,9},{5,13},{9,1},{13,5},{2,10},{6,14},... | collective-permute-start | bytes 12296 | tf_op jit(solution)/shard_map/ppermute | solution.py:444
  21.9 1.0 %collective-permute-done.4 = f32[8,128]{1,0:T(8,128)S(1)} collective-permute-done((f32[8,128]{1,0:T(8,128)S(1)}, f32[8,128]{1,0:T(8,128)S(1)}, u32[]{:S(2)}, u32[]{:S(2)}) %collective-permute-start.4) | collective-permute-done | bytes 4128 | tf_op jit(solution)/shard_map/ppermute | solution.py:444
  22.9 4.2 %collective-permute-start.5 = (f32[8,128]{1,0:T(8,128)S(1)}, f32[8,128]{1,0:T(8,128)S(1)}, u32[]{:S(2)}, u32[]{:S(2)}) collective-permute-start(f32[8,128]{1,0:T(8,128)S(1)} %add.3.a_ref), channel_id=1, source_target_pairs={{0,4},{4,0},{8,12},{12,8},{1,5},{5,1},{9,13},{13,9},{2,6},{6,2},{1... | collective-permute-start | bytes 12296 | tf_op jit(solution)/shard_map/ppermute | solution.py:444
  27.2 0.0 copy-start
  27.2 0.0 copy-start.1
  27.2 1.5 %shard_map.134 = (f32[512,128]{1,0:T(8,128)S(1)}, f32[512,128]{1,0:T(8,128)S(1)}, f32[32,128]{1,0:T(8,128)S(1)}) custom-call(f32[736,128]{1,0:T(8,128)S(1)} %get-tuple-element.25.fv_ref, f32[736,128]{1,0:T(8,128)S(1)} %get-tuple-element.26.ft_ref, f32[32,128]{1,0:T(8,128)S(1)} %copy-done.7, f32[184,128]{1,0:T(8,128)S(1)} %collective-permute-done.a_ref, ...), custom_call_target="tpu_custom_call" | custom-call | flops 10000000 | tf_op jit(solution)/shard_map/pallas_call | solution.py:457
  28.6 0.0 copy-done
  28.7 0.0 copy-done.1
  28.7 0.9 %shard_map.135 = (f32[512,128]{1,0:T(8,128)S(1)}, f32[32,128]{1,0:T(8,128)S(1)}) custom-call(f32[512,128]{1,0:T(8,128)S(1)} %get-tuple-element.29.fl_ref, f32[32,128]{1,0:T(8,128)S(1)} %copy-done.3, f32[120,128]{1,0:T(8,128)S(1)} %get-tuple-element.21.mine_ref, f32[120,128]{1,0:T(8,128)S(1)} %collective-permute-done.2.got_ref.rest_0_, ...), custom_call_target="tpu_custom_call" | custom-call | flops 10000000 | tf_op jit(solution)/shard_map/pallas_call | solution.py:457
  29.6 0.0 collective-permute-done.5.b_ref
  29.6 1.1 %shard_map.136 = (f32[16,32,128]{2,1,0:T(8,128)}, f32[16,32,128]{2,1,0:T(8,128)}, f32[16,32,128]{2,1,0:T(8,128)}) custom-call(f32[8,128]{1,0:T(8,128)S(1)} %add.3.a_ref, f32[8,128]{1,0:T(8,128)S(1)} %collective-permute-done.5.b_ref, f32[512,128]{1,0:T(8,128)S(1)} %get-tuple-element.23.v_ref, f32[512,128]{1,0:T(8,128)S(1)} %get-tuple-element.24.t_ref, ...), custom_call_target="tpu_custom_call" | custom-call | flops 1000000 | tf_op jit(solution)/shard_map/pallas_call | solution.py:457
  (1 shorter events, 0.0 us)
Async XLA Ops:
  0.6 0.9 %copy-start.2 = (bf16[16,32,128]{2,1,0:T(8,128)(2,1)S(1)}, bf16[16,32,128]{2,1,0:T(8,128)(2,1)}, u32[]{:S(2)}) copy-start(bf16[16,32,128]{2,1,0:T(8,128)(2,1)} %load_ref.1) | copy-start | bytes 393220
  1.5 0.7 %copy-start.4 = (f32[32,128]{1,0:T(8,128)S(1)}, f32[32,128]{1,0:T(8,128)}, u32[]{:S(2)}) copy-start(f32[32,128]{1,0:T(8,128)} %rc_ref.3) | copy-start | bytes 49156
  2.3 0.7 %copy-start.5 = (f32[32,128]{1,0:T(8,128)S(1)}, f32[32,128]{1,0:T(8,128)}, u32[]{:S(2)}) copy-start(f32[32,128]{1,0:T(8,128)} %vc_ref.3) | copy-start | bytes 49156
  3.0 0.7 %copy-start.6 = (s32[32,128]{1,0:T(8,128)S(1)}, s32[32,128]{1,0:T(8,128)}, u32[]{:S(2)}) copy-start(s32[32,128]{1,0:T(8,128)} %vm_ref.3) | copy-start | bytes 49156
  3.7 0.7 %copy-start.7 = (f32[32,128]{1,0:T(8,128)S(1)}, f32[32,128]{1,0:T(8,128)}, u32[]{:S(2)}) copy-start(f32[32,128]{1,0:T(8,128)} %rr_ref.3) | copy-start | bytes 49156
  4.4 1.8 %copy-start.3 = (f32[32,128]{1,0:T(8,128)S(1)}, f32[32,128]{1,0:T(8,128)}, u32[]{:S(2)}) copy-start(f32[32,128]{1,0:T(8,128)} %cr_ref.3) | copy-start | bytes 49156
  4.4 1.8 %copy-start.8 = (f32[48,128]{1,0:T(8,128)S(1)}, f32[48,128]{1,0:T(8,128)}, u32[]{:S(2)}) copy-start(f32[48,128]{1,0:T(8,128)} %constant.6.clone.pick_ref) | copy-start | bytes 73732
  4.4 1.8 %copy-start.9 = (f32[32,128]{1,0:T(8,128)S(1)}, f32[32,128]{1,0:T(8,128)}, u32[]{:S(2)}) copy-start(f32[32,128]{1,0:T(8,128)} %cc_ref.1) | copy-start | bytes 49156
  4.4 1.8 %copy-start.10 = (s32[32,128]{1,0:T(8,128)S(1)}, s32[32,128]{1,0:T(8,128)}, u32[]{:S(2)}) copy-start(s32[32,128]{1,0:T(8,128)} %pm_ref.1) | copy-start | bytes 49156
  4.6 1.7 %collective-permute-start = (f32[184,128]{1,0:T(8,128)S(1)}, f32[184,128]{1,0:T(8,128)S(1)}, u32[]{:S(2)}, u32[]{:S(2)}) collective-permute-start(f32[184,128]{1,0:T(8,128)S(1)} %get-tuple-element.19), channel_id=1, source_target_pairs={{0,4},{4,0},{8,12},{12,8},{1,5},{5,1},{9,13},{13,9},{2,6},{6,2},{1... | collective-permute-start | bytes 282632 | tf_op jit(solution)/shard_map/ppermute | solution.py:453
  5.3 0.9 %collective-permute-start.1 = (f32[184,128]{1,0:T(8,128)S(1)}, f32[184,128]{1,0:T(8,128)S(1)}, u32[]{:S(2)}, u32[]{:S(2)}) collective-permute-start(f32[184,128]{1,0:T(8,128)S(1)} %get-tuple-element.20), channel_id=1, source_target_pairs={{4,8},{8,4},{5,9},{9,5},{6,10},{10,6},{7,11},{11,7},{20,24},{24,20... | collective-permute-start | bytes 282632 | tf_op jit(solution)/shard_map/ppermute | solution.py:453
  7.6 3.2 %collective-permute-start.2 = (f32[120,128]{1,0:T(8,128)S(1)}, f32[120,128]{1,0:T(8,128)S(1)}, u32[]{:S(2)}, u32[]{:S(2)}) collective-permute-start(f32[120,128]{1,0:T(8,128)S(1)} %get-tuple-element.21.mine_ref), channel_id=1, source_target_pairs={{0,1},{1,0},{2,3},{3,2},{4,5},{5,4},{6,7},{7,6},{8,9},{9,8},{10,11... | collective-permute-start | bytes 184328 | tf_op jit(solution)/shard_map/ppermute | solution.py:444
  11.6 4.6 %collective-permute-start.3 = (f32[120,128]{1,0:T(8,128)S(1)}, f32[120,128]{1,0:T(8,128)S(1)}, u32[]{:S(2)}, u32[]{:S(2)}) collective-permute-start(f32[120,128]{1,0:T(8,128)S(1)} %get-tuple-element.22.mine_ref), channel_id=1, source_target_pairs={{0,2},{1,3},{2,0},{3,1},{4,6},{5,7},{6,4},{7,5},{8,10},{9,11},{10,... | collective-permute-start | bytes 184328 | tf_op jit(solution)/shard_map/ppermute | solution.py:444
  16.5 6.4 %collective-permute-start.4 = (f32[8,128]{1,0:T(8,128)S(1)}, f32[8,128]{1,0:T(8,128)S(1)}, u32[]{:S(2)}, u32[]{:S(2)}) collective-permute-start(f32[8,128]{1,0:T(8,128)S(1)} %shard_map.133), channel_id=1, source_target_pairs={{0,8},{4,12},{8,0},{12,4},{1,9},{5,13},{9,1},{13,5},{2,10},{6,14},... | collective-permute-start | bytes 12296 | tf_op jit(solution)/shard_map/ppermute | solution.py:444
  22.9 6.6 %collective-permute-start.5 = (f32[8,128]{1,0:T(8,128)S(1)}, f32[8,128]{1,0:T(8,128)S(1)}, u32[]{:S(2)}, u32[]{:S(2)}) collective-permute-start(f32[8,128]{1,0:T(8,128)S(1)} %add.3.a_ref), channel_id=1, source_target_pairs={{0,4},{4,0},{8,12},{12,8},{1,5},{5,1},{9,13},{13,9},{2,6},{6,2},{1... | collective-permute-start | bytes 12296 | tf_op jit(solution)/shard_map/ppermute | solution.py:444
  27.2 1.5 %copy-start = (f32[4,152,128]{2,1,0:T(8,128)S(1)}, f32[4,152,128]{2,1,0:T(8,128)}, u32[]{:S(2)}) copy-start(f32[4,152,128]{2,1,0:T(8,128)} %constant.7.clone.rest_2_) | copy-start | bytes 933892
  27.2 1.5 %copy-start.1 = (f32[4,144,128]{2,1,0:T(8,128)S(1)}, f32[4,144,128]{2,1,0:T(8,128)}, u32[]{:S(2)}) copy-start(f32[4,144,128]{2,1,0:T(8,128)} %constant.8.clone.rest_3_) | copy-start | bytes 884740

commit v2 on v1

--- a/solution.py
+++ b/solution.py
@@ -94,15 +94,24 @@
     return at, at == 0, at == count - 1
 
 
-def pack_kernel(load_ref, rc_ref, vc_ref, vm_ref, rr_ref, lf_ref, a_ref, b_ref):
+def pack_kernel(*refs):
+    args, (lf_ref, h_ref, via_ref, a_ref, b_ref), held, sem = refs[:5], refs[5:10], refs[10:15], refs[15]
+    copies = [pltpu.make_async_copy(src, dst, sem.at[i]) for i, (src, dst) in enumerate(zip(args, held))]
+    for copy in copies:
+        copy.start()
+    load_ref, rc_ref, vc_ref, vm_ref, rr_ref = held
     scen, rows, cols = load_ref.shape
     at, first, _ = place("gx")
     even = lax.rem(at, 2) == 0
+    for copy in copies:
+        copy.wait()
     for s in range(scen):
         lf_ref[pl.ds(s, rows, stride=scen), :] = load_ref[s].astype(F32)
     row = lax.broadcasted_iota(jnp.int32, (rows, cols), 0)
     h = jnp.where(jnp.logical_and(first, row == 0), 0.0, rc_ref[...])
     via = vm_ref[...].astype(F32) * vc_ref[...]
+    h_ref[...] = h
+    via_ref[...] = via
     n = HALO * scen
 
     def put(where, top, bottom):
@@ -116,12 +125,12 @@
 
 
 def fields_kernel(
-    scen, lf_ref, rc_ref, cc_ref, vc_ref, pm_ref, vm_ref, cr_ref, a_ref, b_ref, pick_ref,
+    scen, lf_ref, h_ref, via_ref, cc_ref, pm_ref, cr_ref, a_ref, b_ref, pick_ref,
     v_ref, t_ref, fv_ref, ft_ref, fl_ref, msg_ref,
     inv_s, h_s, tie_s, low_s, w_s,
 ):
-    rows, cols = rc_ref.shape
-    at_x, first_x, _ = place("gx")
+    rows, cols = h_ref.shape
+    at_x = lax.axis_index("gx")
     odd = lax.rem(at_x, 2) == 1
     _, first_y, last_y = place("gy")
     n = HALO * scen
@@ -132,10 +141,8 @@
     def after(where):
         return jnp.where(odd, b_ref[where, :], a_ref[where, :])
 
-    row = lax.broadcasted_iota(jnp.int32, (rows, cols), 0)
     lane = lax.broadcasted_iota(jnp.int32, (rows, cols), 1)
-    h = jnp.where(jnp.logical_and(first_x, row == 0), 0.0, rc_ref[...])
-    via = vm_ref[...].astype(F32) * vc_ref[...]
+    h, via = h_ref[...], via_ref[...]
     at = pl.ds(n, SLOT)
     h_ext = jnp.concatenate([before(at), h, after(at)], 0)
     at = pl.ds(n + SLOT, SLOT)
@@ -453,11 +460,11 @@
     return lax.ppermute(even_side, axis, pairs(0)), lax.ppermute(odd_side, axis, pairs(1))
 
 
-def call(kernel, out, scratch, cost, *args):
+def call(kernel, out, scratch, cost, *args, space=pltpu.VMEM):
     return pl.pallas_call(
         kernel,
         out_shape=out,
-        in_specs=[pl.BlockSpec(memory_space=pltpu.VMEM)] * len(args),
+        in_specs=[pl.BlockSpec(memory_space=space)] * len(args),
         out_specs=jax.tree.map(lambda _: pl.BlockSpec(memory_space=pltpu.VMEM), out),
         scratch_shapes=scratch,
         compiler_params=pltpu.CompilerParams(vmem_limit_bytes=24 * 2**20),
@@ -481,12 +488,14 @@
     source, start = (jnp.asarray(m) for m in spread(cols))
 
     wide = HALO * scen + 2 * SLOT + 8
-    lf, msg_a, msg_b = call(
+    sources = (load_current, row_conductance, via_conductance, via_mask, row_residual)
+    lf, h, via, msg_a, msg_b = call(
         pack_kernel,
-        (f32(size, cols), f32(wide, cols), f32(wide, cols)),
-        [],
+        (f32(size, cols), f32(rows, cols), f32(rows, cols), f32(wide, cols), f32(wide, cols)),
+        [pltpu.VMEM(x.shape, x.dtype) for x in sources] + [pltpu.SemaphoreType.DMA((len(sources),))],
         10**5,
-        load_current, row_conductance, via_conductance, via_mask, row_residual,
+        *(pltpu.with_memory_space_constraint(x, pltpu.HBM) for x in sources),
+        space=pltpu.HBM,
     )
     got_a, got_b = exchange(msg_a, msg_b, "gx")
 
@@ -501,7 +510,7 @@
         ),
         [vmem(ext, cols), vmem(ext, cols), vmem(ext, cols), vmem(5, rows, cols), vmem(packed, cols)],
         10**7,
-        lf, row_conductance, col_conductance, via_conductance, pad_mask, via_mask, col_residual, got_a, got_b, pick,
+        lf, h, via, col_conductance, pad_mask, col_residual, got_a, got_b, pick,
     )
 
     gv, gt, br = call(
@@ -518,6 +527,8 @@
     while step < count:
         got = swap(msg, "gy", step)
         received.append(got)
+        if step == 1:
+            got, br = lax.optimization_barrier((got, br))
         merge = functools.partial(merge_kernel, scen, "gy", step)
         if 2 * step < count:
             msg, sums = call(merge, (f32(*msg.shape), f32(8, cols)), [], 10**5, msg, got)
@@ -535,7 +546,10 @@
 
     step = lax.axis_size("gx") // 2
     while step > 1:
-        sums = sums + swap(sums, "gx", step)
+        got = swap(sums, "gx", step)
+        if 2 * step == lax.axis_size("gx"):
+            got, bc = lax.optimization_barrier((got, bc))
+        sums = sums + got
         step //= 2
     other = swap(sums, "gx", 1)
 

time: 31.2 us -> 26.7 us (0.86)
  the two profiles are of different devices: /device:TPU:31 before, /device:TPU:0 now
where the time goes in v2:
time: 26.7 us; the launch traced here: 26.5 us
  starting transfers between devices  13.8 us (52%)
  Pallas kernels  6.98 us (26%)
  waiting for transfers between devices  4.97 us (19%)
  between operations  0.73 us (3%)
    ppermute x4, starting transfers between devices, swap(): return lax.ppermute(block, axis, [(i, i ^ step) for i in range(count)])  12.6 us
    pallas_call x7, Pallas kernels, call(): pl.pallas_call(kernel, out_shape=out, in_specs=[pl.BlockSpec(memory_space...  6.98 us
    ppermute x4, waiting for transfers between devices, swap(): return lax.ppermute(block, axis, [(i, i ^ step) for i in range(count)])  4.69 us
    ppermute x1, starting transfers between devices, exchange(): lax.ppermute(odd_side, axis, pairs(1))  0.65 us
  transfers between devices with their start and end apart: 6, of which 5 were waited for; matrix products, arithmetic and copies ran while one was open for 0% of the time, Pallas kernels for 9%

profile of v2, /device:TPU:0, one launch (start us, length us, event | category | flops | bytes accessed | tf_op | source)
XLA Modules:
  0.0 26.5 jit_solution(15461724522088147648)
XLA Ops:
  0.6 0.0 copy-start.2
  0.6 0.0 copy-start.4
  0.7 0.0 copy-start.5
  0.7 0.0 copy-start.6
  0.7 1.1 %shard_map.130 = (f32[512,128]{1,0:T(8,128)S(1)}, f32[32,128]{1,0:T(8,128)S(1)}, f32[32,128]{1,0:T(8,128)S(1)}, f32[184,128]{1,0:T(8,128)S(1)}, f32[184,128]{1,0:T(8,128)S(1)}) custom-call(bf16[16,32,128]{2,1,0:T(8,128)(2,1)} %refs_0_.1, f32[32,128]{1,0:T(8,128)} %refs_1_.1, f32[32,128]{1,0:T(8,128)} %refs_2_.1, s32[32,128]{1,0:T(8,128)} %refs_3_.1, ...), custom_call_target="tpu_custom_call" | custom-call | flops 100000 | tf_op jit(solution)/shard_map/pallas_call | solution.py:464
  1.8 0.5 %collective-permute-start = (f32[184,128]{1,0:T(8,128)S(1)}, f32[184,128]{1,0:T(8,128)S(1)}, u32[]{:S(2)}, u32[]{:S(2)}) collective-permute-start(f32[184,128]{1,0:T(8,128)S(1)} %get-tuple-element.27), channel_id=1, source_target_pairs={{0,4},{4,0},{8,12},{12,8},{1,5},{5,1},{9,13},{13,9},{2,6},{6,2},{1... | collective-permute-start | bytes 282632 | tf_op jit(solution)/shard_map/ppermute | solution.py:460
  2.3 0.7 %collective-permute-start.1 = (f32[184,128]{1,0:T(8,128)S(1)}, f32[184,128]{1,0:T(8,128)S(1)}, u32[]{:S(2)}, u32[]{:S(2)}) collective-permute-start(f32[184,128]{1,0:T(8,128)S(1)} %get-tuple-element.28), channel_id=1, source_target_pairs={{4,8},{8,4},{5,9},{9,5},{6,10},{10,6},{7,11},{11,7},{20,24},{24,20... | collective-permute-start | bytes 282632 | tf_op jit(solution)/shard_map/ppermute | solution.py:460
  3.0 0.3 %collective-permute-done.a_ref = f32[184,128]{1,0:T(8,128)S(1)} collective-permute-done((f32[184,128]{1,0:T(8,128)S(1)}, f32[184,128]{1,0:T(8,128)S(1)}, u32[]{:S(2)}, u32[]{:S(2)}) %collective-permute-start) | collective-permute-done | bytes 94240 | tf_op jit(solution)/shard_map/ppermute | solution.py:460
  3.2 0.0 collective-permute-done.1.b_ref
  3.2 0.0 copy-done.2
  3.2 0.0 copy-done.4
  3.2 0.0 copy-done.5
  3.3 0.0 copy-done.6
  3.3 0.0 copy-start.3
  3.3 1.3 %shard_map.131 = (f32[512,128]{1,0:T(8,128)S(1)}, f32[512,128]{1,0:T(8,128)S(1)}, f32[736,128]{1,0:T(8,128)S(1)}, f32[736,128]{1,0:T(8,128)S(1)}, f32[512,128]{1,0:T(8,128)S(1)}, /*index=5*/f32[120,128]{1,0:T(8,128)S(1)}) custom-call(f32[512,128]{1,0:T(8,128)S(1)} %get-tuple-element.24.lf_ref, f32[32,128]{1,0:T(8,128)S(1)} %get-tuple-element.25.h_ref, ...), custom_call_target="tpu_custom_call" | custom-call | flops 10000000 | tf_op jit(solution)/shard_map/pallas_call | solution.py:464
  4.6 3.0 %collective-permute-start.2 = (f32[120,128]{1,0:T(8,128)S(1)}, f32[120,128]{1,0:T(8,128)S(1)}, u32[]{:S(2)}, u32[]{:S(2)}) collective-permute-start(f32[120,128]{1,0:T(8,128)S(1)} %get-tuple-element.29.mine_ref), channel_id=1, source_target_pairs={{0,1},{1,0},{2,3},{3,2},{4,5},{5,4},{6,7},{7,6},{8,9},{9,8},{10,11... | collective-permute-start | bytes 184328 | tf_op jit(solution)/shard_map/ppermute | solution.py:451
  7.6 0.0 copy-done.3
  7.6 0.0 copy-start
  7.6 0.0 copy-start.1
  7.6 1.5 %shard_map.132 = (f32[512,128]{1,0:T(8,128)S(1)}, f32[512,128]{1,0:T(8,128)S(1)}, f32[32,128]{1,0:T(8,128)S(1)}) custom-call(f32[736,128]{1,0:T(8,128)S(1)} %get-tuple-element.30.fv_ref, f32[736,128]{1,0:T(8,128)S(1)} %get-tuple-element.31.ft_ref, f32[32,128]{1,0:T(8,128)S(1)} %copy-done.3, f32[184,128]{1,0:T(8,128)S(1)} %collective-permute-done.a_ref, ...), custom_call_target="tpu_custom_call" | custom-call | flops 10000000 | tf_op jit(solution)/shard_map/pallas_call | solution.py:464
  9.1 0.7 %collective-permute-done.2.got_ref.rest_0_ = f32[120,128]{1,0:T(8,128)S(1)} collective-permute-done((f32[120,128]{1,0:T(8,128)S(1)}, f32[120,128]{1,0:T(8,128)S(1)}, u32[]{:S(2)}, u32[]{:S(2)}) %collective-permute-start.2) | collective-permute-done | bytes 61472 | tf_op jit(solution)/shard_map/ppermute | solution.py:451
  9.8 0.8 %shard_map.133 = (f32[120,128]{1,0:T(8,128)S(1)}, f32[8,128]{1,0:T(8,128)}) custom-call(f32[120,128]{1,0:T(8,128)S(1)} %get-tuple-element.29.mine_ref, f32[120,128]{1,0:T(8,128)S(1)} %collective-permute-done.2.got_ref.rest_0_), custom_call_target="tpu_custom_call" | custom-call | flops 100000 | tf_op jit(solution)/shard_map/pallas_call | solution.py:464
  10.6 3.0 %collective-permute-start.3 = (f32[120,128]{1,0:T(8,128)S(1)}, f32[120,128]{1,0:T(8,128)S(1)}, u32[]{:S(2)}, u32[]{:S(2)}) collective-permute-start(f32[120,128]{1,0:T(8,128)S(1)} %get-tuple-element.34.mine_ref), channel_id=1, source_target_pairs={{0,2},{1,3},{2,0},{3,1},{4,6},{5,7},{6,4},{7,5},{8,10},{9,11},{10,... | collective-permute-start | bytes 184328 | tf_op jit(solution)/shard_map/ppermute | solution.py:451
  13.6 2.2 %collective-permute-done.3.got_ref.rest_1_ = f32[120,128]{1,0:T(8,128)S(1)} collective-permute-done((f32[120,128]{1,0:T(8,128)S(1)}, f32[120,128]{1,0:T(8,128)S(1)}, u32[]{:S(2)}, u32[]{:S(2)}) %collective-permute-start.3) | collective-permute-done | bytes 61472 | tf_op jit(solution)/shard_map/ppermute | solution.py:451
  15.8 0.2 shard_map.134
  16.1 6.6 %collective-permute-start.4 = (f32[8,128]{1,0:T(8,128)S(1)}, f32[8,128]{1,0:T(8,128)S(1)}, u32[]{:S(2)}, u32[]{:S(2)}) collective-permute-start(f32[8,128]{1,0:T(8,128)S(1)} %shard_map.134), channel_id=1, source_target_pairs={{0,8},{4,12},{8,0},{12,4},{1,9},{5,13},{9,1},{13,5},{2,10},{6,14},... | collective-permute-start | bytes 12296 | tf_op jit(solution)/shard_map/ppermute | solution.py:451
  22.7 0.0 copy-done
  22.7 0.0 copy-done.1
  22.7 0.9 %shard_map.135 = (f32[512,128]{1,0:T(8,128)S(1)}, f32[32,128]{1,0:T(8,128)S(1)}) custom-call(f32[512,128]{1,0:T(8,128)S(1)} %get-tuple-element.35.fl_ref, f32[32,128]{1,0:T(8,128)S(1)} %copy-done.2, f32[120,128]{1,0:T(8,128)S(1)} %get-tuple-element.29.mine_ref, f32[120,128]{1,0:T(8,128)S(1)} %collective-permute-done.2.got_ref.rest_0_, ...), custom_call_target="tpu_custom_call" | custom-call | flops 10000000 | tf_op jit(solution)/shard_map/pallas_call | solution.py:464
  23.6 0.7 %collective-permute-done.4 = f32[8,128]{1,0:T(8,128)S(1)} collective-permute-done((f32[8,128]{1,0:T(8,128)S(1)}, f32[8,128]{1,0:T(8,128)S(1)}, u32[]{:S(2)}, u32[]{:S(2)}) %collective-permute-start.4) | collective-permute-done | bytes 4128 | tf_op jit(solution)/shard_map/ppermute | solution.py:451
  24.2 0.0 collective-permute-start.5
  24.2 1.2 %collective-permute-done.5.b_ref = f32[8,128]{1,0:T(8,128)S(1)} collective-permute-done((f32[8,128]{1,0:T(8,128)S(1)}, f32[8,128]{1,0:T(8,128)S(1)}, u32[]{:S(2)}, u32[]{:S(2)}) %collective-permute-start.5) | collective-permute-done | bytes 4128 | tf_op jit(solution)/shard_map/ppermute | solution.py:451
  25.4 1.1 %shard_map.136 = (f32[16,32,128]{2,1,0:T(8,128)}, f32[16,32,128]{2,1,0:T(8,128)}, f32[16,32,128]{2,1,0:T(8,128)}) custom-call(f32[8,128]{1,0:T(8,128)S(1)} %add.3.a_ref, f32[8,128]{1,0:T(8,128)S(1)} %collective-permute-done.5.b_ref, f32[512,128]{1,0:T(8,128)S(1)} %get-tuple-element.38.v_ref, f32[512,128]{1,0:T(8,128)S(1)} %get-tuple-element.39.t_ref, ...), custom_call_target="tpu_custom_call" | custom-call | flops 1000000 | tf_op jit(solution)/shard_map/pallas_call | solution.py:464
  (1 shorter events, 0.0 us)
Async XLA Ops:
  0.6 2.6 %copy-start.2 = (f32[32,128]{1,0:T(8,128)S(1)}, f32[32,128]{1,0:T(8,128)}, u32[]{:S(2)}) copy-start(f32[32,128]{1,0:T(8,128)} %cr_ref.3) | copy-start | bytes 49156
  0.6 2.6 %copy-start.4 = (f32[48,128]{1,0:T(8,128)S(1)}, f32[48,128]{1,0:T(8,128)}, u32[]{:S(2)}) copy-start(f32[48,128]{1,0:T(8,128)} %constant.6.clone.pick_ref) | copy-start | bytes 73732
  0.7 2.6 %copy-start.5 = (f32[32,128]{1,0:T(8,128)S(1)}, f32[32,128]{1,0:T(8,128)}, u32[]{:S(2)}) copy-start(f32[32,128]{1,0:T(8,128)} %cc_ref.1) | copy-start | bytes 49156
  0.7 2.6 %copy-start.6 = (s32[32,128]{1,0:T(8,128)S(1)}, s32[32,128]{1,0:T(8,128)}, u32[]{:S(2)}) copy-start(s32[32,128]{1,0:T(8,128)} %pm_ref.1) | copy-start | bytes 49156
  1.8 1.5 %collective-permute-start = (f32[184,128]{1,0:T(8,128)S(1)}, f32[184,128]{1,0:T(8,128)S(1)}, u32[]{:S(2)}, u32[]{:S(2)}) collective-permute-start(f32[184,128]{1,0:T(8,128)S(1)} %get-tuple-element.27), channel_id=1, source_target_pairs={{0,4},{4,0},{8,12},{12,8},{1,5},{5,1},{9,13},{13,9},{2,6},{6,2},{1... | collective-permute-start | bytes 282632 | tf_op jit(solution)/shard_map/ppermute | solution.py:460
  2.3 0.9 %collective-permute-start.1 = (f32[184,128]{1,0:T(8,128)S(1)}, f32[184,128]{1,0:T(8,128)S(1)}, u32[]{:S(2)}, u32[]{:S(2)}) collective-permute-start(f32[184,128]{1,0:T(8,128)S(1)} %get-tuple-element.28), channel_id=1, source_target_pairs={{4,8},{8,4},{5,9},{9,5},{6,10},{10,6},{7,11},{11,7},{20,24},{24,20... | collective-permute-start | bytes 282632 | tf_op jit(solution)/shard_map/ppermute | solution.py:460
  3.3 4.3 %copy-start.3 = (f32[32,128]{1,0:T(8,128)S(1)}, f32[32,128]{1,0:T(8,128)}, u32[]{:S(2)}) copy-start(f32[32,128]{1,0:T(8,128)} %rr_ref.1) | copy-start | bytes 49156
  4.6 5.2 %collective-permute-start.2 = (f32[120,128]{1,0:T(8,128)S(1)}, f32[120,128]{1,0:T(8,128)S(1)}, u32[]{:S(2)}, u32[]{:S(2)}) collective-permute-start(f32[120,128]{1,0:T(8,128)S(1)} %get-tuple-element.29.mine_ref), channel_id=1, source_target_pairs={{0,1},{1,0},{2,3},{3,2},{4,5},{5,4},{6,7},{7,6},{8,9},{9,8},{10,11... | collective-permute-start | bytes 184328 | tf_op jit(solution)/shard_map/ppermute | solution.py:451
  7.6 15.1 %copy-start = (f32[4,152,128]{2,1,0:T(8,128)S(1)}, f32[4,152,128]{2,1,0:T(8,128)}, u32[]{:S(2)}) copy-start(f32[4,152,128]{2,1,0:T(8,128)} %constant.7.clone.rest_2_) | copy-start | bytes 933892
  7.6 15.1 %copy-start.1 = (f32[4,144,128]{2,1,0:T(8,128)S(1)}, f32[4,144,128]{2,1,0:T(8,128)}, u32[]{:S(2)}) copy-start(f32[4,144,128]{2,1,0:T(8,128)} %constant.8.clone.rest_3_) | copy-start | bytes 884740
  10.6 5.2 %collective-permute-start.3 = (f32[120,128]{1,0:T(8,128)S(1)}, f32[120,128]{1,0:T(8,128)S(1)}, u32[]{:S(2)}, u32[]{:S(2)}) collective-permute-start(f32[120,128]{1,0:T(8,128)S(1)} %get-tuple-element.34.mine_ref), channel_id=1, source_target_pairs={{0,2},{1,3},{2,0},{3,1},{4,6},{5,7},{6,4},{7,5},{8,10},{9,11},{10,... | collective-permute-start | bytes 184328 | tf_op jit(solution)/shard_map/ppermute | solution.py:451
  16.1 8.2 %collective-permute-start.4 = (f32[8,128]{1,0:T(8,128)S(1)}, f32[8,128]{1,0:T(8,128)S(1)}, u32[]{:S(2)}, u32[]{:S(2)}) collective-permute-start(f32[8,128]{1,0:T(8,128)S(1)} %shard_map.134), channel_id=1, source_target_pairs={{0,8},{4,12},{8,0},{12,4},{1,9},{5,13},{9,1},{13,5},{2,10},{6,14},... | collective-permute-start | bytes 12296 | tf_op jit(solution)/shard_map/ppermute | solution.py:451
  24.2 1.2 %collective-permute-start.5 = (f32[8,128]{1,0:T(8,128)S(1)}, f32[8,128]{1,0:T(8,128)S(1)}, u32[]{:S(2)}, u32[]{:S(2)}) collective-permute-start(f32[8,128]{1,0:T(8,128)S(1)} %add.3.a_ref), channel_id=1, source_target_pairs={{0,4},{4,0},{8,12},{12,8},{1,5},{5,1},{9,13},{13,9},{2,6},{6,2},{1... | collective-permute-start | bytes 12296 | tf_op jit(solution)/shard_map/ppermute | solution.py:451

commit v3 on v2

v3 whole, which is shorter than its diff:
```python
import functools

import jax
import jax.numpy as jnp
import numpy as np
from jax import lax
from jax.experimental import pallas as pl
from jax.experimental.pallas import tpu as pltpu
from jax.sharding import PartitionSpec as P

STEPS = 8
RELAX = 0.45
DRIVE = 4.0
PAD = 20.0
LEAK = 0.05

F32 = jnp.float32
HALO = STEPS + 1
SLOT = 16

SUM_LANES = [0, 12, -1, 13, 14, 9, 15, -2]
FIRST_LANES = [11, 1, 2, 3, 4, 5, 6]
LAST_LANES = [8, -7, -6, -5, -4, -3]
PICKED = 8 + 8 + 8


def dot_nt(a, b):
    return lax.dot_general(
        a, b, (((1,), (1,)), ((), ())), precision=lax.Precision.HIGHEST, preferred_element_type=F32
    )


def dot_nn(a, b):
    return lax.dot_general(
        a, b, (((1,), (0,)), ((), ())), precision=lax.Precision.HIGHEST, preferred_element_type=F32
    )


def dot_tn(a, b):
    return lax.dot_general(
        a, b, (((0,), (0,)), ((), ())), precision=lax.Precision.HIGHEST, preferred_element_type=F32
    )


def picker(cols):
    e = np.zeros((PICKED + 8 + 16, cols), np.float32)
    for base, lanes in ((0, SUM_LANES), (8, FIRST_LANES), (16, LAST_LANES)):
        for i, lane in enumerate(lanes):
            e[base + i, lane % cols] = 1
    e[PICKED : PICKED + 8] = 1
    for i in range(8):
        e[PICKED + 8 + i, i] = 1
        e[PICKED + 16 + i, cols - 8 + i] = 1
    return e


def spread(cols):
    size = cols + 16
    sources, starts = [], []
    for first, last in ((0, 0), (1, 0), (0, 1), (1, 1)):
        rate = np.full(size + 1, RELAX)
        rate[0] = rate[size] = 0
        if first:
            rate[8] = 0
        if last:
            rate[8 + cols] = 0
        step = np.eye(size)
        for i in range(size):
            step[i, i] -= rate[i] + rate[i + 1]
            if i:
                step[i, i - 1] += rate[i]
            if i + 1 < size:
                step[i, i + 1] += rate[i + 1]
        power, total = np.eye(size), np.zeros((size, size))
        for _ in range(STEPS):
            total += power
            power = step @ power
        source = (RELAX * DRIVE * total)[8 : 8 + cols].T
        start = power[8 : 8 + cols].T
        extra = np.zeros((24, cols))
        extra[0:7] = source[1:8]
        extra[8:15] = source[8 + cols : 15 + cols]
        extra[16] = source[8]
        extra[17] = source[8 + cols - 2]
        extra[18] = source[8 + cols - 1]
        sources.append(np.concatenate([source[8 : 8 + cols], extra]))
        starts.append(np.concatenate([start[8 : 8 + cols], start[:8], start[8 + cols :]]))
    return np.stack(sources).astype(np.float32), np.stack(starts).astype(np.float32)


def place(axis):
    at, count = lax.axis_index(axis), lax.axis_size(axis)
    return at, at == 0, at == count - 1


def pick_side(odd, even_ref, odd_ref):
    def before(*where):
        return jnp.where(odd, even_ref[where], odd_ref[where])

    def after(*where):
        return jnp.where(odd, odd_ref[where], even_ref[where])

    return before, after


def pack_kernel(*refs):
    args, outs, held, sem = refs[:5], refs[5:10], refs[10:15], refs[15]
    copies = [pltpu.make_async_copy(src, dst, sem.at[i]) for i, (src, dst) in enumerate(zip(args, held))]
    for copy in copies:
        copy.start()
    load_ref, rc_ref, vc_ref, vm_ref, rr_ref = held
    lf_ref, h_ref, via_ref, a_ref, b_ref = outs
    scen, rows, cols = load_ref.shape
    at, first, _ = place("gx")
    even = lax.rem(at, 2) == 0
    for copy in copies:
        copy.wait()
    for s in range(scen):
        lf_ref[pl.ds(s, rows, stride=scen), :] = load_ref[s].astype(F32)
    row = lax.broadcasted_iota(jnp.int32, (rows, cols), 0)
    h = jnp.where(jnp.logical_and(first, row == 0), 0.0, rc_ref[...])
    via = vm_ref[...].astype(F32) * vc_ref[...]
    h_ref[...] = h
    via_ref[...] = via

    def put(where, top, bottom):
        a_ref[where, :] = jnp.where(even, bottom, top)
        b_ref[where, :] = jnp.where(even, top, bottom)

    n = HALO * scen
    put(pl.ds(0, n), lf_ref[0:n, :], lf_ref[rows * scen - n :, :])
    put(pl.ds(n, SLOT), h[:SLOT], h[rows - SLOT :])
    put(pl.ds(n + SLOT, SLOT), via[:SLOT], via[rows - SLOT :])
    put(pl.ds(n + 2 * SLOT, 8), rr_ref[:8, :], rr_ref[rows - 8 :, :])


def packer(scen, cols):
    lane = lax.broadcasted_iota(jnp.int32, (scen, cols), 1)
    is_flux = jnp.logical_or(
        jnp.logical_and(lane >= 1, lane <= 6), jnp.logical_and(lane >= cols - 7, lane <= cols - 3)
    )
    is_t = jnp.logical_or(lane == 0, lane == cols - 2)
    is_end = lane == cols - 1
    is_rolled = jnp.logical_and(lane >= 8, lane <= 11)

    def pack(tl, q, jl, fl, p, grid_row):
        moved = jl if p is None else jnp.where(is_end, p, jl)
        rolled = pltpu.roll(moved, 10, 1)
        return jnp.where(
            is_flux, fl, jnp.where(is_t, tl, jnp.where(is_end, q, jnp.where(is_rolled, rolled, grid_row)))
        )

    def add_p(w, p):
        return jnp.where(lane == 9, pltpu.roll(p, 10, 1), w)

    return pack, add_p


def lower_row(v, via, minus_inv, vs, cols):
    q = via * v
    tl = q * minus_inv
    dl = pltpu.roll(tl, 1, 1) - tl
    jl = vs * dl
    return q, tl, dl, jl, jl - pltpu.roll(jl, cols - 1, 1)


def core_kernel(
    scen, lf_ref, h_ref, via_ref, cc_ref, pm_ref, cr_ref, pick_ref,
    fl_ref, acc_ref, edge_ref, low_ref, strip_ref, res_ref,
    inv_s, low_s, w_s,
):
    rows, cols = h_ref.shape
    _, first_y, last_y = place("gy")
    lane = lax.broadcasted_iota(jnp.int32, (rows, cols), 1)
    h, via = h_ref[...], via_ref[...]
    inv_s[...] = 1.0 / (h + pltpu.roll(h, rows - 1, 0) + via + LEAK)

    tie_low = via + pm_ref[...].astype(F32) * PAD + LEAK
    vs = jnp.where(jnp.logical_and(first_y, lane == 0), 0.0, cc_ref[...])
    open_end = jnp.logical_and(jnp.logical_not(last_y), lane == cols - 1)
    vs_next = jnp.where(lane == cols - 1, 0.0, pltpu.roll(vs, cols - 1, 1))
    diag_low = vs + vs_next + tie_low
    low_s[0] = jnp.where(open_end, 0.0, -1.0 / diag_low)
    low_s[1] = tie_low
    low_s[2] = jnp.where(jnp.logical_or(open_end, lane == 0), 0.0, vs)
    low_s[3] = jnp.where(
        lane == 12,
        pltpu.roll(vs, 12, 1),
        jnp.where(
            lane == 13,
            pltpu.roll(diag_low, 14, 1),
            jnp.where(lane == 14, pltpu.roll(tie_low, 15, 1), pltpu.roll(vs, 16, 1)),
        ),
    )
    low_ref[...] = jnp.concatenate([low_s[k, rows - 1 : rows, :] for k in range(4)] * 2, 0)
    pack, _ = packer(scen, cols)

    def bc(ref, r):
        return jnp.broadcast_to(ref[pl.ds(r, 1), :], (scen, cols))

    def low(k, r):
        return jnp.broadcast_to(low_s[k, pl.ds(r, 1), :], (scen, cols))

    def keep(i, x):
        edge_ref[pl.ds(i * scen, scen), :] = x

    zero = jnp.zeros((scen, cols), F32)
    g0 = g1 = g2 = g3 = zero
    v0 = hv0 = t0 = None
    last = rows - 1
    for r in range(rows):
        v1 = hv1 = dv1 = None
        if r < last:
            load = lf_ref[pl.ds(r * scen, scen), :]
            v1 = load * bc(inv_s, r)
            g0 += load * v1
            g1 += (bc(via_ref, r) + LEAK) * v1 * v1
            if r > 0:
                dv1 = v0 - v1
                hv1 = bc(h_ref, r) * dv1
                g1 += hv1 * dv1
        if r > 0:
            m = r - 1
            via_m = bc(via_ref, m)
            tie = via_m + LEAK
            q, tl, dl, jl, fl = lower_row(v0, via_m, low(0, m), low(2, m), cols)
            fl_ref[pl.ds(m * scen, scen), :] = fl
            g2 -= q * tl
            g3 += low(1, m) * tl * tl + jl * dl
            p = t1 = None
            if 0 < m < last - 1:
                q_up = tie * v0 - hv0 + hv1
                t1 = q_up * bc(inv_s, m)
                p = via_m * t1
                g2 += q_up * t1
                g3 += tie * t1 * t1 - 2.0 * p * tl
                if m > 1:
                    dt = t0 - t1
                    g3 += bc(h_ref, m) * dt * dt
            w = pack(tl, q, jl, fl, p, low(3, m))
            w_s[pl.ds(m * scen, scen), :] = w
            if m == 0:
                keep(0, v0)
                keep(1, hv1)
                keep(3, tl)
                keep(8, w)
            if m == 1:
                keep(2, t1)
            if m == last - 2:
                keep(6, t1)
            if m == last - 1:
                keep(4, v0)
                keep(5, hv0)
                keep(7, tl)
                keep(9, w)
            t0 = t1
        v0, hv0 = v1, hv1

    size = rows * scen
    fl_ref[pl.ds(last * scen, scen), :] = zero
    w_s[pl.ds(last * scen, scen), :] = zero
    w_s[pl.ds(size, rows), :] = cr_ref[...]
    w_s[size + rows :, :] = jnp.zeros((w_s.shape[0] - size - rows, cols), F32)
    for k, g in enumerate((g0, g1, g2, g3)):
        acc_ref[pl.ds(k * scen, scen), :] = g
    picked = dot_nt(pick_ref[...], w_s[...])
    for k in range(size // cols):
        strip_ref[pl.ds(k * PICKED, PICKED), :] = picked[:PICKED, k * cols : (k + 1) * cols]
    res_ref[...] = picked[PICKED + 8 :, size : size + cols]


def join_kernel(
    scen, lf_ref, h_ref, via_ref, acc_ref, edge_ref, low_ref, strip_ref, res_ref, a_ref, b_ref, pick_ref,
    msg_ref, other_ref, fl_ref,
    w_s,
):
    rows, cols = h_ref.shape
    odd_x = lax.rem(lax.axis_index("gx"), 2) == 1
    even_y = lax.rem(lax.axis_index("gy"), 2) == 0
    before, after = pick_side(odd_x, a_ref, b_ref)
    n = HALO * scen
    last = rows - 1

    def grid(h, via):
        tie = via + LEAK
        inv = 1.0 / (h + pltpu.roll(h, 15, 0) + tie)

        def row(x, i):
            return jnp.broadcast_to(x[i : i + 1], (scen, cols))

        return (lambda i: row(h, i)), (lambda i: row(tie, i)), (lambda i: row(inv, i)), (lambda i: row(via, i))

    def edge(i):
        return edge_ref[pl.ds(i * scen, scen), :]

    pack, add_p = packer(scen, cols)

    h, tie, inv, via = grid(
        jnp.concatenate([before(pl.ds(n + SLOT - 8, 8)), h_ref[:8, :]], 0),
        jnp.concatenate([before(pl.ds(n + 2 * SLOT - 8, 8)), via_ref[:8, :]], 0),
    )
    v0, hv1, t1, tl0 = (edge(i) for i in range(4))
    far, near = before(pl.ds(n - 2 * scen, scen)) * inv(6), before(pl.ds(n - scen, scen)) * inv(7)
    dv0 = near - v0
    hv0 = h(8) * dv0
    t_near = (tie(7) * near - h(7) * (far - near) + hv0) * inv(7)
    q_up = tie(8) * v0 - hv0 + hv1
    t0 = q_up * inv(8)
    d0, d1 = t_near - t0, t0 - t1
    p = via(8) * t0
    g1 = hv0 * dv0
    g2 = q_up * t0
    g3 = tie(8) * t0 * t0 + h(8) * d0 * d0 + h(9) * d1 * d1 - 2.0 * p * tl0
    w_first = add_p(edge(8), p)

    h, tie, inv, via = grid(
        jnp.concatenate([h_ref[rows - 8 :, :], after(pl.ds(n, 8))], 0),
        jnp.concatenate([via_ref[rows - 8 :, :], after(pl.ds(n + SLOT, 8))], 0),
    )
    v0, hv0, t0, tl0 = (edge(i) for i in range(4, 8))
    load = lf_ref[pl.ds(last * scen, scen), :]
    v1 = load * inv(7)
    v2 = after(pl.ds(0, scen)) * inv(8)
    dv1 = v0 - v1
    hv1, hv2 = h(7) * dv1, h(8) * (v1 - v2)
    q0 = tie(6) * v0 - hv0 + hv1
    q1 = tie(7) * v1 - hv1 + hv2
    t1 = q0 * inv(6)
    t2 = q1 * inv(7)
    d1, d2 = t0 - t1, t1 - t2
    p0, p1 = via(6) * t1, via(7) * t2
    g0 = load * v1
    g1 += hv1 * dv1 + tie(7) * v1 * v1
    g2 += q0 * t1 + q1 * t2
    g3 += tie(6) * t1 * t1 + tie(7) * t2 * t2 + h(6) * d1 * d1 + h(7) * d2 * d2 - 2.0 * p0 * tl0

    def low(k):
        return jnp.broadcast_to(low_ref[pl.ds(k, 1), :], (scen, cols))

    q, tl, dl, jl, fl = lower_row(v1, via(7), low(0), low(2), cols)
    fl_ref[...] = fl
    g2 -= q * tl
    g3 += tl * (low(1) * tl - 2.0 * p1) + jl * dl

    w_s[...] = jnp.zeros_like(w_s)
    w_s[0:scen, :] = w_first
    for k, g in enumerate((g0, g1, g2, g3)):
        w_s[pl.ds((k + 1) * scen, scen), :] = acc_ref[pl.ds(k * scen, scen), :] + g
    w_s[cols - 2 * scen : cols - scen, :] = add_p(edge(9), p0)
    w_s[cols - scen :, :] = pack(tl, q, jl, fl, p1, low(3))
    fresh = dot_nt(pick_ref[: PICKED + 8, :], w_s[...])

    lane = lax.broadcasted_iota(jnp.int32, (PICKED, cols), 1)
    parts = rows * scen // cols
    for k in range(parts):
        strip = strip_ref[pl.ds(k * PICKED, PICKED), :]
        if k == 0:
            strip = jnp.where(lane < scen, fresh[:PICKED], strip)
        if k == parts - 1:
            strip = jnp.where(lane >= cols - 2 * scen, fresh[:PICKED], strip)
        firsts, lasts = strip[8:16], strip[16:24]
        msg_ref[pl.ds(k * 16, 8), :] = strip[:8]
        msg_ref[pl.ds(k * 16 + 8, 8), :] = jnp.where(even_y, lasts, firsts)
        other_ref[pl.ds(k * 8, 8), :] = jnp.where(even_y, firsts, lasts)
    msg_ref[pl.ds(parts * 16, 8), :] = jnp.where(even_y, res_ref[8:, :], res_ref[:8, :])
    other_ref[pl.ds(parts * 8, 8), :] = jnp.where(even_y, res_ref[:8, :], res_ref[8:, :])
    msg_ref[pl.ds(parts * 16 + 8, 8), :] = fresh[PICKED:]


def across(ref, offset):
    parts = ref.shape[0] // 16 - 1
    return jnp.concatenate([ref[pl.ds(16 * k + offset, 8), :] for k in range(parts)], 1)


def merge_kernel(scen, axis, step, mine_ref, got_ref, other_ref, out_ref):
    cols = mine_ref.shape[1]
    parts = mine_ref.shape[0] // 16 - 1
    on_left = lax.rem(lax.div(lax.axis_index(axis), step), 2) == 0
    mine, got = across(mine_ref, 0), across(got_ref, 0)
    left, right = jnp.where(on_left, mine, got), jnp.where(on_left, got, mine)
    t_next, vs_next = right[0:1], right[1:2]
    q, d, tie, p, vs, t_in = (left[i : i + 1] for i in range(2, 8))
    t = -q / (d + vs_next)
    d_in, d_out = t_in - t, t - t_next
    i2 = -q * t
    i3 = t * (tie * t - 2.0 * p) + vs * d_in * d_in + vs_next * d_out * d_out
    both = jnp.concatenate([i2, i3], 0)
    both = sum(both[:, k * cols : (k + 1) * cols] for k in range(parts))
    shift = scen
    while shift < cols:
        both = both + pltpu.roll(both, shift, 1)
        shift *= 2
    group = lax.div(lax.broadcasted_iota(jnp.int32, (8, cols), 1), scen)
    add = jnp.where(group == 3, both[0:1], jnp.where(group == 4, both[1:2], 0.0))
    sums = mine_ref[parts * 16 + 8 :, :] + got_ref[parts * 16 + 8 :, :] + add
    if out_ref.shape[0] == 8:
        out_ref[...] = sums
    else:
        row = lax.broadcasted_iota(jnp.int32, (8, cols), 0)
        for k in range(parts):
            at = slice(k * cols, (k + 1) * cols)
            out_ref[pl.ds(k * 16, 8), :] = jnp.where(row < 2, left[:, at], right[:, at])
            out_ref[pl.ds(k * 16 + 8, 8), :] = other_ref[pl.ds(k * 8, 8), :]
        out_ref[pl.ds(parts * 16, 8), :] = other_ref[pl.ds(parts * 8, 8), :]
        out_ref[parts * 16 + 8 :, :] = sums


def row_kernel(
    scen, lf_ref, h_ref, via_ref, rr_ref, a_ref, b_ref,
    v_ref, t_ref, gv_ref, gt_ref, br_ref,
    inv_s, h_s, tie_s, fv_s, ft_s, sv_s, st_s, s0_s,
):
    rows, cols = h_ref.shape
    at_x, first, last = place("gx")
    before, after = pick_side(lax.rem(at_x, 2) == 1, a_ref, b_ref)
    n = HALO * scen
    at = pl.ds(n, SLOT)
    h = jnp.concatenate([before(at), h_ref[...], after(at)], 0)
    at = pl.ds(n + SLOT, SLOT)
    tie = jnp.concatenate([before(at), via_ref[...], after(at)], 0) + LEAK
    h_s[...] = h
    tie_s[...] = tie
    inv_s[...] = 1.0 / (h + pltpu.roll(h, h.shape[0] - 1, 0) + tie)

    def load(r):
        if r < 0:
            return before(pl.ds((r + HALO) * scen, scen))
        if r >= rows:
            return after(pl.ds((r - rows) * scen, scen))
        return lf_ref[pl.ds(r * scen, scen), :]

    def bc(ref, r):
        return jnp.broadcast_to(ref[pl.ds(r + SLOT, 1), :], (scen, cols))

    v0 = hv0 = t0 = ht0 = None
    for r in range(-HALO, rows + HALO):
        v1 = load(r) * bc(inv_s, r)
        hv1 = None
        if r > -HALO:
            hv1 = bc(h_s, r) * (v0 - v1)
        if r > 1 - HALO:
            m = r - 1
            fv = hv0 - hv1
            t1 = (bc(tie_s, m) * v0 - fv) * bc(inv_s, m)
            ht1 = None
            if m > 1 - HALO:
                ht1 = bc(h_s, m) * (t0 - t1)
                if m > 2 - HALO:
                    ft = ht0 - ht1
                    at = pl.ds((m - 1 + STEPS - 1) * scen, scen)
                    ft_s[at, :] = ft
                    st_s[at, :] = ft
                if m < rows + STEPS - 1:
                    at = pl.ds((m + STEPS - 1) * scen, scen)
                    fv_s[at, :] = fv
                    sv_s[at, :] = fv
            if 0 <= m < rows:
                v_ref[pl.ds(m, scen, stride=rows), :] = v0
                t_ref[pl.ds(m, scen, stride=rows), :] = t1
            t0, ht0 = t1, ht1
        v0, hv0 = v1, hv1

    n += 2 * SLOT
    count = rows + 2 * (STEPS - 1)
    rate_first = jnp.where(first, 0.0, RELAX)
    rate_last = jnp.where(last, 0.0, RELAX)

    def rate(r):
        return rate_first if r == 0 else rate_last if r == rows else RELAX

    size = rows + 16
    row = lax.broadcasted_iota(jnp.int32, (size, cols), 0)
    rates = jnp.where(row == 8, rate_first, jnp.where(row == 8 + rows, rate_last, RELAX))
    s0_s[...] = jnp.concatenate([before(pl.ds(n, 8)), rr_ref[...], after(pl.ds(n, 8))], 0)

    def start_step():
        now = s0_s[...]
        flux = rates * (pltpu.roll(now, 1, 0) - now)
        return now + flux - pltpu.roll(flux, size - 1, 0)

    def one(_, carry):
        s0_s[...] = start_step()
        for f_ref, s_ref in ((fv_s, sv_s), (ft_s, st_s)):
            here = s_ref[pl.ds(0, scen), :]
            flux = jnp.zeros_like(here)
            for i in range(count):
                r = i - (STEPS - 1)
                at = pl.ds(i * scen, scen)
                if i + 1 < count:
                    following = s_ref[pl.ds((i + 1) * scen, scen), :]
                    flux_next = rate(r + 1) * (here - following)
                else:
                    following, flux_next = here, jnp.zeros_like(here)
                s_ref[at, :] = here + (flux - flux_next) + f_ref[at, :]
                here, flux = following, flux_next
        return carry

    lax.fori_loop(0, STEPS - 1, one, 0)
    br_ref[...] = start_step()[8 : 8 + rows]
    gain = RELAX * DRIVE
    for m in range(rows):
        at = pl.ds((m + STEPS - 1) * scen, scen)
        gv_ref[pl.ds(m, scen, stride=rows), :] = gain * sv_s[at, :]
        gt_ref[pl.ds(m, scen, stride=rows), :] = gain * st_s[at, :]


def col_kernel(scen, fl_ref, fl_last_ref, cr_ref, own_ref, *rest):
    *got_refs, source_ref, start_ref, gl_ref, bc_ref, out_s = rest
    rows, cols = cr_ref.shape
    at, first, last = place("gy")
    kind = first.astype(jnp.int32) + 2 * last.astype(jnp.int32)
    odd = lax.rem(at, 2) == 1
    res_at = pl.ds(own_ref.shape[0] - 16, 8)

    def contents(ref):
        return across(ref, 0), across(ref, 8), ref[res_at, :]

    paired = contents(got_refs[0])
    met = tuple(jnp.zeros_like(x) for x in paired)
    for k, ref in enumerate(got_refs[1:], 1):
        span = lax.rem(at, 2 << k)
        here = jnp.logical_or(span == (1 << k) - 1, span == 1 << k)
        met = tuple(jnp.where(here, x, y) for x, y in zip(contents(ref), met))
    sums_before, before, res_before = (jnp.where(odd, x, y) for x, y in zip(paired, met))
    sums_after, after, res_after = (jnp.where(odd, y, x) for x, y in zip(paired, met))
    own = across(own_ref, 0)

    def seam(left, right):
        q, d, _, _, vs, t_in = (left[i : i + 1] for i in range(2, 8))
        t_next, vs_next = right[0:1], right[1:2]
        diag = d + vs_next
        t = -q / jnp.where(diag > 0, diag, 1.0)
        return vs * (t_in - t), vs_next * (t - t_next)

    jl_last, jl_0 = seam(sums_before, own)
    jr_last, jr_0 = seam(own, sums_after)
    jr_last = jnp.where(last, 0.0, jr_last)
    jr_0 = jnp.where(last, 0.0, jr_0)
    zero = jnp.zeros_like(jl_0)
    strip = jnp.concatenate(
        [
            before[1:6],
            before[0:1] - jl_last,
            jl_last - jl_0,
            zero,
            jr_0 - after[0:1],
            after[1:7],
            zero,
            jl_0,
            -jr_last,
            jr_last - jr_0,
            zero,
            zero,
            zero,
            zero,
            zero,
        ],
        0,
    )
    source = source_ref[kind]
    edge = dot_tn(strip, source[cols:])
    done = (rows - 1) * scen
    out_s[0:done, :] = dot_nn(fl_ref[0:done, :], source[:cols]) + edge[:done]
    out_s[done:, :] = dot_nn(fl_last_ref[...], source[:cols]) + edge[done:]
    for m in range(rows):
        gl_ref[pl.ds(m, scen, stride=rows), :] = out_s[pl.ds(m * scen, scen), :]
    start = start_ref[kind]
    edge = dot_tn(jnp.concatenate([res_before, res_after], 0), start[cols:])
    bc_ref[...] = dot_nn(cr_ref[...], start[:cols]) + edge[:rows]


def final_kernel(
    scen, rows, a_ref, b_ref, v_ref, t_ref, gv_ref, gt_ref, gl_ref, br_ref, bc_ref, up_ref, row_ref, col_ref
):
    cols = v_ref.shape[1]
    sums = a_ref[...] + b_ref[...]
    g0, g1, g2, g3 = (pltpu.roll(sums, cols - (k + 1) * scen, 1) for k in range(4))
    alpha = g0 / g1
    rz = alpha * alpha * g2 - g0
    grow = alpha * g2 / g1
    beta_alpha = rz / (alpha * alpha * (g3 - g2 * g2 / g1))
    c0 = alpha + beta_alpha * grow
    c1 = -alpha * beta_alpha
    lane = lax.broadcasted_iota(jnp.int32, (scen, cols), 1)
    sub = lax.broadcasted_iota(jnp.int32, (scen, cols), 0)

    def column(c):
        tall = jnp.concatenate([c] * (scen // 8), 0)
        return jnp.sum(jnp.where(lane == sub, tall, 0.0), 1, keepdims=True)

    c0, c1 = column(c0), column(c1)
    br, bc = br_ref[...], bc_ref[...]
    for s in range(scen):
        at = pl.ds(s * rows, rows)
        a = jnp.broadcast_to(c0[s : s + 1], (rows, cols))
        b = jnp.broadcast_to(c1[s : s + 1], (rows, cols))
        up_ref[s] = a * v_ref[at, :] + b * t_ref[at, :]
        row_ref[s] = br + a * gv_ref[at, :] + b * gt_ref[at, :]
        col_ref[s] = bc + b * gl_ref[at, :]


def swap(block, axis, mask):
    count = lax.axis_size(axis)
    return lax.ppermute(block, axis, [(i, i ^ mask) for i in range(count)])


def exchange(even_side, odd_side, axis):
    count = lax.axis_size(axis)

    def pairs(start):
        return [(i + a, i + 1 - a) for i in range(start, count - 1, 2) for a in (0, 1)]

    second = lax.ppermute(odd_side, axis, pairs(1))
    return lax.ppermute(even_side, axis, pairs(0)), second


def call(kernel, out, scratch, cost, *args, space=pltpu.VMEM):
    return pl.pallas_call(
        kernel,
        out_shape=out,
        in_specs=[pl.BlockSpec(memory_space=space)] * len(args),
        out_specs=jax.tree.map(lambda _: pl.BlockSpec(memory_space=pltpu.VMEM), out),
        scratch_shapes=scratch,
        compiler_params=pltpu.CompilerParams(vmem_limit_bytes=24 * 2**20),
        cost_estimate=pl.CostEstimate(flops=cost, bytes_accessed=0, transcendentals=0),
    )(*args)


def on_device(
    load_current, row_conductance, col_conductance, via_conductance, pad_mask, via_mask, row_residual, col_residual
):
    scen, rows, cols = load_current.shape
    size = rows * scen
    parts = size // cols

    def f32(*shape):
        return jax.ShapeDtypeStruct(shape, F32)

    def vmem(*shape):
        return pltpu.VMEM(shape, F32)

    pick = jnp.asarray(picker(cols))
    source, start = (jnp.asarray(m) for m in spread(cols))
    grid, field = f32(rows, cols), f32(size, cols)

    wide = f32(HALO * scen + 2 * SLOT + 8, cols)
    sources = (load_current, row_conductance, via_conductance, via_mask, row_residual)
    lf, h, via, x_a, x_b = call(
        pack_kernel,
        (field, grid, grid, wide, wide),
        [pltpu.VMEM(x.shape, x.dtype) for x in sources] + [pltpu.SemaphoreType.DMA((len(sources),))],
        10**5,
        *(pltpu.with_memory_space_constraint(x, pltpu.HBM) for x in sources),
        space=pltpu.HBM,
    )
    x_a, x_b = exchange(x_a, x_b, "gx")

    fl, acc, edge, low, strip, res = call(
        functools.partial(core_kernel, scen),
        (field, f32(4 * scen, cols), f32(10 * scen, cols), f32(8, cols), f32(parts * PICKED, cols), f32(16, cols)),
        [vmem(rows, cols), vmem(4, rows, cols), vmem(size + cols * (-(-rows // cols)), cols)],
        10**7,
        lf, h, via, col_conductance, pad_mask, col_residual, pick,
    )
    x_a, x_b, acc = lax.optimization_barrier((x_a, x_b, acc))

    msg, other, fl_last = call(
        functools.partial(join_kernel, scen),
        (f32(parts * 16 + 16, cols), f32(parts * 8 + 8, cols), f32(scen, cols)),
        [vmem(cols, cols)],
        10**6,
        lf, h, via, acc, edge, low, strip, res, x_a, x_b, pick,
    )

    ext = rows + 2 * SLOT
    reach = (rows + 2 * (STEPS - 1)) * scen
    v, t, gv, gt, br = call(
        functools.partial(row_kernel, scen),
        (field, field, field, field, grid),
        [vmem(ext, cols)] * 3 + [vmem(reach, cols)] * 4 + [vmem(rows + 16, cols)],
        10**7,
        lf, h, via, row_residual, x_a, x_b,
    )

    first_msg, received = msg, []
    step, count = 1, lax.axis_size("gy")
    while step < count:
        got = swap(msg, "gy", 2 * step - 1)
        received.append(got)
        if 2 * step >= count:
            got, br = lax.optimization_barrier((got, br))
        out = f32(*msg.shape) if 2 * step < count else f32(8, cols)
        msg = call(functools.partial(merge_kernel, scen, "gy", step), out, [], 10**5, msg, got, other)
        step *= 2
    sums = msg

    gl, bc = call(
        functools.partial(col_kernel, scen),
        (field, grid),
        [vmem(size, cols)],
        10**7,
        fl, fl_last, col_residual, first_msg, *received, source, start,
    )

    step = lax.axis_size("gx") // 2
    while step > 1:
        got = swap(sums, "gx", step)
        if 2 * step == lax.axis_size("gx"):
            got, bc = lax.optimization_barrier((got, bc))
        sums = sums + got
        step //= 2
    rest = swap(sums, "gx", 1)

    shape = f32(scen, rows, cols)
    return call(
        functools.partial(final_kernel, scen, rows),
        (shape, shape, shape),
        [],
        10**6,
        sums, rest, v, t, gv, gt, gl, br, bc,
    )


def solution(mesh):
    field = P(None, ("grp", "gx"), "gy")
    grid = P(("grp", "gx"), "gy")
    return jax.shard_map(
        on_device,
        mesh=mesh,
        in_specs=(field,) + (grid,) * 7,
        out_specs=(field,) * 3,
        check_vma=False,
    )
```

time: 26.7 us -> 25.5 us (0.955)
  waiting for transfers between devices: 4.97 us -> 4.12 us
  starting transfers between devices: 13.8 us -> 13.4 us
    ppermute x6, waiting for transfers between devices: 4.97 us -> 4.12 us  [the longest x4 4.11 us: swap(): return lax.ppermute(block, axis, [(i, i ^ mask) for i in range(count)])]
    ppermute x6, starting transfers between devices: 13.8 us -> 13.4 us  [the longest x4 12.3 us: swap(): return lax.ppermute(block, axis, [(i, i ^ mask) for i in range(count)])]
    pallas_call x7 -> x8, Pallas kernels: 6.98 us -> 6.91 us  [call(): pl.pallas_call(kernel, out_shape=out, in_specs=[pl.BlockSpec(memory_space...]
  transfers between devices with their start and end apart: 6 -> 6, of which waited for: 5 -> 4; matrix products, arithmetic and copies ran while one was open for 0% -> 0% of each run, Pallas kernels for 9% -> 15%
where the time goes in v3:
time: 25.5 us; the launch traced here: 25.3 us
  starting transfers between devices  13.4 us (53%)
  Pallas kernels  6.91 us (27%)
  waiting for transfers between devices  4.12 us (16%)
  between operations  0.76 us (3%)
    ppermute x4, starting transfers between devices, swap(): return lax.ppermute(block, axis, [(i, i ^ mask) for i in range(count)])  12.3 us
    pallas_call x8, Pallas kernels, call(): pl.pallas_call(kernel, out_shape=out, in_specs=[pl.BlockSpec(memory_space...  6.91 us
    ppermute x4, waiting for transfers between devices, swap(): return lax.ppermute(block, axis, [(i, i ^ mask) for i in range(count)])  4.11 us
    ppermute x1, starting transfers between devices, exchange(): second = lax.ppermute(odd_side, axis, pairs(1))  0.65 us
    ppermute x1, starting transfers between devices, exchange(): return (lax.ppermute(even_side, axis, pairs(0)), second)  0.52 us
  transfers between devices with their start and end apart: 6, of which 4 were waited for; matrix products, arithmetic and copies ran while one was open for 0% of the time, Pallas kernels for 15%

profile of v3, /device:TPU:0, one launch (start us, length us, event | category | flops | bytes accessed | tf_op | source)
XLA Modules:
  0.0 25.3 jit_solution(5584330250087313758)
XLA Ops:
  0.6 0.0 copy-start.2
  0.6 0.0 copy-start.3
  0.7 0.0 copy-start.5
  0.7 0.0 copy-start.6
  0.7 1.1 %shard_map.130 = (f32[512,128]{1,0:T(8,128)S(1)}, f32[32,128]{1,0:T(8,128)S(1)}, f32[32,128]{1,0:T(8,128)S(1)}, f32[184,128]{1,0:T(8,128)S(1)}, f32[184,128]{1,0:T(8,128)S(1)}) custom-call(bf16[16,32,128]{2,1,0:T(8,128)(2,1)} %refs_0_.1, f32[32,128]{1,0:T(8,128)} %refs_1_.1, f32[32,128]{1,0:T(8,128)} %refs_2_.1, s32[32,128]{1,0:T(8,128)} %refs_3_.1, ...), custom_call_target="tpu_custom_call" | custom-call | flops 100000 | tf_op jit(solution)/shard_map/pallas_call | solution.py:618
  1.8 0.5 %collective-permute-start = (f32[184,128]{1,0:T(8,128)S(1)}, f32[184,128]{1,0:T(8,128)S(1)}, u32[]{:S(2)}, u32[]{:S(2)}) collective-permute-start(f32[184,128]{1,0:T(8,128)S(1)} %get-tuple-element.34), channel_id=1, source_target_pairs={{0,4},{4,0},{8,12},{12,8},{1,5},{5,1},{9,13},{13,9},{2,6},{6,2},{1... | collective-permute-start | bytes 282632 | tf_op jit(solution)/shard_map/ppermute | solution.py:614
  2.3 0.7 %collective-permute-start.1 = (f32[184,128]{1,0:T(8,128)S(1)}, f32[184,128]{1,0:T(8,128)S(1)}, u32[]{:S(2)}, u32[]{:S(2)}) collective-permute-start(f32[184,128]{1,0:T(8,128)S(1)} %get-tuple-element.35), channel_id=1, source_target_pairs={{4,8},{8,4},{5,9},{9,5},{6,10},{10,6},{7,11},{11,7},{20,24},{24,20... | collective-permute-start | bytes 282632 | tf_op jit(solution)/shard_map/ppermute | solution.py:613
  3.0 0.0 copy-done.2
  3.0 0.0 copy-done.3
  3.0 0.0 copy-done.5
  3.0 0.0 copy-done.6
  3.0 1.0 %shard_map.131 = (f32[512,128]{1,0:T(8,128)S(1)}, f32[64,128]{1,0:T(8,128)S(1)}, f32[160,128]{1,0:T(8,128)S(1)}, f32[8,128]{1,0:T(8,128)S(1)}, f32[96,128]{1,0:T(8,128)S(1)}, /*index=5*/f32[16,128]{1,0:T(8,128)S(1)}) custom-call(f32[512,128]{1,0:T(8,128)S(1)} %get-tuple-element.31.lf_ref, f32[32,128]{1,0:T(8,128)S(1)} %get-tuple-element.32.h_ref, ...), custom_call_target="tpu_custom_call" | custom-call | flops 10000000 | tf_op jit(solution)/shard_map/pallas_call | solution.py:618
  4.0 0.0 collective-permute-done.a_ref
  4.0 0.0 collective-permute-done.1.b_ref
  4.0 0.3 %shard_map.132 = (f32[80,128]{1,0:T(8,128)S(1)}, f32[40,128]{1,0:T(8,128)S(1)}, f32[16,128]{1,0:T(8,128)S(1)}) custom-call(f32[512,128]{1,0:T(8,128)S(1)} %get-tuple-element.31.lf_ref, f32[32,128]{1,0:T(8,128)S(1)} %get-tuple-element.32.h_ref, f32[32,128]{1,0:T(8,128)S(1)} %get-tuple-element.33.via_ref, f32[64,128]{1,0:T(8,128)S(1)} %get-tuple-element.37.acc_ref, ...), custom_call_target="tpu_custom_call" | custom-call | flops 1000000 | tf_op jit(solution)/shard_map/pallas_call | solution.py:618
  4.4 2.6 %collective-permute-start.2 = (f32[80,128]{1,0:T(8,128)S(1)}, f32[80,128]{1,0:T(8,128)S(1)}, u32[]{:S(2)}, u32[]{:S(2)}) collective-permute-start(f32[80,128]{1,0:T(8,128)S(1)} %get-tuple-element.44.mine_ref.own_ref), channel_id=1, source_target_pairs={{0,1},{1,0},{2,3},{3,2},{4,5},{5,4},{6,7},{7,6},{8,9},{9,8},{10,11... | collective-permute-start | bytes 122888 | tf_op jit(solution)/shard_map/ppermute | solution.py:604
  7.0 2.0 %collective-permute-done.2.got_ref.rest_0_ = f32[80,128]{1,0:T(8,128)S(1)} collective-permute-done((f32[80,128]{1,0:T(8,128)S(1)}, f32[80,128]{1,0:T(8,128)S(1)}, u32[]{:S(2)}, u32[]{:S(2)}) %collective-permute-start.2) | collective-permute-done | bytes 40992 | tf_op jit(solution)/shard_map/ppermute | solution.py:604
  9.0 0.0 copy-start.4
  9.0 0.2 shard_map.133.mine_ref
  9.2 0.0 copy-start
  9.2 0.0 copy-start.1
  9.2 4.1 %collective-permute-start.3 = (f32[80,128]{1,0:T(8,128)S(1)}, f32[80,128]{1,0:T(8,128)S(1)}, u32[]{:S(2)}, u32[]{:S(2)}) collective-permute-start(f32[80,128]{1,0:T(8,128)S(1)} %shard_map.133.mine_ref), channel_id=1, source_target_pairs={{0,3},{1,2},{2,1},{3,0},{4,7},{5,6},{6,5},{7,4},{8,11},{9,10},{10,... | collective-permute-start | bytes 122888 | tf_op jit(solution)/shard_map/ppermute | solution.py:604
  13.3 0.0 copy-done.4
  13.3 2.0 %shard_map.134 = (f32[512,128]{1,0:T(8,128)S(1)}, f32[512,128]{1,0:T(8,128)S(1)}, f32[512,128]{1,0:T(8,128)S(1)}, f32[512,128]{1,0:T(8,128)S(1)}, f32[32,128]{1,0:T(8,128)S(1)}) custom-call(f32[512,128]{1,0:T(8,128)S(1)} %get-tuple-element.31.lf_ref, f32[32,128]{1,0:T(8,128)S(1)} %get-tuple-element.32.h_ref, f32[32,128]{1,0:T(8,128)S(1)} %get-tuple-element.33.via_ref, ...), custom_call_target="tpu_custom_call" | custom-call | flops 10000000 | tf_op jit(solution)/shard_map/pallas_call | solution.py:618
  15.3 0.3 %collective-permute-done.3.got_ref.rest_1_ = f32[80,128]{1,0:T(8,128)S(1)} collective-permute-done((f32[80,128]{1,0:T(8,128)S(1)}, f32[80,128]{1,0:T(8,128)S(1)}, u32[]{:S(2)}, u32[]{:S(2)}) %collective-permute-start.3) | collective-permute-done | bytes 40992 | tf_op jit(solution)/shard_map/ppermute | solution.py:604
  15.5 0.2 shard_map.135
  15.8 5.6 %collective-permute-start.4 = (f32[8,128]{1,0:T(8,128)S(1)}, f32[8,128]{1,0:T(8,128)S(1)}, u32[]{:S(2)}, u32[]{:S(2)}) collective-permute-start(f32[8,128]{1,0:T(8,128)S(1)} %shard_map.135), channel_id=1, source_target_pairs={{0,8},{4,12},{8,0},{12,4},{1,9},{5,13},{9,1},{13,5},{2,10},{6,14},... | collective-permute-start | bytes 12296 | tf_op jit(solution)/shard_map/ppermute | solution.py:604
  21.4 0.0 copy-done
  21.4 0.0 copy-done.1
  21.4 0.9 %shard_map.136 = (f32[512,128]{1,0:T(8,128)S(1)}, f32[32,128]{1,0:T(8,128)S(1)}) custom-call(f32[512,128]{1,0:T(8,128)S(1)} %get-tuple-element.48.fl_ref, f32[16,128]{1,0:T(8,128)S(1)} %get-tuple-element.49.fl_last_ref, f32[32,128]{1,0:T(8,128)S(1)} %copy-done.3, f32[80,128]{1,0:T(8,128)S(1)} %get-tuple-element.44.mine_ref.own_ref, ...), custom_call_target="tpu_custom_call" | custom-call | flops 10000000 | tf_op jit(solution)/shard_map/pallas_call | solution.py:618
  22.2 0.7 %collective-permute-done.4 = f32[8,128]{1,0:T(8,128)S(1)} collective-permute-done((f32[8,128]{1,0:T(8,128)S(1)}, f32[8,128]{1,0:T(8,128)S(1)}, u32[]{:S(2)}, u32[]{:S(2)}) %collective-permute-start.4) | collective-permute-done | bytes 4128 | tf_op jit(solution)/shard_map/ppermute | solution.py:604
  22.9 0.0 collective-permute-start.5
  22.9 1.2 %collective-permute-done.5.b_ref = f32[8,128]{1,0:T(8,128)S(1)} collective-permute-done((f32[8,128]{1,0:T(8,128)S(1)}, f32[8,128]{1,0:T(8,128)S(1)}, u32[]{:S(2)}, u32[]{:S(2)}) %collective-permute-start.5) | collective-permute-done | bytes 4128 | tf_op jit(solution)/shard_map/ppermute | solution.py:604
  24.1 1.1 %shard_map.137 = (f32[16,32,128]{2,1,0:T(8,128)}, f32[16,32,128]{2,1,0:T(8,128)}, f32[16,32,128]{2,1,0:T(8,128)}) custom-call(f32[8,128]{1,0:T(8,128)S(1)} %add.3.a_ref, f32[8,128]{1,0:T(8,128)S(1)} %collective-permute-done.5.b_ref, f32[512,128]{1,0:T(8,128)S(1)} %get-tuple-element.52.v_ref, f32[512,128]{1,0:T(8,128)S(1)} %get-tuple-element.53.t_ref, ...), custom_call_target="tpu_custom_call" | custom-call | flops 1000000 | tf_op jit(solution)/shard_map/pallas_call | solution.py:618
  (1 shorter events, 0.0 us)
Async XLA Ops:
  0.6 2.3 %copy-start.2 = (f32[48,128]{1,0:T(8,128)S(1)}, f32[48,128]{1,0:T(8,128)}, u32[]{:S(2)}) copy-start(f32[48,128]{1,0:T(8,128)} %constant.6.clone.pick_ref) | copy-start | bytes 73732
  0.6 2.3 %copy-start.3 = (f32[32,128]{1,0:T(8,128)S(1)}, f32[32,128]{1,0:T(8,128)}, u32[]{:S(2)}) copy-start(f32[32,128]{1,0:T(8,128)} %cr_ref.3) | copy-start | bytes 49156
  0.7 2.3 %copy-start.5 = (f32[32,128]{1,0:T(8,128)S(1)}, f32[32,128]{1,0:T(8,128)}, u32[]{:S(2)}) copy-start(f32[32,128]{1,0:T(8,128)} %cc_ref.1) | copy-start | bytes 49156
  0.7 2.3 %copy-start.6 = (s32[32,128]{1,0:T(8,128)S(1)}, s32[32,128]{1,0:T(8,128)}, u32[]{:S(2)}) copy-start(s32[32,128]{1,0:T(8,128)} %pm_ref.1) | copy-start | bytes 49156
  1.8 2.2 %collective-permute-start = (f32[184,128]{1,0:T(8,128)S(1)}, f32[184,128]{1,0:T(8,128)S(1)}, u32[]{:S(2)}, u32[]{:S(2)}) collective-permute-start(f32[184,128]{1,0:T(8,128)S(1)} %get-tuple-element.34), channel_id=1, source_target_pairs={{0,4},{4,0},{8,12},{12,8},{1,5},{5,1},{9,13},{13,9},{2,6},{6,2},{1... | collective-permute-start | bytes 282632 | tf_op jit(solution)/shard_map/ppermute | solution.py:614
  2.3 1.7 %collective-permute-start.1 = (f32[184,128]{1,0:T(8,128)S(1)}, f32[184,128]{1,0:T(8,128)S(1)}, u32[]{:S(2)}, u32[]{:S(2)}) collective-permute-start(f32[184,128]{1,0:T(8,128)S(1)} %get-tuple-element.35), channel_id=1, source_target_pairs={{4,8},{8,4},{5,9},{9,5},{6,10},{10,6},{7,11},{11,7},{20,24},{24,20... | collective-permute-start | bytes 282632 | tf_op jit(solution)/shard_map/ppermute | solution.py:613
  4.4 4.6 %collective-permute-start.2 = (f32[80,128]{1,0:T(8,128)S(1)}, f32[80,128]{1,0:T(8,128)S(1)}, u32[]{:S(2)}, u32[]{:S(2)}) collective-permute-start(f32[80,128]{1,0:T(8,128)S(1)} %get-tuple-element.44.mine_ref.own_ref), channel_id=1, source_target_pairs={{0,1},{1,0},{2,3},{3,2},{4,5},{5,4},{6,7},{7,6},{8,9},{9,8},{10,11... | collective-permute-start | bytes 122888 | tf_op jit(solution)/shard_map/ppermute | solution.py:604
  9.0 4.3 %copy-start.4 = (f32[32,128]{1,0:T(8,128)S(1)}, f32[32,128]{1,0:T(8,128)}, u32[]{:S(2)}) copy-start(f32[32,128]{1,0:T(8,128)} %rr_ref.1) | copy-start | bytes 49156
  9.2 12.2 %copy-start = (f32[4,152,128]{2,1,0:T(8,128)S(1)}, f32[4,152,128]{2,1,0:T(8,128)}, u32[]{:S(2)}) copy-start(f32[4,152,128]{2,1,0:T(8,128)} %constant.7.clone.rest_2_) | copy-start | bytes 933892
  9.2 12.2 %copy-start.1 = (f32[4,144,128]{2,1,0:T(8,128)S(1)}, f32[4,144,128]{2,1,0:T(8,128)}, u32[]{:S(2)}) copy-start(f32[4,144,128]{2,1,0:T(8,128)} %constant.8.clone.rest_3_) | copy-start | bytes 884740
  9.2 6.3 %collective-permute-start.3 = (f32[80,128]{1,0:T(8,128)S(1)}, f32[80,128]{1,0:T(8,128)S(1)}, u32[]{:S(2)}, u32[]{:S(2)}) collective-permute-start(f32[80,128]{1,0:T(8,128)S(1)} %shard_map.133.mine_ref), channel_id=1, source_target_pairs={{0,3},{1,2},{2,1},{3,0},{4,7},{5,6},{6,5},{7,4},{8,11},{9,10},{10,... | collective-permute-start | bytes 122888 | tf_op jit(solution)/shard_map/ppermute | solution.py:604
  15.8 7.2 %collective-permute-start.4 = (f32[8,128]{1,0:T(8,128)S(1)}, f32[8,128]{1,0:T(8,128)S(1)}, u32[]{:S(2)}, u32[]{:S(2)}) collective-permute-start(f32[8,128]{1,0:T(8,128)S(1)} %shard_map.135), channel_id=1, source_target_pairs={{0,8},{4,12},{8,0},{12,4},{1,9},{5,13},{9,1},{13,5},{2,10},{6,14},... | collective-permute-start | bytes 12296 | tf_op jit(solution)/shard_map/ppermute | solution.py:604
  22.9 1.2 %collective-permute-start.5 = (f32[8,128]{1,0:T(8,128)S(1)}, f32[8,128]{1,0:T(8,128)S(1)}, u32[]{:S(2)}, u32[]{:S(2)}) collective-permute-start(f32[8,128]{1,0:T(8,128)S(1)} %add.3.a_ref), channel_id=1, source_target_pairs={{0,4},{4,0},{8,12},{12,8},{1,5},{5,1},{9,13},{13,9},{2,6},{6,2},{1... | collective-permute-start | bytes 12296 | tf_op jit(solution)/shard_map/ppermute | solution.py:604

commit v4 on v3

--- a/solution.py
+++ b/solution.py
@@ -271,7 +271,7 @@
 
 def join_kernel(
     scen, lf_ref, h_ref, via_ref, acc_ref, edge_ref, low_ref, strip_ref, res_ref, a_ref, b_ref, pick_ref,
-    msg_ref, other_ref, fl_ref,
+    pair_ref, plain_ref, seam_ref, fl_ref,
     w_s,
 ):
     rows, cols = h_ref.shape
@@ -352,6 +352,7 @@
 
     lane = lax.broadcasted_iota(jnp.int32, (PICKED, cols), 1)
     parts = rows * scen // cols
+    base = parts * 8 + 8
     for k in range(parts):
         strip = strip_ref[pl.ds(k * PICKED, PICKED), :]
         if k == 0:
@@ -359,31 +360,41 @@
         if k == parts - 1:
             strip = jnp.where(lane >= cols - 2 * scen, fresh[:PICKED], strip)
         firsts, lasts = strip[8:16], strip[16:24]
-        msg_ref[pl.ds(k * 16, 8), :] = strip[:8]
-        msg_ref[pl.ds(k * 16 + 8, 8), :] = jnp.where(even_y, lasts, firsts)
-        other_ref[pl.ds(k * 8, 8), :] = jnp.where(even_y, firsts, lasts)
-    msg_ref[pl.ds(parts * 16, 8), :] = jnp.where(even_y, res_ref[8:, :], res_ref[:8, :])
-    other_ref[pl.ds(parts * 8, 8), :] = jnp.where(even_y, res_ref[:8, :], res_ref[8:, :])
-    msg_ref[pl.ds(parts * 16 + 8, 8), :] = fresh[PICKED:]
-
-
-def across(ref, offset):
-    parts = ref.shape[0] // 16 - 1
-    return jnp.concatenate([ref[pl.ds(16 * k + offset, 8), :] for k in range(parts)], 1)
-
-
-def merge_kernel(scen, axis, step, mine_ref, got_ref, other_ref, out_ref):
-    cols = mine_ref.shape[1]
-    parts = mine_ref.shape[0] // 16 - 1
-    on_left = lax.rem(lax.div(lax.axis_index(axis), step), 2) == 0
-    mine, got = across(mine_ref, 0), across(got_ref, 0)
-    left, right = jnp.where(on_left, mine, got), jnp.where(on_left, got, mine)
-    t_next, vs_next = right[0:1], right[1:2]
-    q, d, tie, p, vs, t_in = (left[i : i + 1] for i in range(2, 8))
-    t = -q / (d + vs_next)
-    d_in, d_out = t_in - t, t - t_next
-    i2 = -q * t
-    i3 = t * (tie * t - 2.0 * p) + vs * d_in * d_in + vs_next * d_out * d_out
+        for ref in (pair_ref, plain_ref, seam_ref):
+            ref[pl.ds(k * 8, 8), :] = strip[:8]
+        pair_ref[pl.ds(base + k * 8, 8), :] = jnp.where(even_y, lasts, firsts)
+        seam_ref[pl.ds(base + k * 8, 8), :] = jnp.where(even_y, firsts, lasts)
+    for ref in (pair_ref, plain_ref, seam_ref):
+        ref[pl.ds(parts * 8, 8), :] = fresh[PICKED:]
+    pair_ref[pl.ds(base + parts * 8, 8), :] = jnp.where(even_y, res_ref[8:, :], res_ref[:8, :])
+    seam_ref[pl.ds(base + parts * 8, 8), :] = jnp.where(even_y, res_ref[:8, :], res_ref[8:, :])
+
+
+def across(ref, start, parts):
+    return jnp.concatenate([ref[pl.ds(start + 8 * k, 8), :] for k in range(parts)], 1)
+
+
+def merge_kernel(scen, parts, axis, step, radix, *refs):
+    in_refs, held_refs, out_refs = refs[:radix], refs[radix:-2], refs[-2:]
+    if not held_refs:
+        in_refs, out_refs = refs[:radix], refs[radix:]
+    cols = in_refs[0].shape[1]
+    at = lax.rem(lax.div(lax.axis_index(axis), step), radix)
+    given = [across(ref, 0, parts) for ref in in_refs]
+    blocks = []
+    for j in range(radix):
+        block = given[0]
+        for k in range(1, radix):
+            block = jnp.where(jnp.bitwise_xor(at, k) == j, given[k], block)
+        blocks.append(block)
+    i2 = i3 = 0.0
+    for left, right in zip(blocks, blocks[1:]):
+        t_next, vs_next = right[0:1], right[1:2]
+        q, d, tie, p, vs, t_in = (left[i : i + 1] for i in range(2, 8))
+        t = -q / (d + vs_next)
+        d_in, d_out = t_in - t, t - t_next
+        i2 = i2 - q * t
+        i3 = i3 + t * (tie * t - 2.0 * p) + vs * d_in * d_in + vs_next * d_out * d_out
     both = jnp.concatenate([i2, i3], 0)
     both = sum(both[:, k * cols : (k + 1) * cols] for k in range(parts))
     shift = scen
@@ -391,18 +402,21 @@
         both = both + pltpu.roll(both, shift, 1)
         shift *= 2
     group = lax.div(lax.broadcasted_iota(jnp.int32, (8, cols), 1), scen)
-    add = jnp.where(group == 3, both[0:1], jnp.where(group == 4, both[1:2], 0.0))
-    sums = mine_ref[parts * 16 + 8 :, :] + got_ref[parts * 16 + 8 :, :] + add
-    if out_ref.shape[0] == 8:
-        out_ref[...] = sums
-    else:
-        row = lax.broadcasted_iota(jnp.int32, (8, cols), 0)
+    sums = jnp.where(group == 3, both[0:1], jnp.where(group == 4, both[1:2], 0.0))
+    sum_at = pl.ds(parts * 8, 8)
+    for ref in in_refs:
+        sums = sums + ref[sum_at, :]
+    if not held_refs:
+        out_refs[0][...] = sums
+        return
+    row = lax.broadcasted_iota(jnp.int32, (8, cols), 0)
+    for ref in out_refs:
         for k in range(parts):
-            at = slice(k * cols, (k + 1) * cols)
-            out_ref[pl.ds(k * 16, 8), :] = jnp.where(row < 2, left[:, at], right[:, at])
-            out_ref[pl.ds(k * 16 + 8, 8), :] = other_ref[pl.ds(k * 8, 8), :]
-        out_ref[pl.ds(parts * 16, 8), :] = other_ref[pl.ds(parts * 8, 8), :]
-        out_ref[parts * 16 + 8 :, :] = sums
+            where = slice(k * cols, (k + 1) * cols)
+            ref[pl.ds(k * 8, 8), :] = jnp.where(row < 2, blocks[0][:, where], blocks[-1][:, where])
+        ref[sum_at, :] = sums
+    base = parts * 8 + 8
+    out_refs[1][base:, :] = held_refs[0][base:, :]
 
 
 def row_kernel(
@@ -504,26 +518,26 @@
         gt_ref[pl.ds(m, scen, stride=rows), :] = gain * st_s[at, :]
 
 
-def col_kernel(scen, fl_ref, fl_last_ref, cr_ref, own_ref, *rest):
+def col_kernel(scen, steps, fl_ref, fl_last_ref, cr_ref, own_ref, *rest):
     *got_refs, source_ref, start_ref, gl_ref, bc_ref, out_s = rest
     rows, cols = cr_ref.shape
+    parts = rows * scen // cols
+    base = parts * 8 + 8
     at, first, last = place("gy")
     kind = first.astype(jnp.int32) + 2 * last.astype(jnp.int32)
     odd = lax.rem(at, 2) == 1
-    res_at = pl.ds(own_ref.shape[0] - 16, 8)
 
     def contents(ref):
-        return across(ref, 0), across(ref, 8), ref[res_at, :]
+        return across(ref, 0, parts), across(ref, base, parts), ref[pl.ds(base + parts * 8, 8), :]
 
     paired = contents(got_refs[0])
     met = tuple(jnp.zeros_like(x) for x in paired)
-    for k, ref in enumerate(got_refs[1:], 1):
-        span = lax.rem(at, 2 << k)
-        here = jnp.logical_or(span == (1 << k) - 1, span == 1 << k)
+    for mask, ref in zip(steps[1:], got_refs[1:]):
+        here = jnp.abs(jnp.bitwise_xor(at, mask) - at) == 1
         met = tuple(jnp.where(here, x, y) for x, y in zip(contents(ref), met))
     sums_before, before, res_before = (jnp.where(odd, x, y) for x, y in zip(paired, met))
     sums_after, after, res_after = (jnp.where(odd, y, x) for x, y in zip(paired, met))
-    own = across(own_ref, 0)
+    own = across(own_ref, 0, parts)
 
     def seam(left, right):
         q, d, _, _, vs, t_in = (left[i : i + 1] for i in range(2, 8))
@@ -569,11 +583,10 @@
     bc_ref[...] = dot_nn(cr_ref[...], start[:cols]) + edge[:rows]
 
 
-def final_kernel(
-    scen, rows, a_ref, b_ref, v_ref, t_ref, gv_ref, gt_ref, gl_ref, br_ref, bc_ref, up_ref, row_ref, col_ref
-):
+def final_kernel(scen, rows, v_ref, t_ref, gv_ref, gt_ref, gl_ref, br_ref, bc_ref, *rest):
+    *sum_refs, up_ref, row_ref, col_ref = rest
     cols = v_ref.shape[1]
-    sums = a_ref[...] + b_ref[...]
+    sums = sum(ref[...] for ref in sum_refs)
     g0, g1, g2, g3 = (pltpu.roll(sums, cols - (k + 1) * scen, 1) for k in range(4))
     alpha = g0 / g1
     rz = alpha * alpha * g2 - g0
@@ -664,9 +677,10 @@
     )
     x_a, x_b, acc = lax.optimization_barrier((x_a, x_b, acc))
 
-    msg, other, fl_last = call(
+    plain_shape, full_shape = f32(parts * 8 + 8, cols), f32(parts * 16 + 16, cols)
+    pair, plain, seam, fl_last = call(
         functools.partial(join_kernel, scen),
-        (f32(parts * 16 + 16, cols), f32(parts * 8 + 8, cols), f32(scen, cols)),
+        (full_shape, plain_shape, full_shape, f32(scen, cols)),
         [vmem(cols, cols)],
         10**6,
         lf, h, via, acc, edge, low, strip, res, x_a, x_b, pick,
@@ -682,34 +696,43 @@
         lf, h, via, row_residual, x_a, x_b,
     )
 
-    first_msg, received = msg, []
+    own, masks, received = pair, [], []
     step, count = 1, lax.axis_size("gy")
     while step < count:
-        got = swap(msg, "gy", 2 * step - 1)
-        received.append(got)
-        if 2 * step >= count:
-            got, br = lax.optimization_barrier((got, br))
-        out = f32(*msg.shape) if 2 * step < count else f32(8, cols)
-        msg = call(functools.partial(merge_kernel, scen, "gy", step), out, [], 10**5, msg, got, other)
-        step *= 2
-    sums = msg
+        radix = 4 if 4 * step <= count else 2
+        got = []
+        for k in range(1, radix):
+            mask = k * step + step - 1
+            whole = k % 2 == 1
+            got.append(swap((pair if mask == 1 else seam) if whole else plain, "gy", mask))
+            if whole:
+                masks.append(mask)
+                received.append(got[-1])
+        if step * radix == count:
+            *got, br = lax.optimization_barrier((*got, br))
+        merge = functools.partial(merge_kernel, scen, parts, "gy", step, radix)
+        if step * radix < count:
+            plain, seam = call(merge, (plain_shape, full_shape), [], 10**5, plain, *got, seam)
+        else:
+            sums = call(merge, f32(8, cols), [], 10**5, plain, *got)
+        step *= radix
 
     gl, bc = call(
-        functools.partial(col_kernel, scen),
+        functools.partial(col_kernel, scen, masks),
         (field, grid),
         [vmem(size, cols)],
         10**7,
-        fl, fl_last, col_residual, first_msg, *received, source, start,
-    )
-
-    step = lax.axis_size("gx") // 2
-    while step > 1:
-        got = swap(sums, "gx", step)
-        if 2 * step == lax.axis_size("gx"):
-            got, bc = lax.optimization_barrier((got, bc))
-        sums = sums + got
-        step //= 2
-    rest = swap(sums, "gx", 1)
+        fl, fl_last, col_residual, own, *received, source, start,
+    )
+
+    step, others = 1, []
+    while step < lax.axis_size("gx"):
+        radix = 4 if 4 * step <= lax.axis_size("gx") else 2
+        sums = sum(others, sums)
+        others = [swap(sums, "gx", step * k) for k in range(1, radix)]
+        if step == 1:
+            *others, bc = lax.optimization_barrier((*others, bc))
+        step *= radix
 
     shape = f32(scen, rows, cols)
     return call(
@@ -717,7 +740,7 @@
         (shape, shape, shape),
         [],
         10**6,
-        sums, rest, v, t, gv, gt, gl, br, bc,
+        v, t, gv, gt, gl, br, bc, sums, *others,
     )
 
 

time: 25.5 us -> 23.1 us (0.906)
  the two profiles are of different devices: /device:TPU:0 before, /device:TPU:1 now
where the time goes in v4:
time: 23.1 us; the launch traced here: 22.9 us
  starting transfers between devices  11.9 us (52%)
  Pallas kernels  6.72 us (29%)
  waiting for transfers between devices  3.52 us (15%)
  between operations  0.76 us (3%)
    ppermute x6, starting transfers between devices, swap(): return lax.ppermute(block, axis, [(i, i ^ mask) for i in range(count)])  7.29 us
    pallas_call x7, Pallas kernels, call(): pl.pallas_call(kernel, out_shape=out, in_specs=[pl.BlockSpec(memory_space...  6.72 us
    ppermute x1, starting transfers between devices, exchange(): second = lax.ppermute(odd_side, axis, pairs(1))  4.47 us
    ppermute x6, waiting for transfers between devices, swap(): return lax.ppermute(block, axis, [(i, i ^ mask) for i in range(count)])  2.32 us
    ppermute x1, waiting for transfers between devices, exchange(): second = lax.ppermute(odd_side, axis, pairs(1))  1.2 us
  transfers between devices with their start and end apart: 8, of which 3 were waited for; matrix products, arithmetic and copies ran while one was open for 0% of the time, Pallas kernels for 17%

profile of v4, /device:TPU:1, one launch (start us, length us, event | category | flops | bytes accessed | tf_op | source)
XLA Modules:
  0.0 22.9 jit_solution(14573434926066517262)
XLA Ops:
  0.6 0.0 copy-start.2
  0.6 0.0 copy-start.3
  0.7 0.0 copy-start.5
  0.7 0.0 copy-start.6
  0.7 1.1 %shard_map.130 = (f32[512,128]{1,0:T(8,128)S(1)}, f32[32,128]{1,0:T(8,128)S(1)}, f32[32,128]{1,0:T(8,128)S(1)}, f32[184,128]{1,0:T(8,128)S(1)}, f32[184,128]{1,0:T(8,128)S(1)}) custom-call(bf16[16,32,128]{2,1,0:T(8,128)(2,1)} %refs_0_.1, f32[32,128]{1,0:T(8,128)} %refs_1_.1, f32[32,128]{1,0:T(8,128)} %refs_2_.1, s32[32,128]{1,0:T(8,128)} %refs_3_.1, ...), custom_call_target="tpu_custom_call" | custom-call | flops 100000 | tf_op jit(solution)/shard_map/pallas_call | solution.py:631
  1.8 0.1 collective-permute-start
  1.9 4.5 %collective-permute-start.1 = (f32[184,128]{1,0:T(8,128)S(1)}, f32[184,128]{1,0:T(8,128)S(1)}, u32[]{:S(2)}, u32[]{:S(2)}) collective-permute-start(f32[184,128]{1,0:T(8,128)S(1)} %get-tuple-element.40), channel_id=1, source_target_pairs={{4,8},{8,4},{5,9},{9,5},{6,10},{10,6},{7,11},{11,7},{20,24},{24,20... | collective-permute-start | bytes 282632 | tf_op jit(solution)/shard_map/ppermute | solution.py:626
  6.4 0.0 copy-done.2
  6.4 0.0 copy-done.3
  6.4 0.0 copy-done.5
  6.4 0.0 copy-done.6
  6.4 1.0 %shard_map.131 = (f32[512,128]{1,0:T(8,128)S(1)}, f32[64,128]{1,0:T(8,128)S(1)}, f32[160,128]{1,0:T(8,128)S(1)}, f32[8,128]{1,0:T(8,128)S(1)}, f32[96,128]{1,0:T(8,128)S(1)}, /*index=5*/f32[16,128]{1,0:T(8,128)S(1)}) custom-call(f32[512,128]{1,0:T(8,128)S(1)} %get-tuple-element.36.lf_ref, f32[32,128]{1,0:T(8,128)S(1)} %get-tuple-element.37.h_ref, ...), custom_call_target="tpu_custom_call" | custom-call | flops 10000000 | tf_op jit(solution)/shard_map/pallas_call | solution.py:631
  7.4 0.0 collective-permute-done.a_ref
  7.4 1.2 %collective-permute-done.1.b_ref = f32[184,128]{1,0:T(8,128)S(1)} collective-permute-done((f32[184,128]{1,0:T(8,128)S(1)}, f32[184,128]{1,0:T(8,128)S(1)}, u32[]{:S(2)}, u32[]{:S(2)}) %collective-permute-start.1) | collective-permute-done | bytes 94240 | tf_op jit(solution)/shard_map/ppermute | solution.py:626
  8.6 0.0 copy-start.4
  8.6 0.3 %shard_map.133 = (f32[80,128]{1,0:T(8,128)S(1)}, f32[40,128]{1,0:T(8,128)S(1)}, f32[80,128]{1,0:T(8,128)S(1)}, f32[16,128]{1,0:T(8,128)S(1)}) custom-call(f32[512,128]{1,0:T(8,128)S(1)} %get-tuple-element.36.lf_ref, f32[32,128]{1,0:T(8,128)S(1)} %get-tuple-element.37.h_ref, f32[32,128]{1,0:T(8,128)S(1)} %get-tuple-element.38.via_ref, ...), custom_call_target="tpu_custom_call" | custom-call | flops 1000000 | tf_op jit(solution)/shard_map/pallas_call | solution.py:631
  9.0 4.0 %collective-permute-start.3 = (f32[80,128]{1,0:T(8,128)S(1)}, f32[80,128]{1,0:T(8,128)S(1)}, u32[]{:S(2)}, u32[]{:S(2)}) collective-permute-start(f32[80,128]{1,0:T(8,128)S(1)} %get-tuple-element.56), channel_id=1, source_target_pairs={{0,3},{1,2},{2,1},{3,0},{4,7},{5,6},{6,5},{7,4},{8,11},{9,10},{10,... | collective-permute-start | bytes 122888 | tf_op jit(solution)/shard_map/ppermute | solution.py:617
  12.9 0.0 collective-permute-start.2
  12.9 0.0 copy-start
  12.9 0.0 copy-start.1
  12.9 0.3 %collective-permute-start.4 = (f32[40,128]{1,0:T(8,128)S(1)}, f32[40,128]{1,0:T(8,128)S(1)}, u32[]{:S(2)}, u32[]{:S(2)}) collective-permute-start(f32[40,128]{1,0:T(8,128)S(1)} %get-tuple-element.58.refs_0_), channel_id=1, source_target_pairs={{0,2},{1,3},{2,0},{3,1},{4,6},{5,7},{6,4},{7,5},{8,10},{9,11},{10,... | collective-permute-start | bytes 61448 | tf_op jit(solution)/shard_map/ppermute | solution.py:617
  13.3 0.0 copy-done.4
  13.3 2.0 %shard_map.132 = (f32[512,128]{1,0:T(8,128)S(1)}, f32[512,128]{1,0:T(8,128)S(1)}, f32[512,128]{1,0:T(8,128)S(1)}, f32[512,128]{1,0:T(8,128)S(1)}, f32[32,128]{1,0:T(8,128)S(1)}) custom-call(f32[512,128]{1,0:T(8,128)S(1)} %get-tuple-element.36.lf_ref, f32[32,128]{1,0:T(8,128)S(1)} %get-tuple-element.37.h_ref, f32[32,128]{1,0:T(8,128)S(1)} %get-tuple-element.38.via_ref, ...), custom_call_target="tpu_custom_call" | custom-call | flops 10000000 | tf_op jit(solution)/shard_map/pallas_call | solution.py:631
  15.3 1.2 %collective-permute-done.4.refs_2_ = f32[40,128]{1,0:T(8,128)S(1)} collective-permute-done((f32[40,128]{1,0:T(8,128)S(1)}, f32[40,128]{1,0:T(8,128)S(1)}, u32[]{:S(2)}, u32[]{:S(2)}) %collective-permute-start.4) | collective-permute-done | bytes 20512 | tf_op jit(solution)/shard_map/ppermute | solution.py:617
  16.5 0.0 collective-permute-done.3.rest_1_.refs_3_
  16.5 0.0 collective-permute-done.2.rest_0_.refs_1_
  16.5 0.3 %shard_map.135.rest_0_ = f32[8,128]{1,0:T(8,128)S(1)} custom-call(f32[40,128]{1,0:T(8,128)S(1)} %get-tuple-element.58.refs_0_, f32[80,128]{1,0:T(8,128)S(1)} %collective-permute-done.2.rest_0_.refs_1_, f32[40,128]{1,0:T(8,128)S(1)} %collective-permute-done.4.refs_2_, f32[80,128]{1,0:T(8,128)S(1)} %collective-permute-done.3.rest_1_.refs_3_), custom_call_target="tpu_custom_call" | custom-call | flops 100000 | tf_op jit(solution)/shard_map/pallas_call | solution.py:631
  16.8 2.6 %collective-permute-start.7 = (f32[8,128]{1,0:T(8,128)S(1)}, f32[8,128]{1,0:T(8,128)S(1)}, u32[]{:S(2)}, u32[]{:S(2)}) collective-permute-start(f32[8,128]{1,0:T(8,128)S(1)} %shard_map.135.rest_0_), channel_id=1, source_target_pairs={{0,12},{4,8},{8,4},{12,0},{1,13},{5,9},{9,5},{13,1},{2,14},{6,10},... | collective-permute-start | bytes 12296 | tf_op jit(solution)/shard_map/ppermute | solution.py:617
  19.3 0.0 collective-permute-start.6
  19.3 0.4 %collective-permute-start.5 = (f32[8,128]{1,0:T(8,128)S(1)}, f32[8,128]{1,0:T(8,128)S(1)}, u32[]{:S(2)}, u32[]{:S(2)}) collective-permute-start(f32[8,128]{1,0:T(8,128)S(1)} %shard_map.135.rest_0_), channel_id=1, source_target_pairs={{0,4},{4,0},{8,12},{12,8},{1,5},{5,1},{9,13},{13,9},{2,6},{6,2},{1... | collective-permute-start | bytes 12296 | tf_op jit(solution)/shard_map/ppermute | solution.py:617
  19.7 0.0 copy-done
  19.7 0.0 copy-done.1
  19.8 0.9 %shard_map.134 = (f32[512,128]{1,0:T(8,128)S(1)}, f32[32,128]{1,0:T(8,128)S(1)}) custom-call(f32[512,128]{1,0:T(8,128)S(1)} %get-tuple-element.48.fl_ref, f32[16,128]{1,0:T(8,128)S(1)} %get-tuple-element.54.fl_last_ref, f32[32,128]{1,0:T(8,128)S(1)} %copy-done.3, f32[80,128]{1,0:T(8,128)S(1)} %get-tuple-element.55.own_ref, ...), custom_call_target="tpu_custom_call" | custom-call | flops 10000000 | tf_op jit(solution)/shard_map/pallas_call | solution.py:631
  20.6 0.0 collective-permute-done.7.rest_3_
  20.6 1.1 %collective-permute-done.6.rest_2_ = f32[8,128]{1,0:T(8,128)S(1)} collective-permute-done((f32[8,128]{1,0:T(8,128)S(1)}, f32[8,128]{1,0:T(8,128)S(1)}, u32[]{:S(2)}, u32[]{:S(2)}) %collective-permute-start.6) | collective-permute-done | bytes 4128 | tf_op jit(solution)/shard_map/ppermute | solution.py:617
  21.8 0.0 collective-permute-done.5.rest_1_
  21.8 1.1 %shard_map.136 = (f32[16,32,128]{2,1,0:T(8,128)}, f32[16,32,128]{2,1,0:T(8,128)}, f32[16,32,128]{2,1,0:T(8,128)}) custom-call(f32[512,128]{1,0:T(8,128)S(1)} %get-tuple-element.44.v_ref, f32[512,128]{1,0:T(8,128)S(1)} %get-tuple-element.45.t_ref, f32[512,128]{1,0:T(8,128)S(1)} %get-tuple-element.46.gv_ref, f32[512,128]{1,0:T(8,128)S(1)} %get-tuple-element.47.gt_ref, ...), custom_call_target="tpu_custom_call" | custom-call | flops 1000000 | tf_op jit(solution)/shard_map/pallas_call | solution.py:631
Async XLA Ops:
  0.6 5.8 %copy-start.2 = (f32[48,128]{1,0:T(8,128)S(1)}, f32[48,128]{1,0:T(8,128)}, u32[]{:S(2)}) copy-start(f32[48,128]{1,0:T(8,128)} %constant.6.clone.pick_ref) | copy-start | bytes 73732
  0.6 5.8 %copy-start.3 = (f32[32,128]{1,0:T(8,128)S(1)}, f32[32,128]{1,0:T(8,128)}, u32[]{:S(2)}) copy-start(f32[32,128]{1,0:T(8,128)} %cr_ref.3) | copy-start | bytes 49156
  0.7 5.8 %copy-start.5 = (f32[32,128]{1,0:T(8,128)S(1)}, f32[32,128]{1,0:T(8,128)}, u32[]{:S(2)}) copy-start(f32[32,128]{1,0:T(8,128)} %cc_ref.1) | copy-start | bytes 49156
  0.7 5.8 %copy-start.6 = (s32[32,128]{1,0:T(8,128)S(1)}, s32[32,128]{1,0:T(8,128)}, u32[]{:S(2)}) copy-start(s32[32,128]{1,0:T(8,128)} %pm_ref.1) | copy-start | bytes 49156
  1.8 5.6 %collective-permute-start = (f32[184,128]{1,0:T(8,128)S(1)}, f32[184,128]{1,0:T(8,128)S(1)}, u32[]{:S(2)}, u32[]{:S(2)}) collective-permute-start(f32[184,128]{1,0:T(8,128)S(1)} %get-tuple-element.39), channel_id=1, source_target_pairs={{0,4},{4,0},{8,12},{12,8},{1,5},{5,1},{9,13},{13,9},{2,6},{6,2},{1... | collective-permute-start | bytes 282632 | tf_op jit(solution)/shard_map/ppermute | solution.py:627
  1.9 6.7 %collective-permute-start.1 = (f32[184,128]{1,0:T(8,128)S(1)}, f32[184,128]{1,0:T(8,128)S(1)}, u32[]{:S(2)}, u32[]{:S(2)}) collective-permute-start(f32[184,128]{1,0:T(8,128)S(1)} %get-tuple-element.40), channel_id=1, source_target_pairs={{4,8},{8,4},{5,9},{9,5},{6,10},{10,6},{7,11},{11,7},{20,24},{24,20... | collective-permute-start | bytes 282632 | tf_op jit(solution)/shard_map/ppermute | solution.py:626
  8.6 4.7 %copy-start.4 = (f32[32,128]{1,0:T(8,128)S(1)}, f32[32,128]{1,0:T(8,128)}, u32[]{:S(2)}) copy-start(f32[32,128]{1,0:T(8,128)} %rr_ref.1) | copy-start | bytes 49156
  9.0 7.5 %collective-permute-start.3 = (f32[80,128]{1,0:T(8,128)S(1)}, f32[80,128]{1,0:T(8,128)S(1)}, u32[]{:S(2)}, u32[]{:S(2)}) collective-permute-start(f32[80,128]{1,0:T(8,128)S(1)} %get-tuple-element.56), channel_id=1, source_target_pairs={{0,3},{1,2},{2,1},{3,0},{4,7},{5,6},{6,5},{7,4},{8,11},{9,10},{10,... | collective-permute-start | bytes 122888 | tf_op jit(solution)/shard_map/ppermute | solution.py:617
  12.9 3.5 %collective-permute-start.2 = (f32[80,128]{1,0:T(8,128)S(1)}, f32[80,128]{1,0:T(8,128)S(1)}, u32[]{:S(2)}, u32[]{:S(2)}) collective-permute-start(f32[80,128]{1,0:T(8,128)S(1)} %get-tuple-element.55.own_ref), channel_id=1, source_target_pairs={{0,1},{1,0},{2,3},{3,2},{4,5},{5,4},{6,7},{7,6},{8,9},{9,8},{10,11... | collective-permute-start | bytes 122888 | tf_op jit(solution)/shard_map/ppermute | solution.py:617
  12.9 6.8 %copy-start = (f32[4,152,128]{2,1,0:T(8,128)S(1)}, f32[4,152,128]{2,1,0:T(8,128)}, u32[]{:S(2)}) copy-start(f32[4,152,128]{2,1,0:T(8,128)} %constant.7.clone.rest_2_) | copy-start | bytes 933892
  12.9 6.8 %copy-start.1 = (f32[4,144,128]{2,1,0:T(8,128)S(1)}, f32[4,144,128]{2,1,0:T(8,128)}, u32[]{:S(2)}) copy-start(f32[4,144,128]{2,1,0:T(8,128)} %constant.8.clone.rest_3_) | copy-start | bytes 884740
  12.9 3.5 %collective-permute-start.4 = (f32[40,128]{1,0:T(8,128)S(1)}, f32[40,128]{1,0:T(8,128)S(1)}, u32[]{:S(2)}, u32[]{:S(2)}) collective-permute-start(f32[40,128]{1,0:T(8,128)S(1)} %get-tuple-element.58.refs_0_), channel_id=1, source_target_pairs={{0,2},{1,3},{2,0},{3,1},{4,6},{5,7},{6,4},{7,5},{8,10},{9,11},{10,... | collective-permute-start | bytes 61448 | tf_op jit(solution)/shard_map/ppermute | solution.py:617
  16.8 3.9 %collective-permute-start.7 = (f32[8,128]{1,0:T(8,128)S(1)}, f32[8,128]{1,0:T(8,128)S(1)}, u32[]{:S(2)}, u32[]{:S(2)}) collective-permute-start(f32[8,128]{1,0:T(8,128)S(1)} %shard_map.135.rest_0_), channel_id=1, source_target_pairs={{0,12},{4,8},{8,4},{12,0},{1,13},{5,9},{9,5},{13,1},{2,14},{6,10},... | collective-permute-start | bytes 12296 | tf_op jit(solution)/shard_map/ppermute | solution.py:617
  19.3 2.5 %collective-permute-start.6 = (f32[8,128]{1,0:T(8,128)S(1)}, f32[8,128]{1,0:T(8,128)S(1)}, u32[]{:S(2)}, u32[]{:S(2)}) collective-permute-start(f32[8,128]{1,0:T(8,128)S(1)} %shard_map.135.rest_0_), channel_id=1, source_target_pairs={{0,8},{4,12},{8,0},{12,4},{1,9},{5,13},{9,1},{13,5},{2,10},{6,14},... | collective-permute-start | bytes 12296 | tf_op jit(solution)/shard_map/ppermute | solution.py:617
  19.3 2.5 %collective-permute-start.5 = (f32[8,128]{1,0:T(8,128)S(1)}, f32[8,128]{1,0:T(8,128)S(1)}, u32[]{:S(2)}, u32[]{:S(2)}) collective-permute-start(f32[8,128]{1,0:T(8,128)S(1)} %shard_map.135.rest_0_), channel_id=1, source_target_pairs={{0,4},{4,0},{8,12},{12,8},{1,5},{5,1},{9,13},{13,9},{2,6},{6,2},{1... | collective-permute-start | bytes 12296 | tf_op jit(solution)/shard_map/ppermute | solution.py:617

commit v5 on v4

--- a/solution.py
+++ b/solution.py
@@ -93,12 +93,15 @@
     return at, at == 0, at == count - 1
 
 
-def pick_side(odd, even_ref, odd_ref):
+def sides(axis, even_ref, odd_ref):
+    at, first, last = place(axis)
+    odd = lax.rem(at, 2) == 1
+
     def before(*where):
-        return jnp.where(odd, even_ref[where], odd_ref[where])
+        return jnp.where(odd, even_ref[where], jnp.where(first, 0.0, odd_ref[where]))
 
     def after(*where):
-        return jnp.where(odd, odd_ref[where], even_ref[where])
+        return jnp.where(odd, jnp.where(last, 0.0, odd_ref[where]), even_ref[where])
 
     return before, after
 
@@ -275,9 +278,8 @@
     w_s,
 ):
     rows, cols = h_ref.shape
-    odd_x = lax.rem(lax.axis_index("gx"), 2) == 1
     even_y = lax.rem(lax.axis_index("gy"), 2) == 0
-    before, after = pick_side(odd_x, a_ref, b_ref)
+    before, after = sides("gx", a_ref, b_ref)
     n = HALO * scen
     last = rows - 1
 
@@ -425,8 +427,8 @@
     inv_s, h_s, tie_s, fv_s, ft_s, sv_s, st_s, s0_s,
 ):
     rows, cols = h_ref.shape
-    at_x, first, last = place("gx")
-    before, after = pick_side(lax.rem(at_x, 2) == 1, a_ref, b_ref)
+    _, first, last = place("gx")
+    before, after = sides("gx", a_ref, b_ref)
     n = HALO * scen
     at = pl.ds(n, SLOT)
     h = jnp.concatenate([before(at), h_ref[...], after(at)], 0)
@@ -621,7 +623,7 @@
     count = lax.axis_size(axis)
 
     def pairs(start):
-        return [(i + a, i + 1 - a) for i in range(start, count - 1, 2) for a in (0, 1)]
+        return [((i + a) % count, (i + 1 - a) % count) for i in range(start, count, 2) for a in (0, 1)]
 
     second = lax.ppermute(odd_side, axis, pairs(1))
     return lax.ppermute(even_side, axis, pairs(0)), second

time: 23.1 us -> 21.9 us (0.948)
  the two profiles are of different devices: /device:TPU:1 before, /device:TPU:0 now
where the time goes in v5:
time: 21.9 us; the launch traced here: 21.7 us
  starting transfers between devices  9.4 us (43%)
  Pallas kernels  6.71 us (31%)
  waiting for transfers between devices  4.82 us (22%)
  between operations  0.72 us (3%)
    pallas_call x7, Pallas kernels, call(): pl.pallas_call(kernel, out_shape=out, in_specs=[pl.BlockSpec(memory_space...  6.71 us
    ppermute x6, starting transfers between devices, swap(): return lax.ppermute(block, axis, [(i, i ^ mask) for i in range(count)])  6.27 us
    ppermute x6, waiting for transfers between devices, swap(): return lax.ppermute(block, axis, [(i, i ^ mask) for i in range(count)])  2.85 us
    ppermute x1, starting transfers between devices, exchange(): second = lax.ppermute(odd_side, axis, pairs(1))  2.61 us
    ppermute x1, waiting for transfers between devices, exchange(): second = lax.ppermute(odd_side, axis, pairs(1))  1.97 us
    ppermute x1, starting transfers between devices, exchange(): return (lax.ppermute(even_side, axis, pairs(0)), second)  0.52 us
  transfers between devices with their start and end apart: 8, of which 4 were waited for; matrix products, arithmetic and copies ran while one was open for 0% of the time, Pallas kernels for 18%

profile of v5, /device:TPU:0, one launch (start us, length us, event | category | flops | bytes accessed | tf_op | source)
XLA Modules:
  0.0 21.7 jit_solution(18041922566815281201)
XLA Ops:
  0.6 0.0 copy-start.2
  0.6 0.0 copy-start.3
  0.7 0.0 copy-start.5
  0.7 0.0 copy-start.6
  0.7 1.1 %shard_map.130 = (f32[512,128]{1,0:T(8,128)S(1)}, f32[32,128]{1,0:T(8,128)S(1)}, f32[32,128]{1,0:T(8,128)S(1)}, f32[184,128]{1,0:T(8,128)S(1)}, f32[184,128]{1,0:T(8,128)S(1)}) custom-call(bf16[16,32,128]{2,1,0:T(8,128)(2,1)} %refs_0_.1, f32[32,128]{1,0:T(8,128)} %refs_1_.1, f32[32,128]{1,0:T(8,128)} %refs_2_.1, s32[32,128]{1,0:T(8,128)} %refs_3_.1, ...), custom_call_target="tpu_custom_call" | custom-call | flops 100000 | tf_op jit(solution)/shard_map/pallas_call | solution.py:633
  1.8 0.5 %collective-permute-start = (f32[184,128]{1,0:T(8,128)S(1)}, f32[184,128]{1,0:T(8,128)S(1)}, u32[]{:S(2)}, u32[]{:S(2)}) collective-permute-start(f32[184,128]{1,0:T(8,128)S(1)} %get-tuple-element.39), channel_id=1, source_target_pairs={{0,4},{4,0},{8,12},{12,8},{1,5},{5,1},{9,13},{13,9},{2,6},{6,2},{1... | collective-permute-start | bytes 282632 | tf_op jit(solution)/shard_map/ppermute | solution.py:629
  2.3 2.6 %collective-permute-start.1 = (f32[184,128]{1,0:T(8,128)S(1)}, f32[184,128]{1,0:T(8,128)S(1)}, u32[]{:S(2)}, u32[]{:S(2)}) collective-permute-start(f32[184,128]{1,0:T(8,128)S(1)} %get-tuple-element.40), channel_id=1, source_target_pairs={{4,8},{8,4},{12,0},{0,12},{5,9},{9,5},{13,1},{1,13},{6,10},{10,6},... | collective-permute-start | bytes 282632 | tf_op jit(solution)/shard_map/ppermute | solution.py:628
  4.9 0.0 copy-done.2
  4.9 0.0 copy-done.3
  4.9 0.0 copy-done.5
  4.9 0.0 copy-done.6
  4.9 1.0 %shard_map.131 = (f32[512,128]{1,0:T(8,128)S(1)}, f32[64,128]{1,0:T(8,128)S(1)}, f32[160,128]{1,0:T(8,128)S(1)}, f32[8,128]{1,0:T(8,128)S(1)}, f32[96,128]{1,0:T(8,128)S(1)}, /*index=5*/f32[16,128]{1,0:T(8,128)S(1)}) custom-call(f32[512,128]{1,0:T(8,128)S(1)} %get-tuple-element.36.lf_ref, f32[32,128]{1,0:T(8,128)S(1)} %get-tuple-element.37.h_ref, ...), custom_call_target="tpu_custom_call" | custom-call | flops 10000000 | tf_op jit(solution)/shard_map/pallas_call | solution.py:633
  5.9 0.0 collective-permute-done.a_ref
  5.9 2.0 %collective-permute-done.1.b_ref = f32[184,128]{1,0:T(8,128)S(1)} collective-permute-done((f32[184,128]{1,0:T(8,128)S(1)}, f32[184,128]{1,0:T(8,128)S(1)}, u32[]{:S(2)}, u32[]{:S(2)}) %collective-permute-start.1) | collective-permute-done | bytes 94240 | tf_op jit(solution)/shard_map/ppermute | solution.py:628
  7.9 0.0 copy-start.4
  7.9 0.3 %shard_map.133 = (f32[80,128]{1,0:T(8,128)S(1)}, f32[40,128]{1,0:T(8,128)S(1)}, f32[80,128]{1,0:T(8,128)S(1)}, f32[16,128]{1,0:T(8,128)S(1)}) custom-call(f32[512,128]{1,0:T(8,128)S(1)} %get-tuple-element.36.lf_ref, f32[32,128]{1,0:T(8,128)S(1)} %get-tuple-element.37.h_ref, f32[32,128]{1,0:T(8,128)S(1)} %get-tuple-element.38.via_ref, ...), custom_call_target="tpu_custom_call" | custom-call | flops 1000000 | tf_op jit(solution)/shard_map/pallas_call | solution.py:633
  8.2 3.6 %collective-permute-start.3 = (f32[80,128]{1,0:T(8,128)S(1)}, f32[80,128]{1,0:T(8,128)S(1)}, u32[]{:S(2)}, u32[]{:S(2)}) collective-permute-start(f32[80,128]{1,0:T(8,128)S(1)} %get-tuple-element.56), channel_id=1, source_target_pairs={{0,3},{1,2},{2,1},{3,0},{4,7},{5,6},{6,5},{7,4},{8,11},{9,10},{10,... | collective-permute-start | bytes 122888 | tf_op jit(solution)/shard_map/ppermute | solution.py:619
  11.8 0.0 collective-permute-start.2
  11.8 0.0 copy-start
  11.8 0.0 copy-start.1
  11.8 0.8 %collective-permute-start.4 = (f32[40,128]{1,0:T(8,128)S(1)}, f32[40,128]{1,0:T(8,128)S(1)}, u32[]{:S(2)}, u32[]{:S(2)}) collective-permute-start(f32[40,128]{1,0:T(8,128)S(1)} %get-tuple-element.58.refs_0_), channel_id=1, source_target_pairs={{0,2},{1,3},{2,0},{3,1},{4,6},{5,7},{6,4},{7,5},{8,10},{9,11},{10,... | collective-permute-start | bytes 61448 | tf_op jit(solution)/shard_map/ppermute | solution.py:619
  12.7 0.0 copy-done.4
  12.7 2.0 %shard_map.132 = (f32[512,128]{1,0:T(8,128)S(1)}, f32[512,128]{1,0:T(8,128)S(1)}, f32[512,128]{1,0:T(8,128)S(1)}, f32[512,128]{1,0:T(8,128)S(1)}, f32[32,128]{1,0:T(8,128)S(1)}) custom-call(f32[512,128]{1,0:T(8,128)S(1)} %get-tuple-element.36.lf_ref, f32[32,128]{1,0:T(8,128)S(1)} %get-tuple-element.37.h_ref, f32[32,128]{1,0:T(8,128)S(1)} %get-tuple-element.38.via_ref, ...), custom_call_target="tpu_custom_call" | custom-call | flops 10000000 | tf_op jit(solution)/shard_map/pallas_call | solution.py:633
  14.7 1.8 %collective-permute-done.4.refs_2_ = f32[40,128]{1,0:T(8,128)S(1)} collective-permute-done((f32[40,128]{1,0:T(8,128)S(1)}, f32[40,128]{1,0:T(8,128)S(1)}, u32[]{:S(2)}, u32[]{:S(2)}) %collective-permute-start.4) | collective-permute-done | bytes 20512 | tf_op jit(solution)/shard_map/ppermute | solution.py:619
  16.5 0.0 collective-permute-done.3.rest_1_.refs_3_
  16.5 0.0 collective-permute-done.2.rest_0_.refs_1_
  16.5 0.3 %shard_map.135.rest_0_ = f32[8,128]{1,0:T(8,128)S(1)} custom-call(f32[40,128]{1,0:T(8,128)S(1)} %get-tuple-element.58.refs_0_, f32[80,128]{1,0:T(8,128)S(1)} %collective-permute-done.2.rest_0_.refs_1_, f32[40,128]{1,0:T(8,128)S(1)} %collective-permute-done.4.refs_2_, f32[80,128]{1,0:T(8,128)S(1)} %collective-permute-done.3.rest_1_.refs_3_), custom_call_target="tpu_custom_call" | custom-call | flops 100000 | tf_op jit(solution)/shard_map/pallas_call | solution.py:633
  16.8 0.1 collective-permute-start.7
  16.9 1.4 %collective-permute-start.6 = (f32[8,128]{1,0:T(8,128)S(1)}, f32[8,128]{1,0:T(8,128)S(1)}, u32[]{:S(2)}, u32[]{:S(2)}) collective-permute-start(f32[8,128]{1,0:T(8,128)S(1)} %shard_map.135.rest_0_), channel_id=1, source_target_pairs={{0,8},{4,12},{8,0},{12,4},{1,9},{5,13},{9,1},{13,5},{2,10},{6,14},... | collective-permute-start | bytes 12296 | tf_op jit(solution)/shard_map/ppermute | solution.py:619
  18.3 0.3 %collective-permute-start.5 = (f32[8,128]{1,0:T(8,128)S(1)}, f32[8,128]{1,0:T(8,128)S(1)}, u32[]{:S(2)}, u32[]{:S(2)}) collective-permute-start(f32[8,128]{1,0:T(8,128)S(1)} %shard_map.135.rest_0_), channel_id=1, source_target_pairs={{0,4},{4,0},{8,12},{12,8},{1,5},{5,1},{9,13},{13,9},{2,6},{6,2},{1... | collective-permute-start | bytes 12296 | tf_op jit(solution)/shard_map/ppermute | solution.py:619
  18.6 0.0 copy-done
  18.7 0.0 copy-done.1
  18.7 0.9 %shard_map.134 = (f32[512,128]{1,0:T(8,128)S(1)}, f32[32,128]{1,0:T(8,128)S(1)}) custom-call(f32[512,128]{1,0:T(8,128)S(1)} %get-tuple-element.48.fl_ref, f32[16,128]{1,0:T(8,128)S(1)} %get-tuple-element.54.fl_last_ref, f32[32,128]{1,0:T(8,128)S(1)} %copy-done.3, f32[80,128]{1,0:T(8,128)S(1)} %get-tuple-element.55.own_ref, ...), custom_call_target="tpu_custom_call" | custom-call | flops 10000000 | tf_op jit(solution)/shard_map/pallas_call | solution.py:633
  19.5 0.3 %collective-permute-done.7.rest_3_ = f32[8,128]{1,0:T(8,128)S(1)} collective-permute-done((f32[8,128]{1,0:T(8,128)S(1)}, f32[8,128]{1,0:T(8,128)S(1)}, u32[]{:S(2)}, u32[]{:S(2)}) %collective-permute-start.7) | collective-permute-done | bytes 4128 | tf_op jit(solution)/shard_map/ppermute | solution.py:619
  19.8 0.7 %collective-permute-done.6.rest_2_ = f32[8,128]{1,0:T(8,128)S(1)} collective-permute-done((f32[8,128]{1,0:T(8,128)S(1)}, f32[8,128]{1,0:T(8,128)S(1)}, u32[]{:S(2)}, u32[]{:S(2)}) %collective-permute-start.6) | collective-permute-done | bytes 4128 | tf_op jit(solution)/shard_map/ppermute | solution.py:619
  20.5 0.0 collective-permute-done.5.rest_1_
  20.5 1.1 %shard_map.136 = (f32[16,32,128]{2,1,0:T(8,128)}, f32[16,32,128]{2,1,0:T(8,128)}, f32[16,32,128]{2,1,0:T(8,128)}) custom-call(f32[512,128]{1,0:T(8,128)S(1)} %get-tuple-element.44.v_ref, f32[512,128]{1,0:T(8,128)S(1)} %get-tuple-element.45.t_ref, f32[512,128]{1,0:T(8,128)S(1)} %get-tuple-element.46.gv_ref, f32[512,128]{1,0:T(8,128)S(1)} %get-tuple-element.47.gt_ref, ...), custom_call_target="tpu_custom_call" | custom-call | flops 1000000 | tf_op jit(solution)/shard_map/pallas_call | solution.py:633
Async XLA Ops:
  0.6 4.3 %copy-start.2 = (f32[48,128]{1,0:T(8,128)S(1)}, f32[48,128]{1,0:T(8,128)}, u32[]{:S(2)}) copy-start(f32[48,128]{1,0:T(8,128)} %constant.6.clone.pick_ref) | copy-start | bytes 73732
  0.6 4.3 %copy-start.3 = (f32[32,128]{1,0:T(8,128)S(1)}, f32[32,128]{1,0:T(8,128)}, u32[]{:S(2)}) copy-start(f32[32,128]{1,0:T(8,128)} %cr_ref.3) | copy-start | bytes 49156
  0.7 4.3 %copy-start.5 = (f32[32,128]{1,0:T(8,128)S(1)}, f32[32,128]{1,0:T(8,128)}, u32[]{:S(2)}) copy-start(f32[32,128]{1,0:T(8,128)} %cc_ref.1) | copy-start | bytes 49156
  0.7 4.3 %copy-start.6 = (s32[32,128]{1,0:T(8,128)S(1)}, s32[32,128]{1,0:T(8,128)}, u32[]{:S(2)}) copy-start(s32[32,128]{1,0:T(8,128)} %pm_ref.1) | copy-start | bytes 49156
  1.8 4.1 %collective-permute-start = (f32[184,128]{1,0:T(8,128)S(1)}, f32[184,128]{1,0:T(8,128)S(1)}, u32[]{:S(2)}, u32[]{:S(2)}) collective-permute-start(f32[184,128]{1,0:T(8,128)S(1)} %get-tuple-element.39), channel_id=1, source_target_pairs={{0,4},{4,0},{8,12},{12,8},{1,5},{5,1},{9,13},{13,9},{2,6},{6,2},{1... | collective-permute-start | bytes 282632 | tf_op jit(solution)/shard_map/ppermute | solution.py:629
  2.3 5.6 %collective-permute-start.1 = (f32[184,128]{1,0:T(8,128)S(1)}, f32[184,128]{1,0:T(8,128)S(1)}, u32[]{:S(2)}, u32[]{:S(2)}) collective-permute-start(f32[184,128]{1,0:T(8,128)S(1)} %get-tuple-element.40), channel_id=1, source_target_pairs={{4,8},{8,4},{12,0},{0,12},{5,9},{9,5},{13,1},{1,13},{6,10},{10,6},... | collective-permute-start | bytes 282632 | tf_op jit(solution)/shard_map/ppermute | solution.py:628
  7.9 4.8 %copy-start.4 = (f32[32,128]{1,0:T(8,128)S(1)}, f32[32,128]{1,0:T(8,128)}, u32[]{:S(2)}) copy-start(f32[32,128]{1,0:T(8,128)} %rr_ref.1) | copy-start | bytes 49156
  8.2 8.3 %collective-permute-start.3 = (f32[80,128]{1,0:T(8,128)S(1)}, f32[80,128]{1,0:T(8,128)S(1)}, u32[]{:S(2)}, u32[]{:S(2)}) collective-permute-start(f32[80,128]{1,0:T(8,128)S(1)} %get-tuple-element.56), channel_id=1, source_target_pairs={{0,3},{1,2},{2,1},{3,0},{4,7},{5,6},{6,5},{7,4},{8,11},{9,10},{10,... | collective-permute-start | bytes 122888 | tf_op jit(solution)/shard_map/ppermute | solution.py:619
  11.8 4.7 %collective-permute-start.2 = (f32[80,128]{1,0:T(8,128)S(1)}, f32[80,128]{1,0:T(8,128)S(1)}, u32[]{:S(2)}, u32[]{:S(2)}) collective-permute-start(f32[80,128]{1,0:T(8,128)S(1)} %get-tuple-element.55.own_ref), channel_id=1, source_target_pairs={{0,1},{1,0},{2,3},{3,2},{4,5},{5,4},{6,7},{7,6},{8,9},{9,8},{10,11... | collective-permute-start | bytes 122888 | tf_op jit(solution)/shard_map/ppermute | solution.py:619
  11.8 6.8 %copy-start = (f32[4,152,128]{2,1,0:T(8,128)S(1)}, f32[4,152,128]{2,1,0:T(8,128)}, u32[]{:S(2)}) copy-start(f32[4,152,128]{2,1,0:T(8,128)} %constant.7.clone.rest_2_) | copy-start | bytes 933892
  11.8 6.8 %copy-start.1 = (f32[4,144,128]{2,1,0:T(8,128)S(1)}, f32[4,144,128]{2,1,0:T(8,128)}, u32[]{:S(2)}) copy-start(f32[4,144,128]{2,1,0:T(8,128)} %constant.8.clone.rest_3_) | copy-start | bytes 884740
  11.8 4.7 %collective-permute-start.4 = (f32[40,128]{1,0:T(8,128)S(1)}, f32[40,128]{1,0:T(8,128)S(1)}, u32[]{:S(2)}, u32[]{:S(2)}) collective-permute-start(f32[40,128]{1,0:T(8,128)S(1)} %get-tuple-element.58.refs_0_), channel_id=1, source_target_pairs={{0,2},{1,3},{2,0},{3,1},{4,6},{5,7},{6,4},{7,5},{8,10},{9,11},{10,... | collective-permute-start | bytes 61448 | tf_op jit(solution)/shard_map/ppermute | solution.py:619
  16.8 3.0 %collective-permute-start.7 = (f32[8,128]{1,0:T(8,128)S(1)}, f32[8,128]{1,0:T(8,128)S(1)}, u32[]{:S(2)}, u32[]{:S(2)}) collective-permute-start(f32[8,128]{1,0:T(8,128)S(1)} %shard_map.135.rest_0_), channel_id=1, source_target_pairs={{0,12},{4,8},{8,4},{12,0},{1,13},{5,9},{9,5},{13,1},{2,14},{6,10},... | collective-permute-start | bytes 12296 | tf_op jit(solution)/shard_map/ppermute | solution.py:619
  16.9 3.6 %collective-permute-start.6 = (f32[8,128]{1,0:T(8,128)S(1)}, f32[8,128]{1,0:T(8,128)S(1)}, u32[]{:S(2)}, u32[]{:S(2)}) collective-permute-start(f32[8,128]{1,0:T(8,128)S(1)} %shard_map.135.rest_0_), channel_id=1, source_target_pairs={{0,8},{4,12},{8,0},{12,4},{1,9},{5,13},{9,1},{13,5},{2,10},{6,14},... | collective-permute-start | bytes 12296 | tf_op jit(solution)/shard_map/ppermute | solution.py:619
  18.3 2.2 %collective-permute-start.5 = (f32[8,128]{1,0:T(8,128)S(1)}, f32[8,128]{1,0:T(8,128)S(1)}, u32[]{:S(2)}, u32[]{:S(2)}) collective-permute-start(f32[8,128]{1,0:T(8,128)S(1)} %shard_map.135.rest_0_), channel_id=1, source_target_pairs={{0,4},{4,0},{8,12},{12,8},{1,5},{5,1},{9,13},{13,9},{2,6},{6,2},{1... | collective-permute-start | bytes 12296 | tf_op jit(solution)/shard_map/ppermute | solution.py:619

commit v6 on v5

--- a/solution.py
+++ b/solution.py
@@ -18,10 +18,11 @@
 HALO = STEPS + 1
 SLOT = 16
 
-SUM_LANES = [0, 12, -1, 13, 14, 9, 15, -2]
+SUM_LANES = [-1, 0, 13, 10, 12]
 FIRST_LANES = [11, 1, 2, 3, 4, 5, 6]
-LAST_LANES = [8, -7, -6, -5, -4, -3]
+LAST_LANES = [8, -7, -6, -5, -4, -3, 9, 15]
 PICKED = 8 + 8 + 8
+USED = 6
 
 
 def dot_nt(a, b):
@@ -88,6 +89,13 @@
     return np.stack(sources).astype(np.float32), np.stack(starts).astype(np.float32)
 
 
+def taps():
+    size = 4 * STEPS + 1
+    step = np.eye(size) * (1 - 2 * RELAX) + RELAX * (np.eye(size, k=1) + np.eye(size, k=-1))
+    total = sum(np.linalg.matrix_power(step, k) for k in range(STEPS))
+    return [float(x) for x in RELAX * DRIVE * total[size // 2, size // 2 : size // 2 + STEPS]]
+
+
 def place(axis):
     at, count = lax.axis_index(axis), lax.axis_size(axis)
     return at, at == 0, at == count - 1
@@ -106,35 +114,49 @@
     return before, after
 
 
-def pack_kernel(*refs):
-    args, outs, held, sem = refs[:5], refs[5:10], refs[10:15], refs[15]
+def fetch(args, held, sem):
     copies = [pltpu.make_async_copy(src, dst, sem.at[i]) for i, (src, dst) in enumerate(zip(args, held))]
     for copy in copies:
         copy.start()
-    load_ref, rc_ref, vc_ref, vm_ref, rr_ref = held
-    lf_ref, h_ref, via_ref, a_ref, b_ref = outs
+    for copy in copies:
+        copy.wait()
+
+
+def edge_kernel(load_ref, rc_ref, vc_ref, vm_ref, rr_ref, out_ref, *scratch):
+    *held, lf_s, sem = scratch
+    scen, rows, cols = load_ref.shape
+    odd = lax.rem(lax.axis_index("gx"), 2) == 1
+    part = pl.ds(pl.multiple_of(jnp.where(odd, rows - SLOT, 0), SLOT), SLOT)
+    fetch([load_ref.at[:, part], *(ref.at[part] for ref in (rc_ref, vc_ref, vm_ref, rr_ref))], held, sem)
+    load_v, rc_v, vc_v, vm_v, rr_v = held
+    for s in range(scen):
+        lf_s[pl.ds(s, SLOT, stride=scen), :] = load_v[s].astype(F32)
+    n = HALO * scen
+    out_ref[0:n, :] = jnp.where(odd, lf_s[(SLOT - HALO) * scen :, :], lf_s[0:n, :])
+    out_ref[n : n + SLOT, :] = rc_v[...]
+    out_ref[n + SLOT : n + 2 * SLOT, :] = vm_v[...].astype(F32) * vc_v[...]
+    out_ref[n + 2 * SLOT :, :] = jnp.where(odd, rr_v[SLOT - 8 :, :], rr_v[:8, :])
+
+
+def pack_kernel(load_ref, rc_ref, vc_ref, vm_ref, rr_ref, lf_ref, h_ref, via_ref, out_ref, *scratch):
+    *held, sem = scratch
+    fetch([load_ref, rc_ref, vc_ref, vm_ref, rr_ref], held, sem)
+    load_v, rc_v, vc_v, vm_v, rr_v = held
     scen, rows, cols = load_ref.shape
     at, first, _ = place("gx")
     even = lax.rem(at, 2) == 0
-    for copy in copies:
-        copy.wait()
     for s in range(scen):
-        lf_ref[pl.ds(s, rows, stride=scen), :] = load_ref[s].astype(F32)
+        lf_ref[pl.ds(s, rows, stride=scen), :] = load_v[s].astype(F32)
     row = lax.broadcasted_iota(jnp.int32, (rows, cols), 0)
-    h = jnp.where(jnp.logical_and(first, row == 0), 0.0, rc_ref[...])
-    via = vm_ref[...].astype(F32) * vc_ref[...]
+    h = jnp.where(jnp.logical_and(first, row == 0), 0.0, rc_v[...])
+    via = vm_v[...].astype(F32) * vc_v[...]
     h_ref[...] = h
     via_ref[...] = via
-
-    def put(where, top, bottom):
-        a_ref[where, :] = jnp.where(even, bottom, top)
-        b_ref[where, :] = jnp.where(even, top, bottom)
-
     n = HALO * scen
-    put(pl.ds(0, n), lf_ref[0:n, :], lf_ref[rows * scen - n :, :])
-    put(pl.ds(n, SLOT), h[:SLOT], h[rows - SLOT :])
-    put(pl.ds(n + SLOT, SLOT), via[:SLOT], via[rows - SLOT :])
-    put(pl.ds(n + 2 * SLOT, 8), rr_ref[:8, :], rr_ref[rows - 8 :, :])
+    out_ref[0:n, :] = jnp.where(even, lf_ref[rows * scen - n :, :], lf_ref[0:n, :])
+    out_ref[n : n + SLOT, :] = jnp.where(even, h[rows - SLOT :], h[:SLOT])
+    out_ref[n + SLOT : n + 2 * SLOT, :] = jnp.where(even, via[rows - SLOT :], via[:SLOT])
+    out_ref[n + 2 * SLOT :, :] = jnp.where(even, rr_v[rows - 8 :, :], rr_v[:8, :])
 
 
 def packer(scen, cols):
@@ -142,29 +164,36 @@
     is_flux = jnp.logical_or(
         jnp.logical_and(lane >= 1, lane <= 6), jnp.logical_and(lane >= cols - 7, lane <= cols - 3)
     )
-    is_t = jnp.logical_or(lane == 0, lane == cols - 2)
     is_end = lane == cols - 1
     is_rolled = jnp.logical_and(lane >= 8, lane <= 11)
 
-    def pack(tl, q, jl, fl, p, grid_row):
-        moved = jl if p is None else jnp.where(is_end, p, jl)
-        rolled = pltpu.roll(moved, 10, 1)
+    def pack(q, jl, fl, p, grid_row):
+        ends = jl if p is None else jl + p
         return jnp.where(
-            is_flux, fl, jnp.where(is_t, tl, jnp.where(is_end, q, jnp.where(is_rolled, rolled, grid_row)))
+            is_flux,
+            fl,
+            jnp.where(
+                is_end,
+                q,
+                jnp.where(lane == 0, pltpu.roll(ends, 1, 1), jnp.where(is_rolled, pltpu.roll(jl, 10, 1), grid_row)),
+            ),
         )
 
     def add_p(w, p):
-        return jnp.where(lane == 9, pltpu.roll(p, 10, 1), w)
+        return w + jnp.where(lane == 0, pltpu.roll(p, 1, 1), 0.0)
 
     return pack, add_p
 
 
-def lower_row(v, via, minus_inv, vs, cols):
+def lower_row(v, via, minus_inv, vs, open_end):
+    scen, cols = v.shape
+    lane = lax.broadcasted_iota(jnp.int32, (scen, cols), 1)
     q = via * v
     tl = q * minus_inv
-    dl = pltpu.roll(tl, 1, 1) - tl
+    dl = jnp.where(lane == 0, 0.0, pltpu.roll(tl, 1, 1)) - tl
     jl = vs * dl
-    return q, tl, dl, jl, jl - pltpu.roll(jl, cols - 1, 1)
+    inner = jnp.where(jnp.logical_or(lane == 0, jnp.logical_and(open_end, lane == cols - 1)), 0.0, jl)
+    return q, tl, dl, jl, inner - pltpu.roll(inner, cols - 1, 1)
 
 
 def core_kernel(
@@ -185,14 +214,14 @@
     diag_low = vs + vs_next + tie_low
     low_s[0] = jnp.where(open_end, 0.0, -1.0 / diag_low)
     low_s[1] = tie_low
-    low_s[2] = jnp.where(jnp.logical_or(open_end, lane == 0), 0.0, vs)
+    low_s[2] = vs
     low_s[3] = jnp.where(
         lane == 12,
         pltpu.roll(vs, 12, 1),
         jnp.where(
             lane == 13,
             pltpu.roll(diag_low, 14, 1),
-            jnp.where(lane == 14, pltpu.roll(tie_low, 15, 1), pltpu.roll(vs, 16, 1)),
+            pltpu.roll(vs, 16, 1),
         ),
     )
     low_ref[...] = jnp.concatenate([low_s[k, rows - 1 : rows, :] for k in range(4)] * 2, 0)
@@ -226,7 +255,7 @@
             m = r - 1
             via_m = bc(via_ref, m)
             tie = via_m + LEAK
-            q, tl, dl, jl, fl = lower_row(v0, via_m, low(0, m), low(2, m), cols)
+            q, tl, dl, jl, fl = lower_row(v0, via_m, low(0, m), low(2, m), jnp.logical_not(last_y))
             fl_ref[pl.ds(m * scen, scen), :] = fl
             g2 -= q * tl
             g3 += low(1, m) * tl * tl + jl * dl
@@ -240,7 +269,7 @@
                 if m > 1:
                     dt = t0 - t1
                     g3 += bc(h_ref, m) * dt * dt
-            w = pack(tl, q, jl, fl, p, low(3, m))
+            w = pack(q, jl, fl, p, low(3, m))
             w_s[pl.ds(m * scen, scen), :] = w
             if m == 0:
                 keep(0, v0)
@@ -269,7 +298,16 @@
     picked = dot_nt(pick_ref[...], w_s[...])
     for k in range(size // cols):
         strip_ref[pl.ds(k * PICKED, PICKED), :] = picked[:PICKED, k * cols : (k + 1) * cols]
-    res_ref[...] = picked[PICKED + 8 :, size : size + cols]
+    res = picked[PICKED + 8 :, size : size + cols]
+    per = cols // rows
+    group = lax.div(lax.broadcasted_iota(jnp.int32, (1, cols), 1), rows)
+    packed = []
+    for start in range(0, 16, per):
+        line = res[start : start + 1]
+        for k in range(1, per):
+            line = jnp.where(group == k, pltpu.roll(res[start + k : start + k + 1], k * rows, 1), line)
+        packed.append(line)
+    res_ref[...] = jnp.concatenate(packed + [jnp.zeros((16 - len(packed), cols), F32)], 0)
 
 
 def join_kernel(
@@ -278,7 +316,8 @@
     w_s,
 ):
     rows, cols = h_ref.shape
-    even_y = lax.rem(lax.axis_index("gy"), 2) == 0
+    at_y, _, last_y = place("gy")
+    even_y = lax.rem(at_y, 2) == 0
     before, after = sides("gx", a_ref, b_ref)
     n = HALO * scen
     last = rows - 1
@@ -339,7 +378,7 @@
     def low(k):
         return jnp.broadcast_to(low_ref[pl.ds(k, 1), :], (scen, cols))
 
-    q, tl, dl, jl, fl = lower_row(v1, via(7), low(0), low(2), cols)
+    q, tl, dl, jl, fl = lower_row(v1, via(7), low(0), low(2), jnp.logical_not(last_y))
     fl_ref[...] = fl
     g2 -= q * tl
     g3 += tl * (low(1) * tl - 2.0 * p1) + jl * dl
@@ -349,27 +388,46 @@
     for k, g in enumerate((g0, g1, g2, g3)):
         w_s[pl.ds((k + 1) * scen, scen), :] = acc_ref[pl.ds(k * scen, scen), :] + g
     w_s[cols - 2 * scen : cols - scen, :] = add_p(edge(9), p0)
-    w_s[cols - scen :, :] = pack(tl, q, jl, fl, p1, low(3))
+    w_s[cols - scen :, :] = pack(q, jl, fl, p1, low(3))
     fresh = dot_nt(pick_ref[: PICKED + 8, :], w_s[...])
 
     lane = lax.broadcasted_iota(jnp.int32, (PICKED, cols), 1)
     parts = rows * scen // cols
-    base = parts * 8 + 8
+    base = parts * USED
+    half = 8 * rows // cols
+    row = lax.broadcasted_iota(jnp.int32, (8, cols), 0)
+    groups, pair_groups, seam_groups = [], [], []
     for k in range(parts):
         strip = strip_ref[pl.ds(k * PICKED, PICKED), :]
         if k == 0:
             strip = jnp.where(lane < scen, fresh[:PICKED], strip)
         if k == parts - 1:
             strip = jnp.where(lane >= cols - 2 * scen, fresh[:PICKED], strip)
+        group = strip[:8]
+        if k == 0:
+            group = jnp.where(row == USED - 1, fresh[PICKED:], group)
+        of_pair = of_seam = group
+        if 1 <= k <= half:
+            firsts, lasts = res_ref[k - 1 : k, :], res_ref[half + k - 1 : half + k, :]
+            of_pair = jnp.where(row == USED - 1, jnp.where(even_y, lasts, firsts), group)
+            of_seam = jnp.where(row == USED - 1, jnp.where(even_y, firsts, lasts), group)
+        groups.append(group)
+        pair_groups.append(of_pair)
+        seam_groups.append(of_seam)
         firsts, lasts = strip[8:16], strip[16:24]
-        for ref in (pair_ref, plain_ref, seam_ref):
-            ref[pl.ds(k * 8, 8), :] = strip[:8]
         pair_ref[pl.ds(base + k * 8, 8), :] = jnp.where(even_y, lasts, firsts)
         seam_ref[pl.ds(base + k * 8, 8), :] = jnp.where(even_y, firsts, lasts)
-    for ref in (pair_ref, plain_ref, seam_ref):
-        ref[pl.ds(parts * 8, 8), :] = fresh[PICKED:]
-    pair_ref[pl.ds(base + parts * 8, 8), :] = jnp.where(even_y, res_ref[8:, :], res_ref[:8, :])
-    seam_ref[pl.ds(base + parts * 8, 8), :] = jnp.where(even_y, res_ref[:8, :], res_ref[8:, :])
+    pack_rows(pair_ref, pair_groups)
+    pack_rows(plain_ref, groups)
+    pack_rows(seam_ref, seam_groups)
+
+
+def pack_rows(ref, groups):
+    ref[0 : len(groups) * USED, :] = jnp.concatenate([g[:USED] for g in groups], 0)
+
+
+def unpack_rows(ref, parts):
+    return jnp.concatenate([ref[k * USED : (k + 1) * USED, :] for k in range(parts)], 1)
 
 
 def across(ref, start, parts):
@@ -382,7 +440,7 @@
         in_refs, out_refs = refs[:radix], refs[radix:]
     cols = in_refs[0].shape[1]
     at = lax.rem(lax.div(lax.axis_index(axis), step), radix)
-    given = [across(ref, 0, parts) for ref in in_refs]
+    given = [unpack_rows(ref, parts) for ref in in_refs]
     blocks = []
     for j in range(radix):
         block = given[0]
@@ -391,40 +449,40 @@
         blocks.append(block)
     i2 = i3 = 0.0
     for left, right in zip(blocks, blocks[1:]):
-        t_next, vs_next = right[0:1], right[1:2]
-        q, d, tie, p, vs, t_in = (left[i : i + 1] for i in range(2, 8))
-        t = -q / (d + vs_next)
-        d_in, d_out = t_in - t, t - t_next
-        i2 = i2 - q * t
-        i3 = i3 + t * (tie * t - 2.0 * p) + vs * d_in * d_in + vs_next * d_out * d_out
+        q, e, d = (left[i : i + 1] for i in range(3))
+        jl_next, vs_next = right[3:4], right[4:5]
+        r = q / (d + vs_next)
+        i2 = i2 + q * r
+        i3 = i3 + r * (e - jl_next)
+    i3 = i2 + 2.0 * i3
     both = jnp.concatenate([i2, i3], 0)
     both = sum(both[:, k * cols : (k + 1) * cols] for k in range(parts))
     shift = scen
     while shift < cols:
         both = both + pltpu.roll(both, shift, 1)
         shift *= 2
-    group = lax.div(lax.broadcasted_iota(jnp.int32, (8, cols), 1), scen)
+    group = lax.div(lax.broadcasted_iota(jnp.int32, (1, cols), 1), scen)
     sums = jnp.where(group == 3, both[0:1], jnp.where(group == 4, both[1:2], 0.0))
-    sum_at = pl.ds(parts * 8, 8)
-    for ref in in_refs:
-        sums = sums + ref[sum_at, :]
+    sums = sum((block[USED - 1 : USED, :cols] for block in given), sums)
     if not held_refs:
-        out_refs[0][...] = sums
+        out_refs[0][...] = jnp.broadcast_to(sums, (8, cols))
         return
-    row = lax.broadcasted_iota(jnp.int32, (8, cols), 0)
-    for ref in out_refs:
-        for k in range(parts):
-            where = slice(k * cols, (k + 1) * cols)
-            ref[pl.ds(k * 8, 8), :] = jnp.where(row < 2, blocks[0][:, where], blocks[-1][:, where])
-        ref[sum_at, :] = sums
-    base = parts * 8 + 8
-    out_refs[1][base:, :] = held_refs[0][base:, :]
+    row = lax.broadcasted_iota(jnp.int32, (USED, cols), 0)
+    held = unpack_rows(held_refs[0], parts)
+    groups = []
+    for k in range(parts):
+        where = slice(k * cols, (k + 1) * cols)
+        group = jnp.where(row < 3, blocks[-1][:, where], blocks[0][:, where])
+        groups.append(jnp.where(row == USED - 1, sums if k == 0 else held[:, where], group))
+    pack_rows(out_refs[0], groups)
+    pack_rows(out_refs[1], groups)
+    out_refs[1][parts * USED :, :] = held_refs[0][parts * USED :, :]
 
 
 def row_kernel(
     scen, lf_ref, h_ref, via_ref, rr_ref, a_ref, b_ref,
     v_ref, t_ref, gv_ref, gt_ref, br_ref,
-    inv_s, h_s, tie_s, fv_s, ft_s, sv_s, st_s, s0_s,
+    inv_s, h_s, tie_s, fv_s, ft_s, s0_s,
 ):
     rows, cols = h_ref.shape
     _, first, last = place("gx")
@@ -462,14 +520,9 @@
             if m > 1 - HALO:
                 ht1 = bc(h_s, m) * (t0 - t1)
                 if m > 2 - HALO:
-                    ft = ht0 - ht1
-                    at = pl.ds((m - 1 + STEPS - 1) * scen, scen)
-                    ft_s[at, :] = ft
-                    st_s[at, :] = ft
+                    ft_s[pl.ds((m - 1 + STEPS - 1) * scen, scen), :] = ht0 - ht1
                 if m < rows + STEPS - 1:
-                    at = pl.ds((m + STEPS - 1) * scen, scen)
-                    fv_s[at, :] = fv
-                    sv_s[at, :] = fv
+                    fv_s[pl.ds((m + STEPS - 1) * scen, scen), :] = fv
             if 0 <= m < rows:
                 v_ref[pl.ds(m, scen, stride=rows), :] = v0
                 t_ref[pl.ds(m, scen, stride=rows), :] = t1
@@ -477,79 +530,78 @@
         v0, hv0 = v1, hv1
 
     n += 2 * SLOT
-    count = rows + 2 * (STEPS - 1)
-    rate_first = jnp.where(first, 0.0, RELAX)
-    rate_last = jnp.where(last, 0.0, RELAX)
-
-    def rate(r):
-        return rate_first if r == 0 else rate_last if r == rows else RELAX
-
     size = rows + 16
     row = lax.broadcasted_iota(jnp.int32, (size, cols), 0)
-    rates = jnp.where(row == 8, rate_first, jnp.where(row == 8 + rows, rate_last, RELAX))
+    closed = jnp.logical_or(jnp.logical_and(first, row == 8), jnp.logical_and(last, row == 8 + rows))
+    rates = jnp.where(closed, 0.0, RELAX)
     s0_s[...] = jnp.concatenate([before(pl.ds(n, 8)), rr_ref[...], after(pl.ds(n, 8))], 0)
 
-    def start_step():
+    def one(_, carry):
         now = s0_s[...]
         flux = rates * (pltpu.roll(now, 1, 0) - now)
-        return now + flux - pltpu.roll(flux, size - 1, 0)
-
-    def one(_, carry):
-        s0_s[...] = start_step()
-        for f_ref, s_ref in ((fv_s, sv_s), (ft_s, st_s)):
-            here = s_ref[pl.ds(0, scen), :]
-            flux = jnp.zeros_like(here)
-            for i in range(count):
-                r = i - (STEPS - 1)
-                at = pl.ds(i * scen, scen)
-                if i + 1 < count:
-                    following = s_ref[pl.ds((i + 1) * scen, scen), :]
-                    flux_next = rate(r + 1) * (here - following)
-                else:
-                    following, flux_next = here, jnp.zeros_like(here)
-                s_ref[at, :] = here + (flux - flux_next) + f_ref[at, :]
-                here, flux = following, flux_next
+        s0_s[...] = now + flux - pltpu.roll(flux, size - 1, 0)
         return carry
 
-    lax.fori_loop(0, STEPS - 1, one, 0)
-    br_ref[...] = start_step()[8 : 8 + rows]
-    gain = RELAX * DRIVE
-    for m in range(rows):
-        at = pl.ds((m + STEPS - 1) * scen, scen)
-        gv_ref[pl.ds(m, scen, stride=rows), :] = gain * sv_s[at, :]
-        gt_ref[pl.ds(m, scen, stride=rows), :] = gain * st_s[at, :]
-
-
-def col_kernel(scen, steps, fl_ref, fl_last_ref, cr_ref, own_ref, *rest):
+    lax.fori_loop(0, STEPS, one, 0)
+    br_ref[...] = s0_s[8 : 8 + rows, :]
+
+    weights = taps()
+    reach = STEPS - 1
+    for f_ref, out_ref in ((fv_s, gv_ref), (ft_s, gt_ref)):
+
+        def at(r):
+            return f_ref[pl.ds((r + reach) * scen, scen), :]
+
+        window = {}
+        for r in range(-reach, rows + reach):
+            if r < 0:
+                x = jnp.where(first, at(-1 - r), at(r))
+            elif r >= rows:
+                x = jnp.where(last, at(2 * rows - 1 - r), at(r))
+            else:
+                x = at(r)
+            window[r] = x
+            m = r - reach
+            if m >= 0:
+                total = weights[0] * window[m]
+                for d in range(1, STEPS):
+                    total = total + weights[d] * (window[m - d] + window[m + d])
+                out_ref[pl.ds(m, scen, stride=rows), :] = total
+                del window[m - reach]
+
+
+def col_kernel(scen, steps, fl_ref, fl_last_ref, cr_ref, pair_ref, seam_ref, *rest):
     *got_refs, source_ref, start_ref, gl_ref, bc_ref, out_s = rest
     rows, cols = cr_ref.shape
     parts = rows * scen // cols
-    base = parts * 8 + 8
+    base = parts * USED
     at, first, last = place("gy")
     kind = first.astype(jnp.int32) + 2 * last.astype(jnp.int32)
     odd = lax.rem(at, 2) == 1
 
     def contents(ref):
-        return across(ref, 0, parts), across(ref, base, parts), ref[pl.ds(base + parts * 8, 8), :]
+        return unpack_rows(ref, parts), across(ref, base, parts)
 
     paired = contents(got_refs[0])
     met = tuple(jnp.zeros_like(x) for x in paired)
     for mask, ref in zip(steps[1:], got_refs[1:]):
         here = jnp.abs(jnp.bitwise_xor(at, mask) - at) == 1
         met = tuple(jnp.where(here, x, y) for x, y in zip(contents(ref), met))
-    sums_before, before, res_before = (jnp.where(odd, x, y) for x, y in zip(paired, met))
-    sums_after, after, res_after = (jnp.where(odd, y, x) for x, y in zip(paired, met))
-    own = across(own_ref, 0, parts)
-
-    def seam(left, right):
-        q, d, _, _, vs, t_in = (left[i : i + 1] for i in range(2, 8))
-        t_next, vs_next = right[0:1], right[1:2]
+    sums_before, before = (jnp.where(odd, x, y) for x, y in zip(paired, met))
+    sums_after, after = (jnp.where(odd, y, x) for x, y in zip(paired, met))
+    own, own_pair = contents(pair_ref)
+    own_last = jnp.where(odd, across(seam_ref, base, parts), own_pair)
+
+    def seam(left, lasts, right):
+        q, d = left[0:1], left[2:3]
+        u, vs = lasts[6:7], lasts[7:8]
+        jl_next, vs_next = right[3:4], right[4:5]
         diag = d + vs_next
         t = -q / jnp.where(diag > 0, diag, 1.0)
-        return vs * (t_in - t), vs_next * (t - t_next)
-
-    jl_last, jl_0 = seam(sums_before, own)
-    jr_last, jr_0 = seam(own, sums_after)
+        return u - vs * t, vs_next * t + jl_next
+
+    jl_last, jl_0 = seam(sums_before, before, own)
+    jr_last, jr_0 = seam(own, own_last, sums_after)
     jr_last = jnp.where(last, 0.0, jr_last)
     jr_0 = jnp.where(last, 0.0, jr_0)
     zero = jnp.zeros_like(jl_0)
@@ -581,7 +633,13 @@
     for m in range(rows):
         gl_ref[pl.ds(m, scen, stride=rows), :] = out_s[pl.ds(m * scen, scen), :]
     start = start_ref[kind]
-    edge = dot_tn(jnp.concatenate([res_before, res_after], 0), start[cols:])
+    per = cols // rows
+    res = []
+    for block in (sums_before, sums_after):
+        for k in range(8):
+            lanes = block[USED - 1 : USED, (1 + k // per) * cols : (2 + k // per) * cols]
+            res.append(lanes if k % per == 0 else pltpu.roll(lanes, cols - k % per * rows, 1))
+    edge = dot_tn(jnp.concatenate(res, 0), start[cols:])
     bc_ref[...] = dot_nn(cr_ref[...], start[:cols]) + edge[:rows]
 
 
@@ -619,14 +677,19 @@
     return lax.ppermute(block, axis, [(i, i ^ mask) for i in range(count)])
 
 
-def exchange(even_side, odd_side, axis):
-    count = lax.axis_size(axis)
-
-    def pairs(start):
-        return [((i + a) % count, (i + 1 - a) % count) for i in range(start, count, 2) for a in (0, 1)]
-
-    second = lax.ppermute(odd_side, axis, pairs(1))
-    return lax.ppermute(even_side, axis, pairs(0)), second
+def swap_odd(block, axis, idle):
+    count, lines = lax.axis_size(axis), lax.axis_size(idle)
+    pairs = []
+    for line in range(lines):
+        for i in range(count):
+            if 0 < i < count - 1:
+                partner = line * count + (i + 1 if i % 2 else i - 1)
+            elif lines % 2 == 0:
+                partner = (line ^ 1) * count + i
+            else:
+                partner = line * count + count - 1 - i
+            pairs.append((line * count + i, partner))
+    return lax.ppermute(block, (idle, axis), pairs)
 
 
 def call(kernel, out, scratch, cost, *args, space=pltpu.VMEM):
@@ -660,15 +723,27 @@
 
     wide = f32(HALO * scen + 2 * SLOT + 8, cols)
     sources = (load_current, row_conductance, via_conductance, via_mask, row_residual)
-    lf, h, via, x_a, x_b = call(
+    pinned = [pltpu.with_memory_space_constraint(x, pltpu.HBM) for x in sources]
+    sems = pltpu.SemaphoreType.DMA((len(sources),))
+    shapes = [(scen, SLOT, cols)] + [(SLOT, cols)] * 4
+    odd_strip = call(
+        edge_kernel,
+        wide,
+        [pltpu.VMEM(shape, x.dtype) for shape, x in zip(shapes, sources)] + [vmem(SLOT * scen, cols), sems],
+        10**5,
+        *pinned,
+        space=pltpu.HBM,
+    )
+    x_b = swap_odd(odd_strip, "gx", "grp")
+    lf, h, via, even_strip = call(
         pack_kernel,
-        (field, grid, grid, wide, wide),
-        [pltpu.VMEM(x.shape, x.dtype) for x in sources] + [pltpu.SemaphoreType.DMA((len(sources),))],
+        (field, grid, grid, wide),
+        [pltpu.VMEM(x.shape, x.dtype) for x in sources] + [sems],
         10**5,
-        *(pltpu.with_memory_space_constraint(x, pltpu.HBM) for x in sources),
+        *pinned,
         space=pltpu.HBM,
     )
-    x_a, x_b = exchange(x_a, x_b, "gx")
+    x_a = swap(even_strip, "gx", 1)
 
     fl, acc, edge, low, strip, res = call(
         functools.partial(core_kernel, scen),
@@ -679,10 +754,11 @@
     )
     x_a, x_b, acc = lax.optimization_barrier((x_a, x_b, acc))
 
-    plain_shape, full_shape = f32(parts * 8 + 8, cols), f32(parts * 16 + 16, cols)
+    plain_shape, full_shape = f32(parts * USED + 0, cols), f32(parts * (USED + 8) + 0, cols)
+    seam_shape = f32(parts * (USED + 8) + 8, cols)
     pair, plain, seam, fl_last = call(
         functools.partial(join_kernel, scen),
-        (full_shape, plain_shape, full_shape, f32(scen, cols)),
+        (full_shape, plain_shape, seam_shape, f32(scen, cols)),
         [vmem(cols, cols)],
         10**6,
         lf, h, via, acc, edge, low, strip, res, x_a, x_b, pick,
@@ -693,12 +769,12 @@
     v, t, gv, gt, br = call(
         functools.partial(row_kernel, scen),
         (field, field, field, field, grid),
-        [vmem(ext, cols)] * 3 + [vmem(reach, cols)] * 4 + [vmem(rows + 16, cols)],
+        [vmem(ext, cols)] * 3 + [vmem(reach, cols)] * 2 + [vmem(rows + 16, cols)],
         10**7,
         lf, h, via, row_residual, x_a, x_b,
     )
 
-    own, masks, received = pair, [], []
+    own_pair, own_seam, masks, received = pair, seam, [], []
     step, count = 1, lax.axis_size("gy")
     while step < count:
         radix = 4 if 4 * step <= count else 2
@@ -714,7 +790,7 @@
             *got, br = lax.optimization_barrier((*got, br))
         merge = functools.partial(merge_kernel, scen, parts, "gy", step, radix)
         if step * radix < count:
-            plain, seam = call(merge, (plain_shape, full_shape), [], 10**5, plain, *got, seam)
+            plain, seam = call(merge, (plain_shape, seam_shape), [], 10**5, plain, *got, seam)
         else:
             sums = call(merge, f32(8, cols), [], 10**5, plain, *got)
         step *= radix
@@ -724,7 +800,7 @@
         (field, grid),
         [vmem(size, cols)],
         10**7,
-        fl, fl_last, col_residual, own, *received, source, start,
+        fl, fl_last, col_residual, own_pair, own_seam, *received, source, start,
     )
 
     step, others = 1, []

time: 21.9 us -> 21.6 us (0.986)
  waiting for transfers between devices: 4.82 us -> 3.88 us
  starting transfers between devices: 9.4 us -> 9.84 us
  Pallas kernels: 6.71 us -> 6.95 us
    ppermute x2 -> x1, waiting for transfers between devices: 1.97 us -> 0.27 us  [swap_odd(): return lax.ppermute(block, (idle, axis), pairs)]
    ppermute x6 -> x7, waiting for transfers between devices: 2.85 us -> 3.61 us  [swap(): return lax.ppermute(block, axis, [(i, i ^ mask) for i in range(count)])]
    ppermute x6 -> x7, starting transfers between devices: 6.27 us -> 6.81 us  [swap(): return lax.ppermute(block, axis, [(i, i ^ mask) for i in range(count)])]
    pallas_call x7 -> x8, Pallas kernels: 6.71 us -> 6.95 us  [call(): pl.pallas_call(kernel, out_shape=out, in_specs=[pl.BlockSpec(memory_space...]
    ppermute x2 -> x1, starting transfers between devices: 3.13 us -> 3.03 us  [swap_odd(): return lax.ppermute(block, (idle, axis), pairs)]
  transfers between devices with their start and end apart: 8 -> 8, of which waited for: 4 -> 4; matrix products, arithmetic and copies ran while one was open for 0% -> 0% of each run, Pallas kernels for 18% -> 20%
where the time goes in v6:
time: 21.6 us; the launch traced here: 21.4 us
  starting transfers between devices  9.84 us (46%)
  Pallas kernels  6.95 us (32%)
  waiting for transfers between devices  3.88 us (18%)
  between operations  0.69 us (3%)
    pallas_call x8, Pallas kernels, call(): pl.pallas_call(kernel, out_shape=out, in_specs=[pl.BlockSpec(memory_space...  6.95 us
    ppermute x7, starting transfers between devices, swap(): return lax.ppermute(block, axis, [(i, i ^ mask) for i in range(count)])  6.81 us
    ppermute x7, waiting for transfers between devices, swap(): return lax.ppermute(block, axis, [(i, i ^ mask) for i in range(count)])  3.61 us
    ppermute x1, starting transfers between devices, swap_odd(): return lax.ppermute(block, (idle, axis), pairs)  3.03 us
  transfers between devices with their start and end apart: 8, of which 4 were waited for; matrix products, arithmetic and copies ran while one was open for 0% of the time, Pallas kernels for 20%

profile of v6, /device:TPU:0, one launch (start us, length us, event | category | flops | bytes accessed | tf_op | source)
XLA Modules:
  0.0 21.4 jit_solution(15698062746580841202)
XLA Ops:
  0.6 1.0 %shard_map.131 = f32[184,128]{1,0:T(8,128)S(1)} custom-call(bf16[16,32,128]{2,1,0:T(8,128)(2,1)} %load_ref.3, f32[32,128]{1,0:T(8,128)} %rc_ref.3, f32[32,128]{1,0:T(8,128)} %vc_ref.3, s32[32,128]{1,0:T(8,128)} %vm_ref.3, f32[32,128]{1,0:T(8,128)} %rr_ref.5), custom_call_target="tpu_custom_call" | custom-call | flops 100000 | tf_op jit(solution)/shard_map/pallas_call | solution.py:696
  1.6 3.0 %collective-permute-start.1 = (f32[184,128]{1,0:T(8,128)S(1)}, f32[184,128]{1,0:T(8,128)S(1)}, u32[]{:S(2)}, u32[]{:S(2)}) collective-permute-start(f32[184,128]{1,0:T(8,128)S(1)} %shard_map.131), channel_id=1, source_target_pairs={{0,16},{4,8},{8,4},{12,28},{16,0},{20,24},{24,20},{28,12},{1,17},{... | collective-permute-start | bytes 282632 | tf_op jit(solution)/shard_map/ppermute | solution.py:692
  4.6 0.0 copy-start.3
  4.6 0.0 copy-start.4
  4.6 0.0 copy-start.5
  4.6 0.0 copy-start.6
  4.6 1.1 %shard_map.130 = (f32[512,128]{1,0:T(8,128)S(1)}, f32[32,128]{1,0:T(8,128)S(1)}, f32[32,128]{1,0:T(8,128)S(1)}, f32[184,128]{1,0:T(8,128)S(1)}) custom-call(bf16[16,32,128]{2,1,0:T(8,128)(2,1)} %load_ref.3, f32[32,128]{1,0:T(8,128)} %rc_ref.3, f32[32,128]{1,0:T(8,128)} %vc_ref.3, s32[32,128]{1,0:T(8,128)} %vm_ref.3, f32[32,128]{1,0:T(8,128)} %rr_ref.5), custom_call_target="tpu_custom_call" | custom-call | flops 100000 | tf_op jit(solution)/shard_map/pallas_call | solution.py:696
  5.8 0.2 collective-permute-start
  5.9 0.0 copy-done.3
  5.9 0.0 copy-done.4
  5.9 0.0 copy-done.5
  5.9 0.0 copy-done.6
  5.9 1.0 %shard_map.132 = (f32[512,128]{1,0:T(8,128)S(1)}, f32[64,128]{1,0:T(8,128)S(1)}, f32[160,128]{1,0:T(8,128)S(1)}, f32[8,128]{1,0:T(8,128)S(1)}, f32[96,128]{1,0:T(8,128)S(1)}, /*index=5*/f32[16,128]{1,0:T(8,128)S(1)}) custom-call(f32[512,128]{1,0:T(8,128)S(1)} %get-tuple-element.35.lf_ref, f32[32,128]{1,0:T(8,128)S(1)} %get-tuple-element.36.h_ref, ...), custom_call_target="tpu_custom_call" | custom-call | flops 10000000 | tf_op jit(solution)/shard_map/pallas_call | solution.py:696
  6.9 0.3 %collective-permute-done.1.b_ref = f32[184,128]{1,0:T(8,128)S(1)} collective-permute-done((f32[184,128]{1,0:T(8,128)S(1)}, f32[184,128]{1,0:T(8,128)S(1)}, u32[]{:S(2)}, u32[]{:S(2)}) %collective-permute-start.1) | collective-permute-done | bytes 94240 | tf_op jit(solution)/shard_map/ppermute | solution.py:692
  7.2 0.0 collective-permute-done.a_ref
  7.2 0.0 copy-start.2
  7.2 0.0 copy-start.1
  7.2 0.4 %shard_map.134 = (f32[56,128]{1,0:T(8,128)S(1)}, f32[24,128]{1,0:T(8,128)S(1)}, f32[64,128]{1,0:T(8,128)S(1)}, f32[16,128]{1,0:T(8,128)S(1)}) custom-call(f32[512,128]{1,0:T(8,128)S(1)} %get-tuple-element.35.lf_ref, f32[32,128]{1,0:T(8,128)S(1)} %get-tuple-element.36.h_ref, f32[32,128]{1,0:T(8,128)S(1)} %get-tuple-element.37.via_ref, ...), custom_call_target="tpu_custom_call" | custom-call | flops 1000000 | tf_op jit(solution)/shard_map/pallas_call | solution.py:696
  7.5 0.0 copy-start
  7.5 4.2 %collective-permute-start.3 = (f32[64,128]{1,0:T(8,128)S(1)}, f32[64,128]{1,0:T(8,128)S(1)}, u32[]{:S(2)}, u32[]{:S(2)}) collective-permute-start(f32[64,128]{1,0:T(8,128)S(1)} %get-tuple-element.54.seam_ref), channel_id=1, source_target_pairs={{0,3},{1,2},{2,1},{3,0},{4,7},{5,6},{6,5},{7,4},{8,11},{9,10},{10,... | collective-permute-start | bytes 98312 | tf_op jit(solution)/shard_map/ppermute | solution.py:677
  11.7 0.0 collective-permute-start.2
  11.7 0.6 %collective-permute-start.4 = (f32[24,128]{1,0:T(8,128)S(1)}, f32[24,128]{1,0:T(8,128)S(1)}, u32[]{:S(2)}, u32[]{:S(2)}) collective-permute-start(f32[24,128]{1,0:T(8,128)S(1)} %get-tuple-element.56.refs_0_), channel_id=1, source_target_pairs={{0,2},{1,3},{2,0},{3,1},{4,6},{5,7},{6,4},{7,5},{8,10},{9,11},{10,... | collective-permute-start | bytes 36872 | tf_op jit(solution)/shard_map/ppermute | solution.py:677
  12.3 0.0 copy-done.2
  12.3 1.3 %shard_map.133 = (f32[512,128]{1,0:T(8,128)S(1)}, f32[512,128]{1,0:T(8,128)S(1)}, f32[512,128]{1,0:T(8,128)S(1)}, f32[512,128]{1,0:T(8,128)S(1)}, f32[32,128]{1,0:T(8,128)S(1)}) custom-call(f32[512,128]{1,0:T(8,128)S(1)} %get-tuple-element.35.lf_ref, f32[32,128]{1,0:T(8,128)S(1)} %get-tuple-element.36.h_ref, f32[32,128]{1,0:T(8,128)S(1)} %get-tuple-element.37.via_ref, ...), custom_call_target="tpu_custom_call" | custom-call | flops 10000000 | tf_op jit(solution)/shard_map/pallas_call | solution.py:696
  13.6 2.7 %collective-permute-done.4.refs_2_ = f32[24,128]{1,0:T(8,128)S(1)} collective-permute-done((f32[24,128]{1,0:T(8,128)S(1)}, f32[24,128]{1,0:T(8,128)S(1)}, u32[]{:S(2)}, u32[]{:S(2)}) %collective-permute-start.4) | collective-permute-done | bytes 12320 | tf_op jit(solution)/shard_map/ppermute | solution.py:677
  16.3 0.0 collective-permute-done.2.rest_0_.refs_1_
  16.3 0.0 collective-permute-done.3.rest_1_.refs_3_
  16.3 0.3 %shard_map.136.rest_0_ = f32[8,128]{1,0:T(8,128)S(1)} custom-call(f32[24,128]{1,0:T(8,128)S(1)} %get-tuple-element.56.refs_0_, f32[56,128]{1,0:T(8,128)S(1)} %collective-permute-done.2.rest_0_.refs_1_, f32[24,128]{1,0:T(8,128)S(1)} %collective-permute-done.4.refs_2_, f32[64,128]{1,0:T(8,128)S(1)} %collective-permute-done.3.rest_1_.refs_3_), custom_call_target="tpu_custom_call" | custom-call | flops 100000 | tf_op jit(solution)/shard_map/pallas_call | solution.py:696
  16.6 0.0 collective-permute-start.7
  16.6 1.0 %collective-permute-start.6 = (f32[8,128]{1,0:T(8,128)S(1)}, f32[8,128]{1,0:T(8,128)S(1)}, u32[]{:S(2)}, u32[]{:S(2)}) collective-permute-start(f32[8,128]{1,0:T(8,128)S(1)} %shard_map.136.rest_0_), channel_id=1, source_target_pairs={{0,8},{4,12},{8,0},{12,4},{1,9},{5,13},{9,1},{13,5},{2,10},{6,14},... | collective-permute-start | bytes 12296 | tf_op jit(solution)/shard_map/ppermute | solution.py:677
  17.5 0.9 %collective-permute-start.5 = (f32[8,128]{1,0:T(8,128)S(1)}, f32[8,128]{1,0:T(8,128)S(1)}, u32[]{:S(2)}, u32[]{:S(2)}) collective-permute-start(f32[8,128]{1,0:T(8,128)S(1)} %shard_map.136.rest_0_), channel_id=1, source_target_pairs={{0,4},{4,0},{8,12},{12,8},{1,5},{5,1},{9,13},{13,9},{2,6},{6,2},{1... | collective-permute-start | bytes 12296 | tf_op jit(solution)/shard_map/ppermute | solution.py:677
  18.4 0.0 copy-done.1
  18.4 0.0 copy-done
  18.4 0.9 %shard_map.135 = (f32[512,128]{1,0:T(8,128)S(1)}, f32[32,128]{1,0:T(8,128)S(1)}) custom-call(f32[512,128]{1,0:T(8,128)S(1)} %get-tuple-element.46.fl_ref, f32[16,128]{1,0:T(8,128)S(1)} %get-tuple-element.52.fl_last_ref, f32[32,128]{1,0:T(8,128)S(1)} %copy-done.4, f32[56,128]{1,0:T(8,128)S(1)} %get-tuple-element.53.pair_ref, ...), custom_call_target="tpu_custom_call" | custom-call | flops 10000000 | tf_op jit(solution)/shard_map/pallas_call | solution.py:696
  19.3 0.3 %collective-permute-done.7.rest_3_ = f32[8,128]{1,0:T(8,128)S(1)} collective-permute-done((f32[8,128]{1,0:T(8,128)S(1)}, f32[8,128]{1,0:T(8,128)S(1)}, u32[]{:S(2)}, u32[]{:S(2)}) %collective-permute-start.7) | collective-permute-done | bytes 4128 | tf_op jit(solution)/shard_map/ppermute | solution.py:677
  19.6 0.6 %collective-permute-done.6.rest_2_ = f32[8,128]{1,0:T(8,128)S(1)} collective-permute-done((f32[8,128]{1,0:T(8,128)S(1)}, f32[8,128]{1,0:T(8,128)S(1)}, u32[]{:S(2)}, u32[]{:S(2)}) %collective-permute-start.6) | collective-permute-done | bytes 4128 | tf_op jit(solution)/shard_map/ppermute | solution.py:677
  20.2 0.0 collective-permute-done.5.rest_1_
  20.2 1.1 %shard_map.137 = (f32[16,32,128]{2,1,0:T(8,128)}, f32[16,32,128]{2,1,0:T(8,128)}, f32[16,32,128]{2,1,0:T(8,128)}) custom-call(f32[512,128]{1,0:T(8,128)S(1)} %get-tuple-element.42.v_ref, f32[512,128]{1,0:T(8,128)S(1)} %get-tuple-element.43.t_ref, f32[512,128]{1,0:T(8,128)S(1)} %get-tuple-element.44.gv_ref, f32[512,128]{1,0:T(8,128)S(1)} %get-tuple-element.45.gt_ref, ...), custom_call_target="tpu_custom_call" | custom-call | flops 1000000 | tf_op jit(solution)/shard_map/pallas_call | solution.py:696
Async XLA Ops:
  1.6 5.6 %collective-permute-start.1 = (f32[184,128]{1,0:T(8,128)S(1)}, f32[184,128]{1,0:T(8,128)S(1)}, u32[]{:S(2)}, u32[]{:S(2)}) collective-permute-start(f32[184,128]{1,0:T(8,128)S(1)} %shard_map.131), channel_id=1, source_target_pairs={{0,16},{4,8},{8,4},{12,28},{16,0},{20,24},{24,20},{28,12},{1,17},{... | collective-permute-start | bytes 282632 | tf_op jit(solution)/shard_map/ppermute | solution.py:692
  4.6 1.3 %copy-start.3 = (f32[48,128]{1,0:T(8,128)S(1)}, f32[48,128]{1,0:T(8,128)}, u32[]{:S(2)}) copy-start(f32[48,128]{1,0:T(8,128)} %constant.6.clone.pick_ref) | copy-start | bytes 73732
  4.6 1.3 %copy-start.4 = (f32[32,128]{1,0:T(8,128)S(1)}, f32[32,128]{1,0:T(8,128)}, u32[]{:S(2)}) copy-start(f32[32,128]{1,0:T(8,128)} %cr_ref.3) | copy-start | bytes 49156
  4.6 1.3 %copy-start.5 = (f32[32,128]{1,0:T(8,128)S(1)}, f32[32,128]{1,0:T(8,128)}, u32[]{:S(2)}) copy-start(f32[32,128]{1,0:T(8,128)} %cc_ref.1) | copy-start | bytes 49156
  4.6 1.3 %copy-start.6 = (s32[32,128]{1,0:T(8,128)S(1)}, s32[32,128]{1,0:T(8,128)}, u32[]{:S(2)}) copy-start(s32[32,128]{1,0:T(8,128)} %pm_ref.1) | copy-start | bytes 49156
  5.8 1.4 %collective-permute-start = (f32[184,128]{1,0:T(8,128)S(1)}, f32[184,128]{1,0:T(8,128)S(1)}, u32[]{:S(2)}, u32[]{:S(2)}) collective-permute-start(f32[184,128]{1,0:T(8,128)S(1)} %get-tuple-element.38), channel_id=1, source_target_pairs={{0,4},{4,0},{8,12},{12,8},{1,5},{5,1},{9,13},{13,9},{2,6},{6,2},{1... | collective-permute-start | bytes 282632 | tf_op jit(solution)/shard_map/ppermute | solution.py:677
  7.2 5.2 %copy-start.2 = (f32[32,128]{1,0:T(8,128)S(1)}, f32[32,128]{1,0:T(8,128)}, u32[]{:S(2)}) copy-start(f32[32,128]{1,0:T(8,128)} %rr_ref.5) | copy-start | bytes 49156
  7.2 11.2 %copy-start.1 = (f32[4,144,128]{2,1,0:T(8,128)S(1)}, f32[4,144,128]{2,1,0:T(8,128)}, u32[]{:S(2)}) copy-start(f32[4,144,128]{2,1,0:T(8,128)} %constant.8.clone.rest_3_) | copy-start | bytes 884740
  7.5 10.9 %copy-start = (f32[4,152,128]{2,1,0:T(8,128)S(1)}, f32[4,152,128]{2,1,0:T(8,128)}, u32[]{:S(2)}) copy-start(f32[4,152,128]{2,1,0:T(8,128)} %constant.7.clone.rest_2_) | copy-start | bytes 933892
  7.5 8.8 %collective-permute-start.3 = (f32[64,128]{1,0:T(8,128)S(1)}, f32[64,128]{1,0:T(8,128)S(1)}, u32[]{:S(2)}, u32[]{:S(2)}) collective-permute-start(f32[64,128]{1,0:T(8,128)S(1)} %get-tuple-element.54.seam_ref), channel_id=1, source_target_pairs={{0,3},{1,2},{2,1},{3,0},{4,7},{5,6},{6,5},{7,4},{8,11},{9,10},{10,... | collective-permute-start | bytes 98312 | tf_op jit(solution)/shard_map/ppermute | solution.py:677
  11.7 4.6 %collective-permute-start.2 = (f32[56,128]{1,0:T(8,128)S(1)}, f32[56,128]{1,0:T(8,128)S(1)}, u32[]{:S(2)}, u32[]{:S(2)}) collective-permute-start(f32[56,128]{1,0:T(8,128)S(1)} %get-tuple-element.53.pair_ref), channel_id=1, source_target_pairs={{0,1},{1,0},{2,3},{3,2},{4,5},{5,4},{6,7},{7,6},{8,9},{9,8},{10,11... | collective-permute-start | bytes 86024 | tf_op jit(solution)/shard_map/ppermute | solution.py:677
  11.7 4.6 %collective-permute-start.4 = (f32[24,128]{1,0:T(8,128)S(1)}, f32[24,128]{1,0:T(8,128)S(1)}, u32[]{:S(2)}, u32[]{:S(2)}) collective-permute-start(f32[24,128]{1,0:T(8,128)S(1)} %get-tuple-element.56.refs_0_), channel_id=1, source_target_pairs={{0,2},{1,3},{2,0},{3,1},{4,6},{5,7},{6,4},{7,5},{8,10},{9,11},{10,... | collective-permute-start | bytes 36872 | tf_op jit(solution)/shard_map/ppermute | solution.py:677
  16.6 3.0 %collective-permute-start.7 = (f32[8,128]{1,0:T(8,128)S(1)}, f32[8,128]{1,0:T(8,128)S(1)}, u32[]{:S(2)}, u32[]{:S(2)}) collective-permute-start(f32[8,128]{1,0:T(8,128)S(1)} %shard_map.136.rest_0_), channel_id=1, source_target_pairs={{0,12},{4,8},{8,4},{12,0},{1,13},{5,9},{9,5},{13,1},{2,14},{6,10},... | collective-permute-start | bytes 12296 | tf_op jit(solution)/shard_map/ppermute | solution.py:677
  16.6 3.7 %collective-permute-start.6 = (f32[8,128]{1,0:T(8,128)S(1)}, f32[8,128]{1,0:T(8,128)S(1)}, u32[]{:S(2)}, u32[]{:S(2)}) collective-permute-start(f32[8,128]{1,0:T(8,128)S(1)} %shard_map.136.rest_0_), channel_id=1, source_target_pairs={{0,8},{4,12},{8,0},{12,4},{1,9},{5,13},{9,1},{13,5},{2,10},{6,14},... | collective-permute-start | bytes 12296 | tf_op jit(solution)/shard_map/ppermute | solution.py:677
  17.5 2.7 %collective-permute-start.5 = (f32[8,128]{1,0:T(8,128)S(1)}, f32[8,128]{1,0:T(8,128)S(1)}, u32[]{:S(2)}, u32[]{:S(2)}) collective-permute-start(f32[8,128]{1,0:T(8,128)S(1)} %shard_map.136.rest_0_), channel_id=1, source_target_pairs={{0,4},{4,0},{8,12},{12,8},{1,5},{5,1},{9,13},{13,9},{2,6},{6,2},{1... | collective-permute-start | bytes 12296 | tf_op jit(solution)/shard_map/ppermute | solution.py:677

commit v7 on v6

--- a/solution.py
+++ b/solution.py
@@ -22,13 +22,25 @@
 FIRST_LANES = [11, 1, 2, 3, 4, 5, 6]
 LAST_LANES = [8, -7, -6, -5, -4, -3, 9, 15]
 PICKED = 8 + 8 + 8
-USED = 6
+USED = 8
 
 
 def dot_nt(a, b):
     return lax.dot_general(
         a, b, (((1,), (1,)), ((), ())), precision=lax.Precision.HIGHEST, preferred_element_type=F32
     )
+
+
+def pick_nt(pick, b):
+    out = None
+    for _ in range(3):
+        part = b.astype(jnp.bfloat16)
+        b = b - part.astype(F32)
+        term = lax.dot_general(
+            pick.astype(jnp.bfloat16), part, (((1,), (1,)), ((), ())), preferred_element_type=F32
+        )
+        out = term if out is None else out + term
+    return out
 
 
 def dot_nn(a, b):
@@ -295,7 +307,7 @@
     w_s[size + rows :, :] = jnp.zeros((w_s.shape[0] - size - rows, cols), F32)
     for k, g in enumerate((g0, g1, g2, g3)):
         acc_ref[pl.ds(k * scen, scen), :] = g
-    picked = dot_nt(pick_ref[...], w_s[...])
+    picked = pick_nt(pick_ref[...], w_s[...])
     for k in range(size // cols):
         strip_ref[pl.ds(k * PICKED, PICKED), :] = picked[:PICKED, k * cols : (k + 1) * cols]
     res = picked[PICKED + 8 :, size : size + cols]
@@ -389,7 +401,7 @@
         w_s[pl.ds((k + 1) * scen, scen), :] = acc_ref[pl.ds(k * scen, scen), :] + g
     w_s[cols - 2 * scen : cols - scen, :] = add_p(edge(9), p0)
     w_s[cols - scen :, :] = pack(q, jl, fl, p1, low(3))
-    fresh = dot_nt(pick_ref[: PICKED + 8, :], w_s[...])
+    fresh = pick_nt(pick_ref[: PICKED + 8, :], w_s[...])
 
     lane = lax.broadcasted_iota(jnp.int32, (PICKED, cols), 1)
     parts = rows * scen // cols
@@ -648,12 +660,9 @@
     cols = v_ref.shape[1]
     sums = sum(ref[...] for ref in sum_refs)
     g0, g1, g2, g3 = (pltpu.roll(sums, cols - (k + 1) * scen, 1) for k in range(4))
-    alpha = g0 / g1
-    rz = alpha * alpha * g2 - g0
-    grow = alpha * g2 / g1
-    beta_alpha = rz / (alpha * alpha * (g3 - g2 * g2 / g1))
-    c0 = alpha + beta_alpha * grow
-    c1 = -alpha * beta_alpha
+    alpha, ratio = g0 / g1, g2 / g1
+    c1 = (g1 - alpha * g2) / (g3 - ratio * g2)
+    c0 = alpha - ratio * c1
     lane = lax.broadcasted_iota(jnp.int32, (scen, cols), 1)
     sub = lax.broadcasted_iota(jnp.int32, (scen, cols), 0)
 

time: 21.6 us -> 21.6 us (level)
  Pallas kernels: 6.95 us -> 6.71 us
  waiting for transfers between devices: 3.88 us -> 4.1 us
    pallas_call x8, Pallas kernels: 6.95 us -> 6.71 us  [call(): pl.pallas_call(kernel, out_shape=out, in_specs=[pl.BlockSpec(memory_space...]
  transfers between devices with their start and end apart: 8 -> 8, of which waited for: 4 -> 4; matrix products, arithmetic and copies ran while one was open for 0% -> 0% of each run, Pallas kernels for 20% -> 19%
where the time goes in v7:
time: 21.6 us; the launch traced here: 21.4 us
  starting transfers between devices  9.85 us (46%)
  Pallas kernels  6.71 us (31%)
  waiting for transfers between devices  4.1 us (19%)
  between operations  0.7 us (3%)
    ppermute x7, starting transfers between devices, swap(): return lax.ppermute(block, axis, [(i, i ^ mask) for i in range(count)])  6.82 us
    pallas_call x8, Pallas kernels, call(): pl.pallas_call(kernel, out_shape=out, in_specs=[pl.BlockSpec(memory_space...  6.71 us
    ppermute x7, waiting for transfers between devices, swap(): return lax.ppermute(block, axis, [(i, i ^ mask) for i in range(count)])  3.66 us
    ppermute x1, starting transfers between devices, swap_odd(): return lax.ppermute(block, (idle, axis), pairs)  3.03 us
    ppermute x1, waiting for transfers between devices, swap_odd(): return lax.ppermute(block, (idle, axis), pairs)  0.44 us
  transfers between devices with their start and end apart: 8, of which 4 were waited for; matrix products, arithmetic and copies ran while one was open for 0% of the time, Pallas kernels for 19%

profile of v7, /device:TPU:0, one launch (start us, length us, event | category | flops | bytes accessed | tf_op | source)
XLA Modules:
  0.0 21.4 jit_solution(11809584726281540231)
XLA Ops:
  0.6 1.0 %shard_map.131 = f32[184,128]{1,0:T(8,128)S(1)} custom-call(bf16[16,32,128]{2,1,0:T(8,128)(2,1)} %load_ref.3, f32[32,128]{1,0:T(8,128)} %rc_ref.3, f32[32,128]{1,0:T(8,128)} %vc_ref.3, s32[32,128]{1,0:T(8,128)} %vm_ref.3, f32[32,128]{1,0:T(8,128)} %rr_ref.5), custom_call_target="tpu_custom_call" | custom-call | flops 100000 | tf_op jit(solution)/shard_map/pallas_call | solution.py:705
  1.6 3.0 %collective-permute-start.1 = (f32[184,128]{1,0:T(8,128)S(1)}, f32[184,128]{1,0:T(8,128)S(1)}, u32[]{:S(2)}, u32[]{:S(2)}) collective-permute-start(f32[184,128]{1,0:T(8,128)S(1)} %shard_map.131), channel_id=1, source_target_pairs={{0,16},{4,8},{8,4},{12,28},{16,0},{20,24},{24,20},{28,12},{1,17},{... | collective-permute-start | bytes 282632 | tf_op jit(solution)/shard_map/ppermute | solution.py:701
  4.6 0.0 copy-start.3
  4.6 0.0 copy-start.4
  4.6 0.0 copy-start.5
  4.6 0.0 copy-start.6
  4.6 1.1 %shard_map.130 = (f32[512,128]{1,0:T(8,128)S(1)}, f32[32,128]{1,0:T(8,128)S(1)}, f32[32,128]{1,0:T(8,128)S(1)}, f32[184,128]{1,0:T(8,128)S(1)}) custom-call(bf16[16,32,128]{2,1,0:T(8,128)(2,1)} %load_ref.3, f32[32,128]{1,0:T(8,128)} %rc_ref.3, f32[32,128]{1,0:T(8,128)} %vc_ref.3, s32[32,128]{1,0:T(8,128)} %vm_ref.3, f32[32,128]{1,0:T(8,128)} %rr_ref.5), custom_call_target="tpu_custom_call" | custom-call | flops 100000 | tf_op jit(solution)/shard_map/pallas_call | solution.py:705
  5.8 0.2 collective-permute-start
  5.9 0.0 copy-done.3
  5.9 0.0 copy-done.4
  5.9 0.0 copy-done.5
  5.9 0.0 copy-done.6
  5.9 0.8 %shard_map.132 = (f32[512,128]{1,0:T(8,128)S(1)}, f32[64,128]{1,0:T(8,128)S(1)}, f32[160,128]{1,0:T(8,128)S(1)}, f32[8,128]{1,0:T(8,128)S(1)}, f32[96,128]{1,0:T(8,128)S(1)}, /*index=5*/f32[16,128]{1,0:T(8,128)S(1)}) custom-call(f32[512,128]{1,0:T(8,128)S(1)} %get-tuple-element.35.lf_ref, f32[32,128]{1,0:T(8,128)S(1)} %get-tuple-element.36.h_ref, ...), custom_call_target="tpu_custom_call" | custom-call | flops 10000000 | tf_op jit(solution)/shard_map/pallas_call | solution.py:705
  6.7 0.4 %collective-permute-done.1.b_ref = f32[184,128]{1,0:T(8,128)S(1)} collective-permute-done((f32[184,128]{1,0:T(8,128)S(1)}, f32[184,128]{1,0:T(8,128)S(1)}, u32[]{:S(2)}, u32[]{:S(2)}) %collective-permute-start.1) | collective-permute-done | bytes 94240 | tf_op jit(solution)/shard_map/ppermute | solution.py:701
  7.2 0.0 collective-permute-done.a_ref
  7.2 0.0 copy-start.2
  7.2 0.3 %shard_map.134 = (f32[64,128]{1,0:T(8,128)S(1)}, f32[32,128]{1,0:T(8,128)S(1)}, f32[72,128]{1,0:T(8,128)S(1)}, f32[16,128]{1,0:T(8,128)S(1)}) custom-call(f32[512,128]{1,0:T(8,128)S(1)} %get-tuple-element.35.lf_ref, f32[32,128]{1,0:T(8,128)S(1)} %get-tuple-element.36.h_ref, f32[32,128]{1,0:T(8,128)S(1)} %get-tuple-element.37.via_ref, ...), custom_call_target="tpu_custom_call" | custom-call | flops 1000000 | tf_op jit(solution)/shard_map/pallas_call | solution.py:705
  7.5 0.0 copy-start
  7.5 4.2 %collective-permute-start.3 = (f32[72,128]{1,0:T(8,128)S(1)}, f32[72,128]{1,0:T(8,128)S(1)}, u32[]{:S(2)}, u32[]{:S(2)}) collective-permute-start(f32[72,128]{1,0:T(8,128)S(1)} %get-tuple-element.54.seam_ref), channel_id=1, source_target_pairs={{0,3},{1,2},{2,1},{3,0},{4,7},{5,6},{6,5},{7,4},{8,11},{9,10},{10,... | collective-permute-start | bytes 110600 | tf_op jit(solution)/shard_map/ppermute | solution.py:686
  11.7 0.0 collective-permute-start.2
  11.7 0.0 copy-start.1
  11.7 0.6 %collective-permute-start.4 = (f32[32,128]{1,0:T(8,128)S(1)}, f32[32,128]{1,0:T(8,128)S(1)}, u32[]{:S(2)}, u32[]{:S(2)}) collective-permute-start(f32[32,128]{1,0:T(8,128)S(1)} %get-tuple-element.56.refs_0_), channel_id=1, source_target_pairs={{0,2},{1,3},{2,0},{3,1},{4,6},{5,7},{6,4},{7,5},{8,10},{9,11},{10,... | collective-permute-start | bytes 49160 | tf_op jit(solution)/shard_map/ppermute | solution.py:686
  12.3 0.0 copy-done.2
  12.3 1.3 %shard_map.133 = (f32[512,128]{1,0:T(8,128)S(1)}, f32[512,128]{1,0:T(8,128)S(1)}, f32[512,128]{1,0:T(8,128)S(1)}, f32[512,128]{1,0:T(8,128)S(1)}, f32[32,128]{1,0:T(8,128)S(1)}) custom-call(f32[512,128]{1,0:T(8,128)S(1)} %get-tuple-element.35.lf_ref, f32[32,128]{1,0:T(8,128)S(1)} %get-tuple-element.36.h_ref, f32[32,128]{1,0:T(8,128)S(1)} %get-tuple-element.37.via_ref, ...), custom_call_target="tpu_custom_call" | custom-call | flops 10000000 | tf_op jit(solution)/shard_map/pallas_call | solution.py:705
  13.6 2.7 %collective-permute-done.4.refs_2_ = f32[32,128]{1,0:T(8,128)S(1)} collective-permute-done((f32[32,128]{1,0:T(8,128)S(1)}, f32[32,128]{1,0:T(8,128)S(1)}, u32[]{:S(2)}, u32[]{:S(2)}) %collective-permute-start.4) | collective-permute-done | bytes 16416 | tf_op jit(solution)/shard_map/ppermute | solution.py:686
  16.3 0.0 collective-permute-done.2.rest_0_.refs_1_
  16.3 0.0 collective-permute-done.3.rest_1_.refs_3_
  16.3 0.3 %shard_map.136.rest_0_ = f32[8,128]{1,0:T(8,128)S(1)} custom-call(f32[32,128]{1,0:T(8,128)S(1)} %get-tuple-element.56.refs_0_, f32[64,128]{1,0:T(8,128)S(1)} %collective-permute-done.2.rest_0_.refs_1_, f32[32,128]{1,0:T(8,128)S(1)} %collective-permute-done.4.refs_2_, f32[72,128]{1,0:T(8,128)S(1)} %collective-permute-done.3.rest_1_.refs_3_), custom_call_target="tpu_custom_call" | custom-call | flops 100000 | tf_op jit(solution)/shard_map/pallas_call | solution.py:705
  16.6 0.0 collective-permute-start.7
  16.6 1.0 %collective-permute-start.6 = (f32[8,128]{1,0:T(8,128)S(1)}, f32[8,128]{1,0:T(8,128)S(1)}, u32[]{:S(2)}, u32[]{:S(2)}) collective-permute-start(f32[8,128]{1,0:T(8,128)S(1)} %shard_map.136.rest_0_), channel_id=1, source_target_pairs={{0,8},{4,12},{8,0},{12,4},{1,9},{5,13},{9,1},{13,5},{2,10},{6,14},... | collective-permute-start | bytes 12296 | tf_op jit(solution)/shard_map/ppermute | solution.py:686
  17.5 0.9 %collective-permute-start.5 = (f32[8,128]{1,0:T(8,128)S(1)}, f32[8,128]{1,0:T(8,128)S(1)}, u32[]{:S(2)}, u32[]{:S(2)}) collective-permute-start(f32[8,128]{1,0:T(8,128)S(1)} %shard_map.136.rest_0_), channel_id=1, source_target_pairs={{0,4},{4,0},{8,12},{12,8},{1,5},{5,1},{9,13},{13,9},{2,6},{6,2},{1... | collective-permute-start | bytes 12296 | tf_op jit(solution)/shard_map/ppermute | solution.py:686
  18.4 0.0 copy-done
  18.4 0.0 copy-done.1
  18.4 0.9 %shard_map.135 = (f32[512,128]{1,0:T(8,128)S(1)}, f32[32,128]{1,0:T(8,128)S(1)}) custom-call(f32[512,128]{1,0:T(8,128)S(1)} %get-tuple-element.46.fl_ref, f32[16,128]{1,0:T(8,128)S(1)} %get-tuple-element.52.fl_last_ref, f32[32,128]{1,0:T(8,128)S(1)} %copy-done.4, f32[64,128]{1,0:T(8,128)S(1)} %get-tuple-element.53.pair_ref, ...), custom_call_target="tpu_custom_call" | custom-call | flops 10000000 | tf_op jit(solution)/shard_map/pallas_call | solution.py:705
  19.3 0.3 %collective-permute-done.7.rest_3_ = f32[8,128]{1,0:T(8,128)S(1)} collective-permute-done((f32[8,128]{1,0:T(8,128)S(1)}, f32[8,128]{1,0:T(8,128)S(1)}, u32[]{:S(2)}, u32[]{:S(2)}) %collective-permute-start.7) | collective-permute-done | bytes 4128 | tf_op jit(solution)/shard_map/ppermute | solution.py:686
  19.6 0.6 %collective-permute-done.6.rest_2_ = f32[8,128]{1,0:T(8,128)S(1)} collective-permute-done((f32[8,128]{1,0:T(8,128)S(1)}, f32[8,128]{1,0:T(8,128)S(1)}, u32[]{:S(2)}, u32[]{:S(2)}) %collective-permute-start.6) | collective-permute-done | bytes 4128 | tf_op jit(solution)/shard_map/ppermute | solution.py:686
  20.2 0.0 collective-permute-done.5.rest_1_
  20.2 1.1 %shard_map.137 = (f32[16,32,128]{2,1,0:T(8,128)}, f32[16,32,128]{2,1,0:T(8,128)}, f32[16,32,128]{2,1,0:T(8,128)}) custom-call(f32[512,128]{1,0:T(8,128)S(1)} %get-tuple-element.42.v_ref, f32[512,128]{1,0:T(8,128)S(1)} %get-tuple-element.43.t_ref, f32[512,128]{1,0:T(8,128)S(1)} %get-tuple-element.44.gv_ref, f32[512,128]{1,0:T(8,128)S(1)} %get-tuple-element.45.gt_ref, ...), custom_call_target="tpu_custom_call" | custom-call | flops 1000000 | tf_op jit(solution)/shard_map/pallas_call | solution.py:705
Async XLA Ops:
  1.6 5.6 %collective-permute-start.1 = (f32[184,128]{1,0:T(8,128)S(1)}, f32[184,128]{1,0:T(8,128)S(1)}, u32[]{:S(2)}, u32[]{:S(2)}) collective-permute-start(f32[184,128]{1,0:T(8,128)S(1)} %shard_map.131), channel_id=1, source_target_pairs={{0,16},{4,8},{8,4},{12,28},{16,0},{20,24},{24,20},{28,12},{1,17},{... | collective-permute-start | bytes 282632 | tf_op jit(solution)/shard_map/ppermute | solution.py:701
  4.6 1.3 %copy-start.3 = (f32[48,128]{1,0:T(8,128)S(1)}, f32[48,128]{1,0:T(8,128)}, u32[]{:S(2)}) copy-start(f32[48,128]{1,0:T(8,128)} %constant.6.clone.pick_ref) | copy-start | bytes 73732
  4.6 1.3 %copy-start.4 = (f32[32,128]{1,0:T(8,128)S(1)}, f32[32,128]{1,0:T(8,128)}, u32[]{:S(2)}) copy-start(f32[32,128]{1,0:T(8,128)} %cr_ref.3) | copy-start | bytes 49156
  4.6 1.3 %copy-start.5 = (f32[32,128]{1,0:T(8,128)S(1)}, f32[32,128]{1,0:T(8,128)}, u32[]{:S(2)}) copy-start(f32[32,128]{1,0:T(8,128)} %cc_ref.1) | copy-start | bytes 49156
  4.6 1.3 %copy-start.6 = (s32[32,128]{1,0:T(8,128)S(1)}, s32[32,128]{1,0:T(8,128)}, u32[]{:S(2)}) copy-start(s32[32,128]{1,0:T(8,128)} %pm_ref.1) | copy-start | bytes 49156
  5.8 1.4 %collective-permute-start = (f32[184,128]{1,0:T(8,128)S(1)}, f32[184,128]{1,0:T(8,128)S(1)}, u32[]{:S(2)}, u32[]{:S(2)}) collective-permute-start(f32[184,128]{1,0:T(8,128)S(1)} %get-tuple-element.38), channel_id=1, source_target_pairs={{0,4},{4,0},{8,12},{12,8},{1,5},{5,1},{9,13},{13,9},{2,6},{6,2},{1... | collective-permute-start | bytes 282632 | tf_op jit(solution)/shard_map/ppermute | solution.py:686
  7.2 5.1 %copy-start.2 = (f32[32,128]{1,0:T(8,128)S(1)}, f32[32,128]{1,0:T(8,128)}, u32[]{:S(2)}) copy-start(f32[32,128]{1,0:T(8,128)} %rr_ref.5) | copy-start | bytes 49156
  7.5 11.0 %copy-start = (f32[4,152,128]{2,1,0:T(8,128)S(1)}, f32[4,152,128]{2,1,0:T(8,128)}, u32[]{:S(2)}) copy-start(f32[4,152,128]{2,1,0:T(8,128)} %constant.7.clone.rest_2_) | copy-start | bytes 933892
  7.5 8.8 %collective-permute-start.3 = (f32[72,128]{1,0:T(8,128)S(1)}, f32[72,128]{1,0:T(8,128)S(1)}, u32[]{:S(2)}, u32[]{:S(2)}) collective-permute-start(f32[72,128]{1,0:T(8,128)S(1)} %get-tuple-element.54.seam_ref), channel_id=1, source_target_pairs={{0,3},{1,2},{2,1},{3,0},{4,7},{5,6},{6,5},{7,4},{8,11},{9,10},{10,... | collective-permute-start | bytes 110600 | tf_op jit(solution)/shard_map/ppermute | solution.py:686
  11.7 4.6 %collective-permute-start.2 = (f32[64,128]{1,0:T(8,128)S(1)}, f32[64,128]{1,0:T(8,128)S(1)}, u32[]{:S(2)}, u32[]{:S(2)}) collective-permute-start(f32[64,128]{1,0:T(8,128)S(1)} %get-tuple-element.53.pair_ref), channel_id=1, source_target_pairs={{0,1},{1,0},{2,3},{3,2},{4,5},{5,4},{6,7},{7,6},{8,9},{9,8},{10,11... | collective-permute-start | bytes 98312 | tf_op jit(solution)/shard_map/ppermute | solution.py:686
  11.7 6.8 %copy-start.1 = (f32[4,144,128]{2,1,0:T(8,128)S(1)}, f32[4,144,128]{2,1,0:T(8,128)}, u32[]{:S(2)}) copy-start(f32[4,144,128]{2,1,0:T(8,128)} %constant.8.clone.rest_3_) | copy-start | bytes 884740
  11.7 4.6 %collective-permute-start.4 = (f32[32,128]{1,0:T(8,128)S(1)}, f32[32,128]{1,0:T(8,128)S(1)}, u32[]{:S(2)}, u32[]{:S(2)}) collective-permute-start(f32[32,128]{1,0:T(8,128)S(1)} %get-tuple-element.56.refs_0_), channel_id=1, source_target_pairs={{0,2},{1,3},{2,0},{3,1},{4,6},{5,7},{6,4},{7,5},{8,10},{9,11},{10,... | collective-permute-start | bytes 49160 | tf_op jit(solution)/shard_map/ppermute | solution.py:686
  16.6 3.0 %collective-permute-start.7 = (f32[8,128]{1,0:T(8,128)S(1)}, f32[8,128]{1,0:T(8,128)S(1)}, u32[]{:S(2)}, u32[]{:S(2)}) collective-permute-start(f32[8,128]{1,0:T(8,128)S(1)} %shard_map.136.rest_0_), channel_id=1, source_target_pairs={{0,12},{4,8},{8,4},{12,0},{1,13},{5,9},{9,5},{13,1},{2,14},{6,10},... | collective-permute-start | bytes 12296 | tf_op jit(solution)/shard_map/ppermute | solution.py:686
  16.6 3.7 %collective-permute-start.6 = (f32[8,128]{1,0:T(8,128)S(1)}, f32[8,128]{1,0:T(8,128)S(1)}, u32[]{:S(2)}, u32[]{:S(2)}) collective-permute-start(f32[8,128]{1,0:T(8,128)S(1)} %shard_map.136.rest_0_), channel_id=1, source_target_pairs={{0,8},{4,12},{8,0},{12,4},{1,9},{5,13},{9,1},{13,5},{2,10},{6,14},... | collective-permute-start | bytes 12296 | tf_op jit(solution)/shard_map/ppermute | solution.py:686
  17.5 2.7 %collective-permute-start.5 = (f32[8,128]{1,0:T(8,128)S(1)}, f32[8,128]{1,0:T(8,128)S(1)}, u32[]{:S(2)}, u32[]{:S(2)}) collective-permute-start(f32[8,128]{1,0:T(8,128)S(1)} %shard_map.136.rest_0_), channel_id=1, source_target_pairs={{0,4},{4,0},{8,12},{12,8},{1,5},{5,1},{9,13},{13,9},{2,6},{6,2},{1... | collective-permute-start | bytes 12296 | tf_op jit(solution)/shard_map/ppermute | solution.py:686

commit v8 on v7

--- a/solution.py
+++ b/solution.py
@@ -477,7 +477,7 @@
     sums = jnp.where(group == 3, both[0:1], jnp.where(group == 4, both[1:2], 0.0))
     sums = sum((block[USED - 1 : USED, :cols] for block in given), sums)
     if not held_refs:
-        out_refs[0][...] = jnp.broadcast_to(sums, (8, cols))
+        out_refs[0][...] = sums
         return
     row = lax.broadcasted_iota(jnp.int32, (USED, cols), 0)
     held = unpack_rows(held_refs[0], parts)
@@ -667,8 +667,7 @@
     sub = lax.broadcasted_iota(jnp.int32, (scen, cols), 0)
 
     def column(c):
-        tall = jnp.concatenate([c] * (scen // 8), 0)
-        return jnp.sum(jnp.where(lane == sub, tall, 0.0), 1, keepdims=True)
+        return jnp.sum(jnp.where(lane == sub, jnp.broadcast_to(c, lane.shape), 0.0), 1, keepdims=True)
 
     c0, c1 = column(c0), column(c1)
     br, bc = br_ref[...], bc_ref[...]
@@ -801,7 +800,7 @@
         if step * radix < count:
             plain, seam = call(merge, (plain_shape, seam_shape), [], 10**5, plain, *got, seam)
         else:
-            sums = call(merge, f32(8, cols), [], 10**5, plain, *got)
+            sums = call(merge, f32(1, cols), [], 10**5, plain, *got)
         step *= radix
 
     gl, bc = call(

time: 21.6 us -> 21.5 us (level)
  no operation moved by 1% of the time
where the time goes in v8:
time: 21.5 us; the launch traced here: 21.3 us
  starting transfers between devices  9.85 us (46%)
  Pallas kernels  6.71 us (31%)
  waiting for transfers between devices  4.01 us (19%)
  between operations  0.7 us (3%)
    ppermute x7, starting transfers between devices, swap(): return lax.ppermute(block, axis, [(i, i ^ mask) for i in range(count)])  6.82 us
    pallas_call x8, Pallas kernels, call(): pl.pallas_call(kernel, out_shape=out, in_specs=[pl.BlockSpec(memory_space...  6.71 us
    ppermute x7, waiting for transfers between devices, swap(): return lax.ppermute(block, axis, [(i, i ^ mask) for i in range(count)])  3.57 us
    ppermute x1, starting transfers between devices, swap_odd(): return lax.ppermute(block, (idle, axis), pairs)  3.03 us
    ppermute x1, waiting for transfers between devices, swap_odd(): return lax.ppermute(block, (idle, axis), pairs)  0.44 us
  transfers between devices with their start and end apart: 8, of which 4 were waited for; matrix products, arithmetic and copies ran while one was open for 0% of the time, Pallas kernels for 19%

profile of v8, /device:TPU:0, one launch (start us, length us, event | category | flops | bytes accessed | tf_op | source)
XLA Modules:
  0.0 21.3 jit_solution(7018399281232040179)
XLA Ops:
  0.6 1.0 %shard_map.131 = f32[184,128]{1,0:T(8,128)S(1)} custom-call(bf16[16,32,128]{2,1,0:T(8,128)(2,1)} %load_ref.3, f32[32,128]{1,0:T(8,128)} %rc_ref.3, f32[32,128]{1,0:T(8,128)} %vc_ref.3, s32[32,128]{1,0:T(8,128)} %vm_ref.3, f32[32,128]{1,0:T(8,128)} %rr_ref.5), custom_call_target="tpu_custom_call" | custom-call | flops 100000 | tf_op jit(solution)/shard_map/pallas_call | solution.py:704
  1.6 3.0 %collective-permute-start.1 = (f32[184,128]{1,0:T(8,128)S(1)}, f32[184,128]{1,0:T(8,128)S(1)}, u32[]{:S(2)}, u32[]{:S(2)}) collective-permute-start(f32[184,128]{1,0:T(8,128)S(1)} %shard_map.131), channel_id=1, source_target_pairs={{0,16},{4,8},{8,4},{12,28},{16,0},{20,24},{24,20},{28,12},{1,17},{... | collective-permute-start | bytes 282632 | tf_op jit(solution)/shard_map/ppermute | solution.py:700
  4.6 0.0 copy-start.3
  4.6 0.0 copy-start.4
  4.6 0.0 copy-start.5
  4.6 0.0 copy-start.6
  4.6 1.1 %shard_map.130 = (f32[512,128]{1,0:T(8,128)S(1)}, f32[32,128]{1,0:T(8,128)S(1)}, f32[32,128]{1,0:T(8,128)S(1)}, f32[184,128]{1,0:T(8,128)S(1)}) custom-call(bf16[16,32,128]{2,1,0:T(8,128)(2,1)} %load_ref.3, f32[32,128]{1,0:T(8,128)} %rc_ref.3, f32[32,128]{1,0:T(8,128)} %vc_ref.3, s32[32,128]{1,0:T(8,128)} %vm_ref.3, f32[32,128]{1,0:T(8,128)} %rr_ref.5), custom_call_target="tpu_custom_call" | custom-call | flops 100000 | tf_op jit(solution)/shard_map/pallas_call | solution.py:704
  5.8 0.2 collective-permute-start
  5.9 0.0 copy-done.3
  5.9 0.0 copy-done.4
  5.9 0.0 copy-done.5
  5.9 0.0 copy-done.6
  5.9 0.8 %shard_map.132 = (f32[512,128]{1,0:T(8,128)S(1)}, f32[64,128]{1,0:T(8,128)S(1)}, f32[160,128]{1,0:T(8,128)S(1)}, f32[8,128]{1,0:T(8,128)S(1)}, f32[96,128]{1,0:T(8,128)S(1)}, /*index=5*/f32[16,128]{1,0:T(8,128)S(1)}) custom-call(f32[512,128]{1,0:T(8,128)S(1)} %get-tuple-element.35.lf_ref, f32[32,128]{1,0:T(8,128)S(1)} %get-tuple-element.36.h_ref, ...), custom_call_target="tpu_custom_call" | custom-call | flops 10000000 | tf_op jit(solution)/shard_map/pallas_call | solution.py:704
  6.7 0.4 %collective-permute-done.1.b_ref = f32[184,128]{1,0:T(8,128)S(1)} collective-permute-done((f32[184,128]{1,0:T(8,128)S(1)}, f32[184,128]{1,0:T(8,128)S(1)}, u32[]{:S(2)}, u32[]{:S(2)}) %collective-permute-start.1) | collective-permute-done | bytes 94240 | tf_op jit(solution)/shard_map/ppermute | solution.py:700
  7.2 0.0 collective-permute-done.a_ref
  7.2 0.0 copy-start.2
  7.2 0.3 %shard_map.134 = (f32[64,128]{1,0:T(8,128)S(1)}, f32[32,128]{1,0:T(8,128)S(1)}, f32[72,128]{1,0:T(8,128)S(1)}, f32[16,128]{1,0:T(8,128)S(1)}) custom-call(f32[512,128]{1,0:T(8,128)S(1)} %get-tuple-element.35.lf_ref, f32[32,128]{1,0:T(8,128)S(1)} %get-tuple-element.36.h_ref, f32[32,128]{1,0:T(8,128)S(1)} %get-tuple-element.37.via_ref, ...), custom_call_target="tpu_custom_call" | custom-call | flops 1000000 | tf_op jit(solution)/shard_map/pallas_call | solution.py:704
  7.5 0.0 copy-start
  7.5 4.2 %collective-permute-start.3 = (f32[72,128]{1,0:T(8,128)S(1)}, f32[72,128]{1,0:T(8,128)S(1)}, u32[]{:S(2)}, u32[]{:S(2)}) collective-permute-start(f32[72,128]{1,0:T(8,128)S(1)} %get-tuple-element.54.seam_ref), channel_id=1, source_target_pairs={{0,3},{1,2},{2,1},{3,0},{4,7},{5,6},{6,5},{7,4},{8,11},{9,10},{10,... | collective-permute-start | bytes 110600 | tf_op jit(solution)/shard_map/ppermute | solution.py:685
  11.7 0.0 collective-permute-start.2
  11.7 0.0 copy-start.1
  11.7 0.6 %collective-permute-start.4 = (f32[32,128]{1,0:T(8,128)S(1)}, f32[32,128]{1,0:T(8,128)S(1)}, u32[]{:S(2)}, u32[]{:S(2)}) collective-permute-start(f32[32,128]{1,0:T(8,128)S(1)} %get-tuple-element.56.refs_0_), channel_id=1, source_target_pairs={{0,2},{1,3},{2,0},{3,1},{4,6},{5,7},{6,4},{7,5},{8,10},{9,11},{10,... | collective-permute-start | bytes 49160 | tf_op jit(solution)/shard_map/ppermute | solution.py:685
  12.3 0.0 copy-done.2
  12.3 1.3 %shard_map.133 = (f32[512,128]{1,0:T(8,128)S(1)}, f32[512,128]{1,0:T(8,128)S(1)}, f32[512,128]{1,0:T(8,128)S(1)}, f32[512,128]{1,0:T(8,128)S(1)}, f32[32,128]{1,0:T(8,128)S(1)}) custom-call(f32[512,128]{1,0:T(8,128)S(1)} %get-tuple-element.35.lf_ref, f32[32,128]{1,0:T(8,128)S(1)} %get-tuple-element.36.h_ref, f32[32,128]{1,0:T(8,128)S(1)} %get-tuple-element.37.via_ref, ...), custom_call_target="tpu_custom_call" | custom-call | flops 10000000 | tf_op jit(solution)/shard_map/pallas_call | solution.py:704
  13.6 2.7 %collective-permute-done.4.refs_2_ = f32[32,128]{1,0:T(8,128)S(1)} collective-permute-done((f32[32,128]{1,0:T(8,128)S(1)}, f32[32,128]{1,0:T(8,128)S(1)}, u32[]{:S(2)}, u32[]{:S(2)}) %collective-permute-start.4) | collective-permute-done | bytes 16416 | tf_op jit(solution)/shard_map/ppermute | solution.py:685
  16.3 0.0 collective-permute-done.2.rest_0_.refs_1_
  16.3 0.0 collective-permute-done.3.rest_1_.refs_3_
  16.3 0.3 %shard_map.136.rest_0_ = f32[1,128]{1,0:T(1,128)S(1)} custom-call(f32[32,128]{1,0:T(8,128)S(1)} %get-tuple-element.56.refs_0_, f32[64,128]{1,0:T(8,128)S(1)} %collective-permute-done.2.rest_0_.refs_1_, f32[32,128]{1,0:T(8,128)S(1)} %collective-permute-done.4.refs_2_, f32[72,128]{1,0:T(8,128)S(1)} %collective-permute-done.3.rest_1_.refs_3_), custom_call_target="tpu_custom_call" | custom-call | flops 100000 | tf_op jit(solution)/shard_map/pallas_call | solution.py:704
  16.6 0.0 collective-permute-start.7
  16.6 1.0 %collective-permute-start.6 = (f32[1,128]{1,0:T(1,128)S(1)}, f32[1,128]{1,0:T(1,128)S(1)}, u32[]{:S(2)}, u32[]{:S(2)}) collective-permute-start(f32[1,128]{1,0:T(1,128)S(1)} %shard_map.136.rest_0_), channel_id=1, source_target_pairs={{0,8},{4,12},{8,0},{12,4},{1,9},{5,13},{9,1},{13,5},{2,10},{6,14},... | collective-permute-start | bytes 1544 | tf_op jit(solution)/shard_map/ppermute | solution.py:685
  17.5 0.9 %collective-permute-start.5 = (f32[1,128]{1,0:T(1,128)S(1)}, f32[1,128]{1,0:T(1,128)S(1)}, u32[]{:S(2)}, u32[]{:S(2)}) collective-permute-start(f32[1,128]{1,0:T(1,128)S(1)} %shard_map.136.rest_0_), channel_id=1, source_target_pairs={{0,4},{4,0},{8,12},{12,8},{1,5},{5,1},{9,13},{13,9},{2,6},{6,2},{1... | collective-permute-start | bytes 1544 | tf_op jit(solution)/shard_map/ppermute | solution.py:685
  18.4 0.0 copy-done
  18.4 0.0 copy-done.1
  18.4 0.9 %shard_map.135 = (f32[512,128]{1,0:T(8,128)S(1)}, f32[32,128]{1,0:T(8,128)S(1)}) custom-call(f32[512,128]{1,0:T(8,128)S(1)} %get-tuple-element.46.fl_ref, f32[16,128]{1,0:T(8,128)S(1)} %get-tuple-element.52.fl_last_ref, f32[32,128]{1,0:T(8,128)S(1)} %copy-done.4, f32[64,128]{1,0:T(8,128)S(1)} %get-tuple-element.53.pair_ref, ...), custom_call_target="tpu_custom_call" | custom-call | flops 10000000 | tf_op jit(solution)/shard_map/pallas_call | solution.py:704
  19.3 0.2 %collective-permute-done.7.rest_3_ = f32[1,128]{1,0:T(1,128)S(1)} collective-permute-done((f32[1,128]{1,0:T(1,128)S(1)}, f32[1,128]{1,0:T(1,128)S(1)}, u32[]{:S(2)}, u32[]{:S(2)}) %collective-permute-start.7) | collective-permute-done | bytes 544 | tf_op jit(solution)/shard_map/ppermute | solution.py:685
  19.5 0.6 %collective-permute-done.6.rest_2_ = f32[1,128]{1,0:T(1,128)S(1)} collective-permute-done((f32[1,128]{1,0:T(1,128)S(1)}, f32[1,128]{1,0:T(1,128)S(1)}, u32[]{:S(2)}, u32[]{:S(2)}) %collective-permute-start.6) | collective-permute-done | bytes 544 | tf_op jit(solution)/shard_map/ppermute | solution.py:685
  20.1 0.0 collective-permute-done.5.rest_1_
  20.1 1.1 %shard_map.137 = (f32[16,32,128]{2,1,0:T(8,128)}, f32[16,32,128]{2,1,0:T(8,128)}, f32[16,32,128]{2,1,0:T(8,128)}) custom-call(f32[512,128]{1,0:T(8,128)S(1)} %get-tuple-element.42.v_ref, f32[512,128]{1,0:T(8,128)S(1)} %get-tuple-element.43.t_ref, f32[512,128]{1,0:T(8,128)S(1)} %get-tuple-element.44.gv_ref, f32[512,128]{1,0:T(8,128)S(1)} %get-tuple-element.45.gt_ref, ...), custom_call_target="tpu_custom_call" | custom-call | flops 1000000 | tf_op jit(solution)/shard_map/pallas_call | solution.py:704
Async XLA Ops:
  1.6 5.6 %collective-permute-start.1 = (f32[184,128]{1,0:T(8,128)S(1)}, f32[184,128]{1,0:T(8,128)S(1)}, u32[]{:S(2)}, u32[]{:S(2)}) collective-permute-start(f32[184,128]{1,0:T(8,128)S(1)} %shard_map.131), channel_id=1, source_target_pairs={{0,16},{4,8},{8,4},{12,28},{16,0},{20,24},{24,20},{28,12},{1,17},{... | collective-permute-start | bytes 282632 | tf_op jit(solution)/shard_map/ppermute | solution.py:700
  4.6 1.3 %copy-start.3 = (f32[48,128]{1,0:T(8,128)S(1)}, f32[48,128]{1,0:T(8,128)}, u32[]{:S(2)}) copy-start(f32[48,128]{1,0:T(8,128)} %constant.6.clone.pick_ref) | copy-start | bytes 73732
  4.6 1.3 %copy-start.4 = (f32[32,128]{1,0:T(8,128)S(1)}, f32[32,128]{1,0:T(8,128)}, u32[]{:S(2)}) copy-start(f32[32,128]{1,0:T(8,128)} %cr_ref.3) | copy-start | bytes 49156
  4.6 1.3 %copy-start.5 = (f32[32,128]{1,0:T(8,128)S(1)}, f32[32,128]{1,0:T(8,128)}, u32[]{:S(2)}) copy-start(f32[32,128]{1,0:T(8,128)} %cc_ref.1) | copy-start | bytes 49156
  4.6 1.3 %copy-start.6 = (s32[32,128]{1,0:T(8,128)S(1)}, s32[32,128]{1,0:T(8,128)}, u32[]{:S(2)}) copy-start(s32[32,128]{1,0:T(8,128)} %pm_ref.1) | copy-start | bytes 49156
  5.8 1.4 %collective-permute-start = (f32[184,128]{1,0:T(8,128)S(1)}, f32[184,128]{1,0:T(8,128)S(1)}, u32[]{:S(2)}, u32[]{:S(2)}) collective-permute-start(f32[184,128]{1,0:T(8,128)S(1)} %get-tuple-element.38), channel_id=1, source_target_pairs={{0,4},{4,0},{8,12},{12,8},{1,5},{5,1},{9,13},{13,9},{2,6},{6,2},{1... | collective-permute-start | bytes 282632 | tf_op jit(solution)/shard_map/ppermute | solution.py:685
  7.2 5.1 %copy-start.2 = (f32[32,128]{1,0:T(8,128)S(1)}, f32[32,128]{1,0:T(8,128)}, u32[]{:S(2)}) copy-start(f32[32,128]{1,0:T(8,128)} %rr_ref.5) | copy-start | bytes 49156
  7.5 11.0 %copy-start = (f32[4,152,128]{2,1,0:T(8,128)S(1)}, f32[4,152,128]{2,1,0:T(8,128)}, u32[]{:S(2)}) copy-start(f32[4,152,128]{2,1,0:T(8,128)} %constant.7.clone.rest_2_) | copy-start | bytes 933892
  7.5 8.8 %collective-permute-start.3 = (f32[72,128]{1,0:T(8,128)S(1)}, f32[72,128]{1,0:T(8,128)S(1)}, u32[]{:S(2)}, u32[]{:S(2)}) collective-permute-start(f32[72,128]{1,0:T(8,128)S(1)} %get-tuple-element.54.seam_ref), channel_id=1, source_target_pairs={{0,3},{1,2},{2,1},{3,0},{4,7},{5,6},{6,5},{7,4},{8,11},{9,10},{10,... | collective-permute-start | bytes 110600 | tf_op jit(solution)/shard_map/ppermute | solution.py:685
  11.7 4.6 %collective-permute-start.2 = (f32[64,128]{1,0:T(8,128)S(1)}, f32[64,128]{1,0:T(8,128)S(1)}, u32[]{:S(2)}, u32[]{:S(2)}) collective-permute-start(f32[64,128]{1,0:T(8,128)S(1)} %get-tuple-element.53.pair_ref), channel_id=1, source_target_pairs={{0,1},{1,0},{2,3},{3,2},{4,5},{5,4},{6,7},{7,6},{8,9},{9,8},{10,11... | collective-permute-start | bytes 98312 | tf_op jit(solution)/shard_map/ppermute | solution.py:685
  11.7 6.8 %copy-start.1 = (f32[4,144,128]{2,1,0:T(8,128)S(1)}, f32[4,144,128]{2,1,0:T(8,128)}, u32[]{:S(2)}) copy-start(f32[4,144,128]{2,1,0:T(8,128)} %constant.8.clone.rest_3_) | copy-start | bytes 884740
  11.7 4.6 %collective-permute-start.4 = (f32[32,128]{1,0:T(8,128)S(1)}, f32[32,128]{1,0:T(8,128)S(1)}, u32[]{:S(2)}, u32[]{:S(2)}) collective-permute-start(f32[32,128]{1,0:T(8,128)S(1)} %get-tuple-element.56.refs_0_), channel_id=1, source_target_pairs={{0,2},{1,3},{2,0},{3,1},{4,6},{5,7},{6,4},{7,5},{8,10},{9,11},{10,... | collective-permute-start | bytes 49160 | tf_op jit(solution)/shard_map/ppermute | solution.py:685
  16.6 3.0 %collective-permute-start.7 = (f32[1,128]{1,0:T(1,128)S(1)}, f32[1,128]{1,0:T(1,128)S(1)}, u32[]{:S(2)}, u32[]{:S(2)}) collective-permute-start(f32[1,128]{1,0:T(1,128)S(1)} %shard_map.136.rest_0_), channel_id=1, source_target_pairs={{0,12},{4,8},{8,4},{12,0},{1,13},{5,9},{9,5},{13,1},{2,14},{6,10},... | collective-permute-start | bytes 1544 | tf_op jit(solution)/shard_map/ppermute | solution.py:685
  16.6 3.6 %collective-permute-start.6 = (f32[1,128]{1,0:T(1,128)S(1)}, f32[1,128]{1,0:T(1,128)S(1)}, u32[]{:S(2)}, u32[]{:S(2)}) collective-permute-start(f32[1,128]{1,0:T(1,128)S(1)} %shard_map.136.rest_0_), channel_id=1, source_target_pairs={{0,8},{4,12},{8,0},{12,4},{1,9},{5,13},{9,1},{13,5},{2,10},{6,14},... | collective-permute-start | bytes 1544 | tf_op jit(solution)/shard_map/ppermute | solution.py:685
  17.5 2.6 %collective-permute-start.5 = (f32[1,128]{1,0:T(1,128)S(1)}, f32[1,128]{1,0:T(1,128)S(1)}, u32[]{:S(2)}, u32[]{:S(2)}) collective-permute-start(f32[1,128]{1,0:T(1,128)S(1)} %shard_map.136.rest_0_), channel_id=1, source_target_pairs={{0,4},{4,0},{8,12},{12,8},{1,5},{5,1},{9,13},{13,9},{2,6},{6,2},{1... | collective-permute-start | bytes 1544 | tf_op jit(solution)/shard_map/ppermute | solution.py:685

commit v9 on v8

--- a/solution.py
+++ b/solution.py
@@ -667,7 +667,8 @@
     sub = lax.broadcasted_iota(jnp.int32, (scen, cols), 0)
 
     def column(c):
-        return jnp.sum(jnp.where(lane == sub, jnp.broadcast_to(c, lane.shape), 0.0), 1, keepdims=True)
+        picked = jnp.where(lane == sub, jnp.broadcast_to(c, lane.shape), 0.0)
+        return jnp.broadcast_to(jnp.sum(picked, 1, keepdims=True), lane.shape)
 
     c0, c1 = column(c0), column(c1)
     br, bc = br_ref[...], bc_ref[...]

time: 21.5 us -> 21.5 us (level)
  no operation moved by 1% of the time
where the time goes in v9:
time: 21.5 us; the launch traced here: 21.3 us
  starting transfers between devices  9.85 us (46%)
  Pallas kernels  6.71 us (31%)
  waiting for transfers between devices  4.01 us (19%)
  between operations  0.7 us (3%)
    ppermute x7, starting transfers between devices, swap(): return lax.ppermute(block, axis, [(i, i ^ mask) for i in range(count)])  6.82 us
    pallas_call x8, Pallas kernels, call(): pl.pallas_call(kernel, out_shape=out, in_specs=[pl.BlockSpec(memory_space...  6.71 us
    ppermute x7, waiting for transfers between devices, swap(): return lax.ppermute(block, axis, [(i, i ^ mask) for i in range(count)])  3.57 us
    ppermute x1, starting transfers between devices, swap_odd(): return lax.ppermute(block, (idle, axis), pairs)  3.03 us
    ppermute x1, waiting for transfers between devices, swap_odd(): return lax.ppermute(block, (idle, axis), pairs)  0.44 us
  transfers between devices with their start and end apart: 8, of which 4 were waited for; matrix products, arithmetic and copies ran while one was open for 0% of the time, Pallas kernels for 19%

profile of v9, /device:TPU:0, one launch (start us, length us, event | category | flops | bytes accessed | tf_op | source)
XLA Modules:
  0.0 21.3 jit_solution(7018399281232040179)
XLA Ops:
  0.6 1.0 %shard_map.131 = f32[184,128]{1,0:T(8,128)S(1)} custom-call(bf16[16,32,128]{2,1,0:T(8,128)(2,1)} %load_ref.3, f32[32,128]{1,0:T(8,128)} %rc_ref.3, f32[32,128]{1,0:T(8,128)} %vc_ref.3, s32[32,128]{1,0:T(8,128)} %vm_ref.3, f32[32,128]{1,0:T(8,128)} %rr_ref.5), custom_call_target="tpu_custom_call" | custom-call | flops 100000 | tf_op jit(solution)/shard_map/pallas_call | solution.py:705
  1.6 3.0 %collective-permute-start.1 = (f32[184,128]{1,0:T(8,128)S(1)}, f32[184,128]{1,0:T(8,128)S(1)}, u32[]{:S(2)}, u32[]{:S(2)}) collective-permute-start(f32[184,128]{1,0:T(8,128)S(1)} %shard_map.131), channel_id=1, source_target_pairs={{0,16},{4,8},{8,4},{12,28},{16,0},{20,24},{24,20},{28,12},{1,17},{... | collective-permute-start | bytes 282632 | tf_op jit(solution)/shard_map/ppermute | solution.py:701
  4.6 0.0 copy-start.3
  4.6 0.0 copy-start.4
  4.6 0.0 copy-start.5
  4.6 0.0 copy-start.6
  4.6 1.1 %shard_map.130 = (f32[512,128]{1,0:T(8,128)S(1)}, f32[32,128]{1,0:T(8,128)S(1)}, f32[32,128]{1,0:T(8,128)S(1)}, f32[184,128]{1,0:T(8,128)S(1)}) custom-call(bf16[16,32,128]{2,1,0:T(8,128)(2,1)} %load_ref.3, f32[32,128]{1,0:T(8,128)} %rc_ref.3, f32[32,128]{1,0:T(8,128)} %vc_ref.3, s32[32,128]{1,0:T(8,128)} %vm_ref.3, f32[32,128]{1,0:T(8,128)} %rr_ref.5), custom_call_target="tpu_custom_call" | custom-call | flops 100000 | tf_op jit(solution)/shard_map/pallas_call | solution.py:705
  5.8 0.2 collective-permute-start
  5.9 0.0 copy-done.3
  5.9 0.0 copy-done.4
  5.9 0.0 copy-done.5
  5.9 0.0 copy-done.6
  5.9 0.8 %shard_map.132 = (f32[512,128]{1,0:T(8,128)S(1)}, f32[64,128]{1,0:T(8,128)S(1)}, f32[160,128]{1,0:T(8,128)S(1)}, f32[8,128]{1,0:T(8,128)S(1)}, f32[96,128]{1,0:T(8,128)S(1)}, /*index=5*/f32[16,128]{1,0:T(8,128)S(1)}) custom-call(f32[512,128]{1,0:T(8,128)S(1)} %get-tuple-element.35.lf_ref, f32[32,128]{1,0:T(8,128)S(1)} %get-tuple-element.36.h_ref, ...), custom_call_target="tpu_custom_call" | custom-call | flops 10000000 | tf_op jit(solution)/shard_map/pallas_call | solution.py:705
  6.7 0.4 %collective-permute-done.1.b_ref = f32[184,128]{1,0:T(8,128)S(1)} collective-permute-done((f32[184,128]{1,0:T(8,128)S(1)}, f32[184,128]{1,0:T(8,128)S(1)}, u32[]{:S(2)}, u32[]{:S(2)}) %collective-permute-start.1) | collective-permute-done | bytes 94240 | tf_op jit(solution)/shard_map/ppermute | solution.py:701
  7.2 0.0 collective-permute-done.a_ref
  7.2 0.0 copy-start.2
  7.2 0.3 %shard_map.134 = (f32[64,128]{1,0:T(8,128)S(1)}, f32[32,128]{1,0:T(8,128)S(1)}, f32[72,128]{1,0:T(8,128)S(1)}, f32[16,128]{1,0:T(8,128)S(1)}) custom-call(f32[512,128]{1,0:T(8,128)S(1)} %get-tuple-element.35.lf_ref, f32[32,128]{1,0:T(8,128)S(1)} %get-tuple-element.36.h_ref, f32[32,128]{1,0:T(8,128)S(1)} %get-tuple-element.37.via_ref, ...), custom_call_target="tpu_custom_call" | custom-call | flops 1000000 | tf_op jit(solution)/shard_map/pallas_call | solution.py:705
  7.5 0.0 copy-start
  7.5 4.2 %collective-permute-start.3 = (f32[72,128]{1,0:T(8,128)S(1)}, f32[72,128]{1,0:T(8,128)S(1)}, u32[]{:S(2)}, u32[]{:S(2)}) collective-permute-start(f32[72,128]{1,0:T(8,128)S(1)} %get-tuple-element.54.seam_ref), channel_id=1, source_target_pairs={{0,3},{1,2},{2,1},{3,0},{4,7},{5,6},{6,5},{7,4},{8,11},{9,10},{10,... | collective-permute-start | bytes 110600 | tf_op jit(solution)/shard_map/ppermute | solution.py:686
  11.7 0.0 collective-permute-start.2
  11.7 0.0 copy-start.1
  11.7 0.6 %collective-permute-start.4 = (f32[32,128]{1,0:T(8,128)S(1)}, f32[32,128]{1,0:T(8,128)S(1)}, u32[]{:S(2)}, u32[]{:S(2)}) collective-permute-start(f32[32,128]{1,0:T(8,128)S(1)} %get-tuple-element.56.refs_0_), channel_id=1, source_target_pairs={{0,2},{1,3},{2,0},{3,1},{4,6},{5,7},{6,4},{7,5},{8,10},{9,11},{10,... | collective-permute-start | bytes 49160 | tf_op jit(solution)/shard_map/ppermute | solution.py:686
  12.3 0.0 copy-done.2
  12.3 1.3 %shard_map.133 = (f32[512,128]{1,0:T(8,128)S(1)}, f32[512,128]{1,0:T(8,128)S(1)}, f32[512,128]{1,0:T(8,128)S(1)}, f32[512,128]{1,0:T(8,128)S(1)}, f32[32,128]{1,0:T(8,128)S(1)}) custom-call(f32[512,128]{1,0:T(8,128)S(1)} %get-tuple-element.35.lf_ref, f32[32,128]{1,0:T(8,128)S(1)} %get-tuple-element.36.h_ref, f32[32,128]{1,0:T(8,128)S(1)} %get-tuple-element.37.via_ref, ...), custom_call_target="tpu_custom_call" | custom-call | flops 10000000 | tf_op jit(solution)/shard_map/pallas_call | solution.py:705
  13.6 2.7 %collective-permute-done.4.refs_2_ = f32[32,128]{1,0:T(8,128)S(1)} collective-permute-done((f32[32,128]{1,0:T(8,128)S(1)}, f32[32,128]{1,0:T(8,128)S(1)}, u32[]{:S(2)}, u32[]{:S(2)}) %collective-permute-start.4) | collective-permute-done | bytes 16416 | tf_op jit(solution)/shard_map/ppermute | solution.py:686
  16.3 0.0 collective-permute-done.2.rest_0_.refs_1_
  16.3 0.0 collective-permute-done.3.rest_1_.refs_3_
  16.3 0.3 %shard_map.136.rest_0_ = f32[1,128]{1,0:T(1,128)S(1)} custom-call(f32[32,128]{1,0:T(8,128)S(1)} %get-tuple-element.56.refs_0_, f32[64,128]{1,0:T(8,128)S(1)} %collective-permute-done.2.rest_0_.refs_1_, f32[32,128]{1,0:T(8,128)S(1)} %collective-permute-done.4.refs_2_, f32[72,128]{1,0:T(8,128)S(1)} %collective-permute-done.3.rest_1_.refs_3_), custom_call_target="tpu_custom_call" | custom-call | flops 100000 | tf_op jit(solution)/shard_map/pallas_call | solution.py:705
  16.6 0.0 collective-permute-start.7
  16.6 1.0 %collective-permute-start.6 = (f32[1,128]{1,0:T(1,128)S(1)}, f32[1,128]{1,0:T(1,128)S(1)}, u32[]{:S(2)}, u32[]{:S(2)}) collective-permute-start(f32[1,128]{1,0:T(1,128)S(1)} %shard_map.136.rest_0_), channel_id=1, source_target_pairs={{0,8},{4,12},{8,0},{12,4},{1,9},{5,13},{9,1},{13,5},{2,10},{6,14},... | collective-permute-start | bytes 1544 | tf_op jit(solution)/shard_map/ppermute | solution.py:686
  17.5 0.9 %collective-permute-start.5 = (f32[1,128]{1,0:T(1,128)S(1)}, f32[1,128]{1,0:T(1,128)S(1)}, u32[]{:S(2)}, u32[]{:S(2)}) collective-permute-start(f32[1,128]{1,0:T(1,128)S(1)} %shard_map.136.rest_0_), channel_id=1, source_target_pairs={{0,4},{4,0},{8,12},{12,8},{1,5},{5,1},{9,13},{13,9},{2,6},{6,2},{1... | collective-permute-start | bytes 1544 | tf_op jit(solution)/shard_map/ppermute | solution.py:686
  18.4 0.0 copy-done
  18.4 0.0 copy-done.1
  18.4 0.9 %shard_map.135 = (f32[512,128]{1,0:T(8,128)S(1)}, f32[32,128]{1,0:T(8,128)S(1)}) custom-call(f32[512,128]{1,0:T(8,128)S(1)} %get-tuple-element.46.fl_ref, f32[16,128]{1,0:T(8,128)S(1)} %get-tuple-element.52.fl_last_ref, f32[32,128]{1,0:T(8,128)S(1)} %copy-done.4, f32[64,128]{1,0:T(8,128)S(1)} %get-tuple-element.53.pair_ref, ...), custom_call_target="tpu_custom_call" | custom-call | flops 10000000 | tf_op jit(solution)/shard_map/pallas_call | solution.py:705
  19.3 0.2 %collective-permute-done.7.rest_3_ = f32[1,128]{1,0:T(1,128)S(1)} collective-permute-done((f32[1,128]{1,0:T(1,128)S(1)}, f32[1,128]{1,0:T(1,128)S(1)}, u32[]{:S(2)}, u32[]{:S(2)}) %collective-permute-start.7) | collective-permute-done | bytes 544 | tf_op jit(solution)/shard_map/ppermute | solution.py:686
  19.5 0.6 %collective-permute-done.6.rest_2_ = f32[1,128]{1,0:T(1,128)S(1)} collective-permute-done((f32[1,128]{1,0:T(1,128)S(1)}, f32[1,128]{1,0:T(1,128)S(1)}, u32[]{:S(2)}, u32[]{:S(2)}) %collective-permute-start.6) | collective-permute-done | bytes 544 | tf_op jit(solution)/shard_map/ppermute | solution.py:686
  20.1 0.0 collective-permute-done.5.rest_1_
  20.1 1.1 %shard_map.137 = (f32[16,32,128]{2,1,0:T(8,128)}, f32[16,32,128]{2,1,0:T(8,128)}, f32[16,32,128]{2,1,0:T(8,128)}) custom-call(f32[512,128]{1,0:T(8,128)S(1)} %get-tuple-element.42.v_ref, f32[512,128]{1,0:T(8,128)S(1)} %get-tuple-element.43.t_ref, f32[512,128]{1,0:T(8,128)S(1)} %get-tuple-element.44.gv_ref, f32[512,128]{1,0:T(8,128)S(1)} %get-tuple-element.45.gt_ref, ...), custom_call_target="tpu_custom_call" | custom-call | flops 1000000 | tf_op jit(solution)/shard_map/pallas_call | solution.py:705
Async XLA Ops:
  1.6 5.6 %collective-permute-start.1 = (f32[184,128]{1,0:T(8,128)S(1)}, f32[184,128]{1,0:T(8,128)S(1)}, u32[]{:S(2)}, u32[]{:S(2)}) collective-permute-start(f32[184,128]{1,0:T(8,128)S(1)} %shard_map.131), channel_id=1, source_target_pairs={{0,16},{4,8},{8,4},{12,28},{16,0},{20,24},{24,20},{28,12},{1,17},{... | collective-permute-start | bytes 282632 | tf_op jit(solution)/shard_map/ppermute | solution.py:701
  4.6 1.3 %copy-start.3 = (f32[48,128]{1,0:T(8,128)S(1)}, f32[48,128]{1,0:T(8,128)}, u32[]{:S(2)}) copy-start(f32[48,128]{1,0:T(8,128)} %constant.6.clone.pick_ref) | copy-start | bytes 73732
  4.6 1.3 %copy-start.4 = (f32[32,128]{1,0:T(8,128)S(1)}, f32[32,128]{1,0:T(8,128)}, u32[]{:S(2)}) copy-start(f32[32,128]{1,0:T(8,128)} %cr_ref.3) | copy-start | bytes 49156
  4.6 1.3 %copy-start.5 = (f32[32,128]{1,0:T(8,128)S(1)}, f32[32,128]{1,0:T(8,128)}, u32[]{:S(2)}) copy-start(f32[32,128]{1,0:T(8,128)} %cc_ref.1) | copy-start | bytes 49156
  4.6 1.3 %copy-start.6 = (s32[32,128]{1,0:T(8,128)S(1)}, s32[32,128]{1,0:T(8,128)}, u32[]{:S(2)}) copy-start(s32[32,128]{1,0:T(8,128)} %pm_ref.1) | copy-start | bytes 49156
  5.8 1.4 %collective-permute-start = (f32[184,128]{1,0:T(8,128)S(1)}, f32[184,128]{1,0:T(8,128)S(1)}, u32[]{:S(2)}, u32[]{:S(2)}) collective-permute-start(f32[184,128]{1,0:T(8,128)S(1)} %get-tuple-element.38), channel_id=1, source_target_pairs={{0,4},{4,0},{8,12},{12,8},{1,5},{5,1},{9,13},{13,9},{2,6},{6,2},{1... | collective-permute-start | bytes 282632 | tf_op jit(solution)/shard_map/ppermute | solution.py:686
  7.2 5.1 %copy-start.2 = (f32[32,128]{1,0:T(8,128)S(1)}, f32[32,128]{1,0:T(8,128)}, u32[]{:S(2)}) copy-start(f32[32,128]{1,0:T(8,128)} %rr_ref.5) | copy-start | bytes 49156
  7.5 11.0 %copy-start = (f32[4,152,128]{2,1,0:T(8,128)S(1)}, f32[4,152,128]{2,1,0:T(8,128)}, u32[]{:S(2)}) copy-start(f32[4,152,128]{2,1,0:T(8,128)} %constant.7.clone.rest_2_) | copy-start | bytes 933892
  7.5 8.8 %collective-permute-start.3 = (f32[72,128]{1,0:T(8,128)S(1)}, f32[72,128]{1,0:T(8,128)S(1)}, u32[]{:S(2)}, u32[]{:S(2)}) collective-permute-start(f32[72,128]{1,0:T(8,128)S(1)} %get-tuple-element.54.seam_ref), channel_id=1, source_target_pairs={{0,3},{1,2},{2,1},{3,0},{4,7},{5,6},{6,5},{7,4},{8,11},{9,10},{10,... | collective-permute-start | bytes 110600 | tf_op jit(solution)/shard_map/ppermute | solution.py:686
  11.7 4.6 %collective-permute-start.2 = (f32[64,128]{1,0:T(8,128)S(1)}, f32[64,128]{1,0:T(8,128)S(1)}, u32[]{:S(2)}, u32[]{:S(2)}) collective-permute-start(f32[64,128]{1,0:T(8,128)S(1)} %get-tuple-element.53.pair_ref), channel_id=1, source_target_pairs={{0,1},{1,0},{2,3},{3,2},{4,5},{5,4},{6,7},{7,6},{8,9},{9,8},{10,11... | collective-permute-start | bytes 98312 | tf_op jit(solution)/shard_map/ppermute | solution.py:686
  11.7 6.8 %copy-start.1 = (f32[4,144,128]{2,1,0:T(8,128)S(1)}, f32[4,144,128]{2,1,0:T(8,128)}, u32[]{:S(2)}) copy-start(f32[4,144,128]{2,1,0:T(8,128)} %constant.8.clone.rest_3_) | copy-start | bytes 884740
  11.7 4.6 %collective-permute-start.4 = (f32[32,128]{1,0:T(8,128)S(1)}, f32[32,128]{1,0:T(8,128)S(1)}, u32[]{:S(2)}, u32[]{:S(2)}) collective-permute-start(f32[32,128]{1,0:T(8,128)S(1)} %get-tuple-element.56.refs_0_), channel_id=1, source_target_pairs={{0,2},{1,3},{2,0},{3,1},{4,6},{5,7},{6,4},{7,5},{8,10},{9,11},{10,... | collective-permute-start | bytes 49160 | tf_op jit(solution)/shard_map/ppermute | solution.py:686
  16.6 3.0 %collective-permute-start.7 = (f32[1,128]{1,0:T(1,128)S(1)}, f32[1,128]{1,0:T(1,128)S(1)}, u32[]{:S(2)}, u32[]{:S(2)}) collective-permute-start(f32[1,128]{1,0:T(1,128)S(1)} %shard_map.136.rest_0_), channel_id=1, source_target_pairs={{0,12},{4,8},{8,4},{12,0},{1,13},{5,9},{9,5},{13,1},{2,14},{6,10},... | collective-permute-start | bytes 1544 | tf_op jit(solution)/shard_map/ppermute | solution.py:686
  16.6 3.6 %collective-permute-start.6 = (f32[1,128]{1,0:T(1,128)S(1)}, f32[1,128]{1,0:T(1,128)S(1)}, u32[]{:S(2)}, u32[]{:S(2)}) collective-permute-start(f32[1,128]{1,0:T(1,128)S(1)} %shard_map.136.rest_0_), channel_id=1, source_target_pairs={{0,8},{4,12},{8,0},{12,4},{1,9},{5,13},{9,1},{13,5},{2,10},{6,14},... | collective-permute-start | bytes 1544 | tf_op jit(solution)/shard_map/ppermute | solution.py:686
  17.5 2.6 %collective-permute-start.5 = (f32[1,128]{1,0:T(1,128)S(1)}, f32[1,128]{1,0:T(1,128)S(1)}, u32[]{:S(2)}, u32[]{:S(2)}) collective-permute-start(f32[1,128]{1,0:T(1,128)S(1)} %shard_map.136.rest_0_), channel_id=1, source_target_pairs={{0,4},{4,0},{8,12},{12,8},{1,5},{5,1},{9,13},{13,9},{2,6},{6,2},{1... | collective-permute-start | bytes 1544 | tf_op jit(solution)/shard_map/ppermute | solution.py:686

commit v10 on v9

--- a/solution.py
+++ b/solution.py
@@ -395,7 +395,7 @@
     g2 -= q * tl
     g3 += tl * (low(1) * tl - 2.0 * p1) + jl * dl
 
-    w_s[...] = jnp.zeros_like(w_s)
+    w_s[5 * scen : cols - 2 * scen, :] = jnp.zeros((cols - 7 * scen, cols), F32)
     w_s[0:scen, :] = w_first
     for k, g in enumerate((g0, g1, g2, g3)):
         w_s[pl.ds((k + 1) * scen, scen), :] = acc_ref[pl.ds(k * scen, scen), :] + g

time: 21.5 us -> 21.5 us (level)
  no operation moved by 1% of the time
where the time goes in v10:
time: 21.5 us; the launch traced here: 21.3 us
  starting transfers between devices  9.85 us (46%)
  Pallas kernels  6.71 us (31%)
  waiting for transfers between devices  4.01 us (19%)
  between operations  0.7 us (3%)
    ppermute x7, starting transfers between devices, swap(): return lax.ppermute(block, axis, [(i, i ^ mask) for i in range(count)])  6.82 us
    pallas_call x8, Pallas kernels, call(): pl.pallas_call(kernel, out_shape=out, in_specs=[pl.BlockSpec(memory_space...  6.71 us
    ppermute x7, waiting for transfers between devices, swap(): return lax.ppermute(block, axis, [(i, i ^ mask) for i in range(count)])  3.57 us
    ppermute x1, starting transfers between devices, swap_odd(): return lax.ppermute(block, (idle, axis), pairs)  3.03 us
    ppermute x1, waiting for transfers between devices, swap_odd(): return lax.ppermute(block, (idle, axis), pairs)  0.44 us
  transfers between devices with their start and end apart: 8, of which 4 were waited for; matrix products, arithmetic and copies ran while one was open for 0% of the time, Pallas kernels for 19%

profile of v10, /device:TPU:0, one launch (start us, length us, event | category | flops | bytes accessed | tf_op | source)
XLA Modules:
  0.0 21.3 jit_solution(7018399281232040179)
XLA Ops:
  0.6 1.0 %shard_map.131 = f32[184,128]{1,0:T(8,128)S(1)} custom-call(bf16[16,32,128]{2,1,0:T(8,128)(2,1)} %load_ref.3, f32[32,128]{1,0:T(8,128)} %rc_ref.3, f32[32,128]{1,0:T(8,128)} %vc_ref.3, s32[32,128]{1,0:T(8,128)} %vm_ref.3, f32[32,128]{1,0:T(8,128)} %rr_ref.5), custom_call_target="tpu_custom_call" | custom-call | flops 100000 | tf_op jit(solution)/shard_map/pallas_call | solution.py:705
  1.6 3.0 %collective-permute-start.1 = (f32[184,128]{1,0:T(8,128)S(1)}, f32[184,128]{1,0:T(8,128)S(1)}, u32[]{:S(2)}, u32[]{:S(2)}) collective-permute-start(f32[184,128]{1,0:T(8,128)S(1)} %shard_map.131), channel_id=1, source_target_pairs={{0,16},{4,8},{8,4},{12,28},{16,0},{20,24},{24,20},{28,12},{1,17},{... | collective-permute-start | bytes 282632 | tf_op jit(solution)/shard_map/ppermute | solution.py:701
  4.6 0.0 copy-start.3
  4.6 0.0 copy-start.4
  4.6 0.0 copy-start.5
  4.6 0.0 copy-start.6
  4.6 1.1 %shard_map.130 = (f32[512,128]{1,0:T(8,128)S(1)}, f32[32,128]{1,0:T(8,128)S(1)}, f32[32,128]{1,0:T(8,128)S(1)}, f32[184,128]{1,0:T(8,128)S(1)}) custom-call(bf16[16,32,128]{2,1,0:T(8,128)(2,1)} %load_ref.3, f32[32,128]{1,0:T(8,128)} %rc_ref.3, f32[32,128]{1,0:T(8,128)} %vc_ref.3, s32[32,128]{1,0:T(8,128)} %vm_ref.3, f32[32,128]{1,0:T(8,128)} %rr_ref.5), custom_call_target="tpu_custom_call" | custom-call | flops 100000 | tf_op jit(solution)/shard_map/pallas_call | solution.py:705
  5.8 0.2 collective-permute-start
  5.9 0.0 copy-done.3
  5.9 0.0 copy-done.4
  5.9 0.0 copy-done.5
  5.9 0.0 copy-done.6
  5.9 0.8 %shard_map.132 = (f32[512,128]{1,0:T(8,128)S(1)}, f32[64,128]{1,0:T(8,128)S(1)}, f32[160,128]{1,0:T(8,128)S(1)}, f32[8,128]{1,0:T(8,128)S(1)}, f32[96,128]{1,0:T(8,128)S(1)}, /*index=5*/f32[16,128]{1,0:T(8,128)S(1)}) custom-call(f32[512,128]{1,0:T(8,128)S(1)} %get-tuple-element.35.lf_ref, f32[32,128]{1,0:T(8,128)S(1)} %get-tuple-element.36.h_ref, ...), custom_call_target="tpu_custom_call" | custom-call | flops 10000000 | tf_op jit(solution)/shard_map/pallas_call | solution.py:705
  6.7 0.4 %collective-permute-done.1.b_ref = f32[184,128]{1,0:T(8,128)S(1)} collective-permute-done((f32[184,128]{1,0:T(8,128)S(1)}, f32[184,128]{1,0:T(8,128)S(1)}, u32[]{:S(2)}, u32[]{:S(2)}) %collective-permute-start.1) | collective-permute-done | bytes 94240 | tf_op jit(solution)/shard_map/ppermute | solution.py:701
  7.2 0.0 collective-permute-done.a_ref
  7.2 0.0 copy-start.2
  7.2 0.3 %shard_map.134 = (f32[64,128]{1,0:T(8,128)S(1)}, f32[32,128]{1,0:T(8,128)S(1)}, f32[72,128]{1,0:T(8,128)S(1)}, f32[16,128]{1,0:T(8,128)S(1)}) custom-call(f32[512,128]{1,0:T(8,128)S(1)} %get-tuple-element.35.lf_ref, f32[32,128]{1,0:T(8,128)S(1)} %get-tuple-element.36.h_ref, f32[32,128]{1,0:T(8,128)S(1)} %get-tuple-element.37.via_ref, ...), custom_call_target="tpu_custom_call" | custom-call | flops 1000000 | tf_op jit(solution)/shard_map/pallas_call | solution.py:705
  7.5 0.0 copy-start
  7.5 4.2 %collective-permute-start.3 = (f32[72,128]{1,0:T(8,128)S(1)}, f32[72,128]{1,0:T(8,128)S(1)}, u32[]{:S(2)}, u32[]{:S(2)}) collective-permute-start(f32[72,128]{1,0:T(8,128)S(1)} %get-tuple-element.54.seam_ref), channel_id=1, source_target_pairs={{0,3},{1,2},{2,1},{3,0},{4,7},{5,6},{6,5},{7,4},{8,11},{9,10},{10,... | collective-permute-start | bytes 110600 | tf_op jit(solution)/shard_map/ppermute | solution.py:686
  11.7 0.0 collective-permute-start.2
  11.7 0.0 copy-start.1
  11.7 0.6 %collective-permute-start.4 = (f32[32,128]{1,0:T(8,128)S(1)}, f32[32,128]{1,0:T(8,128)S(1)}, u32[]{:S(2)}, u32[]{:S(2)}) collective-permute-start(f32[32,128]{1,0:T(8,128)S(1)} %get-tuple-element.56.refs_0_), channel_id=1, source_target_pairs={{0,2},{1,3},{2,0},{3,1},{4,6},{5,7},{6,4},{7,5},{8,10},{9,11},{10,... | collective-permute-start | bytes 49160 | tf_op jit(solution)/shard_map/ppermute | solution.py:686
  12.3 0.0 copy-done.2
  12.3 1.3 %shard_map.133 = (f32[512,128]{1,0:T(8,128)S(1)}, f32[512,128]{1,0:T(8,128)S(1)}, f32[512,128]{1,0:T(8,128)S(1)}, f32[512,128]{1,0:T(8,128)S(1)}, f32[32,128]{1,0:T(8,128)S(1)}) custom-call(f32[512,128]{1,0:T(8,128)S(1)} %get-tuple-element.35.lf_ref, f32[32,128]{1,0:T(8,128)S(1)} %get-tuple-element.36.h_ref, f32[32,128]{1,0:T(8,128)S(1)} %get-tuple-element.37.via_ref, ...), custom_call_target="tpu_custom_call" | custom-call | flops 10000000 | tf_op jit(solution)/shard_map/pallas_call | solution.py:705
  13.6 2.7 %collective-permute-done.4.refs_2_ = f32[32,128]{1,0:T(8,128)S(1)} collective-permute-done((f32[32,128]{1,0:T(8,128)S(1)}, f32[32,128]{1,0:T(8,128)S(1)}, u32[]{:S(2)}, u32[]{:S(2)}) %collective-permute-start.4) | collective-permute-done | bytes 16416 | tf_op jit(solution)/shard_map/ppermute | solution.py:686
  16.3 0.0 collective-permute-done.2.rest_0_.refs_1_
  16.3 0.0 collective-permute-done.3.rest_1_.refs_3_
  16.3 0.3 %shard_map.136.rest_0_ = f32[1,128]{1,0:T(1,128)S(1)} custom-call(f32[32,128]{1,0:T(8,128)S(1)} %get-tuple-element.56.refs_0_, f32[64,128]{1,0:T(8,128)S(1)} %collective-permute-done.2.rest_0_.refs_1_, f32[32,128]{1,0:T(8,128)S(1)} %collective-permute-done.4.refs_2_, f32[72,128]{1,0:T(8,128)S(1)} %collective-permute-done.3.rest_1_.refs_3_), custom_call_target="tpu_custom_call" | custom-call | flops 100000 | tf_op jit(solution)/shard_map/pallas_call | solution.py:705
  16.6 0.0 collective-permute-start.7
  16.6 1.0 %collective-permute-start.6 = (f32[1,128]{1,0:T(1,128)S(1)}, f32[1,128]{1,0:T(1,128)S(1)}, u32[]{:S(2)}, u32[]{:S(2)}) collective-permute-start(f32[1,128]{1,0:T(1,128)S(1)} %shard_map.136.rest_0_), channel_id=1, source_target_pairs={{0,8},{4,12},{8,0},{12,4},{1,9},{5,13},{9,1},{13,5},{2,10},{6,14},... | collective-permute-start | bytes 1544 | tf_op jit(solution)/shard_map/ppermute | solution.py:686
  17.5 0.9 %collective-permute-start.5 = (f32[1,128]{1,0:T(1,128)S(1)}, f32[1,128]{1,0:T(1,128)S(1)}, u32[]{:S(2)}, u32[]{:S(2)}) collective-permute-start(f32[1,128]{1,0:T(1,128)S(1)} %shard_map.136.rest_0_), channel_id=1, source_target_pairs={{0,4},{4,0},{8,12},{12,8},{1,5},{5,1},{9,13},{13,9},{2,6},{6,2},{1... | collective-permute-start | bytes 1544 | tf_op jit(solution)/shard_map/ppermute | solution.py:686
  18.4 0.0 copy-done
  18.4 0.0 copy-done.1
  18.4 0.9 %shard_map.135 = (f32[512,128]{1,0:T(8,128)S(1)}, f32[32,128]{1,0:T(8,128)S(1)}) custom-call(f32[512,128]{1,0:T(8,128)S(1)} %get-tuple-element.46.fl_ref, f32[16,128]{1,0:T(8,128)S(1)} %get-tuple-element.52.fl_last_ref, f32[32,128]{1,0:T(8,128)S(1)} %copy-done.4, f32[64,128]{1,0:T(8,128)S(1)} %get-tuple-element.53.pair_ref, ...), custom_call_target="tpu_custom_call" | custom-call | flops 10000000 | tf_op jit(solution)/shard_map/pallas_call | solution.py:705
  19.3 0.2 %collective-permute-done.7.rest_3_ = f32[1,128]{1,0:T(1,128)S(1)} collective-permute-done((f32[1,128]{1,0:T(1,128)S(1)}, f32[1,128]{1,0:T(1,128)S(1)}, u32[]{:S(2)}, u32[]{:S(2)}) %collective-permute-start.7) | collective-permute-done | bytes 544 | tf_op jit(solution)/shard_map/ppermute | solution.py:686
  19.5 0.6 %collective-permute-done.6.rest_2_ = f32[1,128]{1,0:T(1,128)S(1)} collective-permute-done((f32[1,128]{1,0:T(1,128)S(1)}, f32[1,128]{1,0:T(1,128)S(1)}, u32[]{:S(2)}, u32[]{:S(2)}) %collective-permute-start.6) | collective-permute-done | bytes 544 | tf_op jit(solution)/shard_map/ppermute | solution.py:686
  20.1 0.0 collective-permute-done.5.rest_1_
  20.1 1.1 %shard_map.137 = (f32[16,32,128]{2,1,0:T(8,128)}, f32[16,32,128]{2,1,0:T(8,128)}, f32[16,32,128]{2,1,0:T(8,128)}) custom-call(f32[512,128]{1,0:T(8,128)S(1)} %get-tuple-element.42.v_ref, f32[512,128]{1,0:T(8,128)S(1)} %get-tuple-element.43.t_ref, f32[512,128]{1,0:T(8,128)S(1)} %get-tuple-element.44.gv_ref, f32[512,128]{1,0:T(8,128)S(1)} %get-tuple-element.45.gt_ref, ...), custom_call_target="tpu_custom_call" | custom-call | flops 1000000 | tf_op jit(solution)/shard_map/pallas_call | solution.py:705
Async XLA Ops:
  1.6 5.6 %collective-permute-start.1 = (f32[184,128]{1,0:T(8,128)S(1)}, f32[184,128]{1,0:T(8,128)S(1)}, u32[]{:S(2)}, u32[]{:S(2)}) collective-permute-start(f32[184,128]{1,0:T(8,128)S(1)} %shard_map.131), channel_id=1, source_target_pairs={{0,16},{4,8},{8,4},{12,28},{16,0},{20,24},{24,20},{28,12},{1,17},{... | collective-permute-start | bytes 282632 | tf_op jit(solution)/shard_map/ppermute | solution.py:701
  4.6 1.3 %copy-start.3 = (f32[48,128]{1,0:T(8,128)S(1)}, f32[48,128]{1,0:T(8,128)}, u32[]{:S(2)}) copy-start(f32[48,128]{1,0:T(8,128)} %constant.6.clone.pick_ref) | copy-start | bytes 73732
  4.6 1.3 %copy-start.4 = (f32[32,128]{1,0:T(8,128)S(1)}, f32[32,128]{1,0:T(8,128)}, u32[]{:S(2)}) copy-start(f32[32,128]{1,0:T(8,128)} %cr_ref.3) | copy-start | bytes 49156
  4.6 1.3 %copy-start.5 = (f32[32,128]{1,0:T(8,128)S(1)}, f32[32,128]{1,0:T(8,128)}, u32[]{:S(2)}) copy-start(f32[32,128]{1,0:T(8,128)} %cc_ref.1) | copy-start | bytes 49156
  4.6 1.3 %copy-start.6 = (s32[32,128]{1,0:T(8,128)S(1)}, s32[32,128]{1,0:T(8,128)}, u32[]{:S(2)}) copy-start(s32[32,128]{1,0:T(8,128)} %pm_ref.1) | copy-start | bytes 49156
  5.8 1.4 %collective-permute-start = (f32[184,128]{1,0:T(8,128)S(1)}, f32[184,128]{1,0:T(8,128)S(1)}, u32[]{:S(2)}, u32[]{:S(2)}) collective-permute-start(f32[184,128]{1,0:T(8,128)S(1)} %get-tuple-element.38), channel_id=1, source_target_pairs={{0,4},{4,0},{8,12},{12,8},{1,5},{5,1},{9,13},{13,9},{2,6},{6,2},{1... | collective-permute-start | bytes 282632 | tf_op jit(solution)/shard_map/ppermute | solution.py:686
  7.2 5.1 %copy-start.2 = (f32[32,128]{1,0:T(8,128)S(1)}, f32[32,128]{1,0:T(8,128)}, u32[]{:S(2)}) copy-start(f32[32,128]{1,0:T(8,128)} %rr_ref.5) | copy-start | bytes 49156
  7.5 11.0 %copy-start = (f32[4,152,128]{2,1,0:T(8,128)S(1)}, f32[4,152,128]{2,1,0:T(8,128)}, u32[]{:S(2)}) copy-start(f32[4,152,128]{2,1,0:T(8,128)} %constant.7.clone.rest_2_) | copy-start | bytes 933892
  7.5 8.8 %collective-permute-start.3 = (f32[72,128]{1,0:T(8,128)S(1)}, f32[72,128]{1,0:T(8,128)S(1)}, u32[]{:S(2)}, u32[]{:S(2)}) collective-permute-start(f32[72,128]{1,0:T(8,128)S(1)} %get-tuple-element.54.seam_ref), channel_id=1, source_target_pairs={{0,3},{1,2},{2,1},{3,0},{4,7},{5,6},{6,5},{7,4},{8,11},{9,10},{10,... | collective-permute-start | bytes 110600 | tf_op jit(solution)/shard_map/ppermute | solution.py:686
  11.7 4.6 %collective-permute-start.2 = (f32[64,128]{1,0:T(8,128)S(1)}, f32[64,128]{1,0:T(8,128)S(1)}, u32[]{:S(2)}, u32[]{:S(2)}) collective-permute-start(f32[64,128]{1,0:T(8,128)S(1)} %get-tuple-element.53.pair_ref), channel_id=1, source_target_pairs={{0,1},{1,0},{2,3},{3,2},{4,5},{5,4},{6,7},{7,6},{8,9},{9,8},{10,11... | collective-permute-start | bytes 98312 | tf_op jit(solution)/shard_map/ppermute | solution.py:686
  11.7 6.8 %copy-start.1 = (f32[4,144,128]{2,1,0:T(8,128)S(1)}, f32[4,144,128]{2,1,0:T(8,128)}, u32[]{:S(2)}) copy-start(f32[4,144,128]{2,1,0:T(8,128)} %constant.8.clone.rest_3_) | copy-start | bytes 884740
  11.7 4.6 %collective-permute-start.4 = (f32[32,128]{1,0:T(8,128)S(1)}, f32[32,128]{1,0:T(8,128)S(1)}, u32[]{:S(2)}, u32[]{:S(2)}) collective-permute-start(f32[32,128]{1,0:T(8,128)S(1)} %get-tuple-element.56.refs_0_), channel_id=1, source_target_pairs={{0,2},{1,3},{2,0},{3,1},{4,6},{5,7},{6,4},{7,5},{8,10},{9,11},{10,... | collective-permute-start | bytes 49160 | tf_op jit(solution)/shard_map/ppermute | solution.py:686
  16.6 3.0 %collective-permute-start.7 = (f32[1,128]{1,0:T(1,128)S(1)}, f32[1,128]{1,0:T(1,128)S(1)}, u32[]{:S(2)}, u32[]{:S(2)}) collective-permute-start(f32[1,128]{1,0:T(1,128)S(1)} %shard_map.136.rest_0_), channel_id=1, source_target_pairs={{0,12},{4,8},{8,4},{12,0},{1,13},{5,9},{9,5},{13,1},{2,14},{6,10},... | collective-permute-start | bytes 1544 | tf_op jit(solution)/shard_map/ppermute | solution.py:686
  16.6 3.6 %collective-permute-start.6 = (f32[1,128]{1,0:T(1,128)S(1)}, f32[1,128]{1,0:T(1,128)S(1)}, u32[]{:S(2)}, u32[]{:S(2)}) collective-permute-start(f32[1,128]{1,0:T(1,128)S(1)} %shard_map.136.rest_0_), channel_id=1, source_target_pairs={{0,8},{4,12},{8,0},{12,4},{1,9},{5,13},{9,1},{13,5},{2,10},{6,14},... | collective-permute-start | bytes 1544 | tf_op jit(solution)/shard_map/ppermute | solution.py:686
  17.5 2.6 %collective-permute-start.5 = (f32[1,128]{1,0:T(1,128)S(1)}, f32[1,128]{1,0:T(1,128)S(1)}, u32[]{:S(2)}, u32[]{:S(2)}) collective-permute-start(f32[1,128]{1,0:T(1,128)S(1)} %shard_map.136.rest_0_), channel_id=1, source_target_pairs={{0,4},{4,0},{8,12},{12,8},{1,5},{5,1},{9,13},{13,9},{2,6},{6,2},{1... | collective-permute-start | bytes 1544 | tf_op jit(solution)/shard_map/ppermute | solution.py:686
